TPU v7x, 256 devices: a whole 4x4x8 slice. The times are simulated.
256 devices in a mesh: md: 32 (over z, y_lo, core), cd: 8 (over x, y_hi).
Axes of the slice: x: 4, y: 4 (y_hi: 2, y_lo: 2; y = y_hi * 2 + y_lo), z: 8, core: 2. Of those that a mesh axis runs over, the one named last changes fastest.
Arguments:
- orientation: float32 [5, 16, 128, 8192], P(None, None, 'cd', 'md'), may hold values from 0.05 to 0.35
- velocity: float32 [3, 16, 128, 8192], P(None, None, 'cd', 'md'), may hold values from -3 to 3
- velocity_grad: float32 [9, 16, 128, 8192], P(None, None, 'cd', 'md'), may hold values from -3 to 3
- rotary: float32 [16, 128, 8192], P(None, 'cd', 'md'), may hold values from 0.05 to 0.5
- target: float32 [5, 16, 128, 8192], P(None, None, 'cd', 'md'), may hold values from 0 to 0.4
- needle_params: float32 [4096, 8, 16], P('md', 'cd'), may hold values from 0 to 0.2
- foot_start: int32 [4096, 8], P(None, 'cd'), may hold values from 0 to 8192, as said below
- foot_end: int32 [4096, 8], P(None, 'cd'), may hold values from 0 to 8192, as said below
- foot_column: int32 [4096, 8], P(None, 'cd'), may hold values from 0 to 15
Outputs:
- final_orientation: float32 [5, 16, 128, 8192], P(None, None, 'cd', 'md')
- initial_sensitivity: float32 [5, 16, 128, 8192], P(None, None, 'cd', 'md')
- needle_gradient: float32 [4096, 8, 16], P('md', 'cd')
Inputs may be any that keep to these rules, and one draw needn't show every extreme that they name: foot_start[r, c] <= foot_end[r, c], and 2 r - 256 <= foot_start[r, c]. foot_end[r, c] <= 2 r + 256. Needle (r, c) lies in cross-direction cell c * 16 + foot_column[r, c].
All inputs are finite; a program needn't handle non-finite values.
Results may differ from a plain program's by a relative error of at most 0.0003.
Values sent between devices are 32-bit elements; how exact they have to be, the bound alone decides.
No kernel may reach another device: no remote copies, remote signals or barrier semaphores. Data moves between devices by JAX's collectives and lax.ppermute only.
A program may use at most 128 MiB of HBM per device.

v0:
```python
import functools

import jax
import jax.numpy as jnp
from jax import lax
from jax.experimental import pallas as pl
from jax.experimental.pallas import tpu as pltpu
from jax.sharding import PartitionSpec as P

XI = 0.95
DT = 0.1
LANES = 128
F32 = jnp.float32
HALO = 4
S0, VEL, GRAD, ROT, TGT, NEEDLES, PLANES = 0, 5, 8, 17, 18, 23, 24
PLACE = {(0, 0): 0, (1, 1): 1, (0, 1): 2, (1, 0): 3, (0, 2): 4, (2, 0): 5, (1, 2): 6, (2, 1): 7}
SPREAD, UX, UZ, COEFS = 8, 9, 10, 11
ROWS = 32
OWN, BEHIND, FRONT = slice(8, 24), slice(7, 23), slice(9, 25)


def lane_iota(shape):
    return lax.broadcasted_iota(jnp.int32, shape, len(shape) - 1)


def row_iota(shape):
    return lax.broadcasted_iota(jnp.int32, shape, len(shape) - 2)


def span(tile):
    return slice(tile * LANES, (tile + 1) * LANES)


def gradient_parts(read):
    g = [read(i) for i in range(9)]
    low = 0.5 * (XI - 1.0) * DT
    m = {}
    for i, j in ((0, 1), (0, 2), (1, 2)):
        a, b = g[3 * i + j], g[3 * j + i]
        both = low * (a + b)
        m[i, j] = DT * a + both
        m[j, i] = DT * b + both
    m[0, 0] = (XI * DT) * (g[0] - g[8])
    m[1, 1] = (XI * DT) * (g[4] - g[8])
    return m


def forward(a, m, base, spread, wind, around):
    a11, a22, a12, a13, a23 = a
    a33 = 1.0 - a11 - a22
    n00 = m[0, 0] * a11 + m[0, 1] * a12 + m[0, 2] * a13
    n01 = m[0, 0] * a12 + m[0, 1] * a22 + m[0, 2] * a23
    n02 = m[0, 0] * a13 + m[0, 1] * a23 + m[0, 2] * a33
    n10 = m[1, 0] * a11 + m[1, 1] * a12 + m[1, 2] * a13
    n11 = m[1, 0] * a12 + m[1, 1] * a22 + m[1, 2] * a23
    n12 = m[1, 0] * a13 + m[1, 1] * a23 + m[1, 2] * a33
    n20 = m[2, 0] * a11 + m[2, 1] * a12
    n21 = m[2, 0] * a12 + m[2, 1] * a22
    n22 = m[2, 0] * a13 + m[2, 1] * a23
    keep = 1.0 - (base + 2.0 * (n00 + n11 + n22))
    gain = (2.0 * n00 + spread, 2.0 * n11 + spread, n01 + n10, n02 + n20, n12 + n21)
    out = []
    for c in range(5):
        total = gain[c] + keep * a[c]
        for u, (behind, front) in zip(wind, around(c)):
            total = total + jnp.abs(u) * jnp.where(u > 0.0, behind, front)
        out.append(total)
    return out


def backward(b, a, m, base, wind, around):
    b1, b2, b3, b4, b5 = b
    a11, a22, a12, a13, a23 = a
    g = -2.0 * (b1 * a11 + b2 * a22 + b3 * a12 + b4 * a13 + b5 * a23)
    trace = (
        m[0, 0] * a11
        + m[1, 1] * a22
        + (m[0, 1] + m[1, 0]) * a12
        + (m[0, 2] + m[2, 0]) * a13
        + (m[1, 2] + m[2, 1]) * a23
    )
    s00, s11, s22 = 2.0 * b1 + g, 2.0 * b2 + g, g
    h00 = m[0, 0] * s00 + m[1, 0] * b3 + m[2, 0] * b4
    h01 = m[0, 0] * b3 + m[1, 0] * s11 + m[2, 0] * b5
    h02 = m[0, 0] * b4 + m[1, 0] * b5 + m[2, 0] * s22
    h10 = m[0, 1] * s00 + m[1, 1] * b3 + m[2, 1] * b4
    h11 = m[0, 1] * b3 + m[1, 1] * s11 + m[2, 1] * b5
    h12 = m[0, 1] * b4 + m[1, 1] * b5 + m[2, 1] * s22
    h20 = m[0, 2] * s00 + m[1, 2] * b3
    h21 = m[0, 2] * b3 + m[1, 2] * s11
    h22 = m[0, 2] * b4 + m[1, 2] * b5
    keep = 1.0 - (base + 2.0 * trace)
    gain = (h00 - h22, h11 - h22, h01 + h10, h02 + h20, h12 + h21)
    weights = [(jnp.minimum(w, 0.0), jnp.maximum(f, 0.0)) for w, f in wind]
    out = []
    for c in range(5):
        total = gain[c] + keep * b[c]
        for (low, high), (behind, front) in zip(weights, around(c)):
            total = total + (high * front - low * behind)
        out.append(total)
    return out


def merged(strips, c, rows):
    left, right = strips[c, 0, rows], strips[c, 1, rows]
    return jnp.where(lane_iota(left.shape) % 8 < HALO, left, right)


def edge_tile(joint, z):
    return pltpu.roll(joint, (2 * LANES - HALO - 8 * z) % LANES, 1)


def x_pair(tiles, tile, edge):
    cur = tiles[tile]
    prev, after = (edge, tiles[1]) if tile == 0 else (tiles[0], edge)
    lane = lane_iota(cur.shape)
    behind = pltpu.roll(jnp.where(lane == LANES - 1, prev, cur), 1, 1)
    front = pltpu.roll(jnp.where(lane == 0, after, cur), LANES - 1, 1)
    return behind, front


def strip_x(cur):
    return pltpu.roll(cur, 1, 1), pltpu.roll(cur, LANES - 1, 1)


def strip_z(cur):
    lane = lane_iota(cur.shape)
    behind = jnp.where(lane < 8, 0.0, pltpu.roll(cur, 8, 1))
    front = jnp.where(lane >= LANES - 8, 0.0, pltpu.roll(cur, LANES - 8, 1))
    return behind, front


def coefficients(coef, base, *at):
    m = {key: coef[(place,) + at] for key, place in PLACE.items()}
    return m, base[at]


class Field:
    def __init__(self, ref, strips, joint=None):
        self.ref, self.strips, self.joint = ref, strips, joint

    def join(self):
        for c in range(self.ref.shape[0]):
            self.joint[c] = merged(self.strips, c, OWN)

    def own(self, c, z, tile):
        return self.ref[c, z + 1, tile, OWN]

    def around(self, z, tile):
        def pairs(c):
            ref = self.ref
            tiles = [ref[c, z + 1, t, OWN] for t in range(2)]
            if self.joint is None:
                edge = jnp.zeros_like(tiles[0])
            else:
                edge = edge_tile(self.joint[c], z)
            return (
                x_pair(tiles, tile, edge),
                (ref[c, z + 1, tile, BEHIND], ref[c, z + 1, tile, FRONT]),
                (ref[c, z, tile, OWN], ref[c, z + 2, tile, OWN]),
            )

        return pairs

    def strip_around(self, side):
        def pairs(c):
            cur = self.strips[c, side, OWN]
            return (
                strip_x(cur),
                (self.strips[c, side, BEHIND], self.strips[c, side, FRONT]),
                strip_z(cur),
            )

        return pairs

    def clear(self):
        last = self.ref.shape[1] - 1
        zero = jnp.zeros((8, LANES), F32)
        clear_planes(self.ref)

        def layer(z, carry):
            for c in range(self.ref.shape[0]):
                for tile in range(2):
                    self.ref[c, z, tile, 0:8] = zero
                    self.ref[c, z, tile, 24:32] = zero
            return carry

        lax.fori_loop(1, last, layer, 0)

    def clear_strips(self):
        zero = jnp.zeros((8, LANES), F32)
        for c in range(self.strips.shape[0]):
            for side in range(2):
                self.strips[c, side, 0:8] = zero
                self.strips[c, side, 24:32] = zero


def clear_planes(ref, planes=None):
    last = ref.shape[1] - 1
    for c in planes or range(ref.shape[0]):
        for tile in range(2):
            for z in (0, last):
                ref[c, z, tile] = jnp.zeros(ref.shape[3:], F32)


def line(z, place, count, layers):
    if z is None:
        return slice(count * layers + place, count * layers + place + 1)
    return pl.ds(place * layers + z, 1)


def back_wind(coef, uy, edge_x, z, tile):
    tiles = [coef[UX, z + 1, t] for t in range(2)]
    return (
        x_pair(tiles, tile, edge_tile(edge_x, z)),
        (uy[z + 1, tile, BEHIND], uy[z + 1, tile, FRONT]),
        (coef[UZ, z, tile], coef[UZ, z + 2, tile]),
    )


def strip_back_wind(coef, uy, side):
    return (
        strip_x(coef[UX, side]),
        (uy[side, BEHIND], uy[side, FRONT]),
        strip_z(coef[UZ, side]),
    )


def pack_kernel(s0, vel, grad, rot, tgt, needle, out, stage, sems):
    layers = stage.shape[1]
    blocks = sems.shape[0]
    deep = layers // blocks
    sources = (s0, vel, grad, rot, tgt)

    def copies(block):
        slot, found = 0, []
        for number, ref in enumerate(sources):
            depth = pl.ds(block * deep, deep)
            target = stage.at[pl.ds(slot, ref.shape[0]), depth]
            found.append(
                pltpu.make_async_copy(ref.at[:, depth], target, sems.at[block, number])
            )
            slot += ref.shape[0]
        return found

    for block in range(blocks):
        for copy in copies(block):
            copy.start()
    out[NEEDLES] = needle[...]
    lane = lane_iota(out.shape[1:])

    def step(block, carry):
        for copy in copies(block):
            copy.wait()
        for c in range(NEEDLES):
            total = out[c]
            for k in range(deep):
                z = block * deep + k
                low, high = stage[c, z, :, span(0)], stage[c, z, :, span(1)]
                both = jnp.where(lane < HALO, low, high)
                moved = pltpu.roll(both, (8 * z + HALO) % LANES, 1)
                total = jnp.where(lane // 8 == z, moved, total)
            out[c] = total
        return carry

    lax.fori_loop(0, blocks, step, 0)


def bulk_kernel(s0, vel, grad, rot, field, coef, base, uy, s1):
    layers = s0.shape[1]
    state = Field(field, None)
    state.clear()
    clear_planes(coef, [UZ])

    def load(z, carry):
        zero = jnp.zeros((8, LANES), F32)
        for tile in range(2):
            for c in range(5):
                field[c, z + 1, tile, OWN] = s0[c, z, :, span(tile)]
            u = [DT * vel[d, z, :, span(tile)] for d in range(3)]
            turn = DT * rot[0, z, :, span(tile)]
            for key, value in gradient_parts(lambda i: grad[i, z, :, span(tile)]).items():
                coef[PLACE[key], z + 1, tile] = value
            coef[SPREAD, z + 1, tile] = 2.0 * turn
            coef[UX, z + 1, tile] = u[0]
            coef[UZ, z + 1, tile] = u[2]
            uy[z + 1, tile, 0:8] = zero
            uy[z + 1, tile, 24:32] = zero
            uy[z + 1, tile, OWN] = u[1]
            base[z + 1, tile] = 6.0 * turn + (jnp.abs(u[0]) + jnp.abs(u[1]) + jnp.abs(u[2]))
        return carry

    lax.fori_loop(0, layers, load, 0)

    def advance(z, carry):
        for tile in range(2):
            at = (z + 1, tile)
            m, damp = coefficients(coef, base, *at)
            wind = (coef[(UX,) + at], uy[at + (OWN,)], coef[(UZ,) + at])
            a = [state.own(c, z, tile) for c in range(5)]
            out = forward(a, m, damp, coef[(SPREAD,) + at], wind, state.around(z, tile))
            for c in range(5):
                s1[c, z + 1, tile, OWN] = out[c]
        return carry

    lax.fori_loop(0, layers, advance, 0)


def split_three(value):
    parts = []
    for _ in range(3):
        part = value.astype(jnp.bfloat16).astype(F32)
        parts.append(part)
        value = value - part
    return parts


def feet_block(ref, block, count):
    place = jnp.clip(block, 0, count - 1) * LANES
    row = ref[:, pl.ds(pl.multiple_of(place, LANES), LANES)]
    return jnp.where((block >= 0) & (block < count), row, 0)


def first_kernel(
    axis_md,
    axis_cd,
    own,
    near_first,
    near_second,
    far_first,
    far_second,
    start,
    end,
    column,
    field,
    coef,
    uy,
    base_in,
    s1_in,
    s1,
    base,
    strip_s0,
    strip_coef,
    strip_base,
    strip_uy,
    strip_s1,
    strip_tgt,
    up,
    down,
    spread,
    cover,
    source,
    joint,
):
    layers = field.shape[1] - 2
    height = own.shape[1]
    md = lax.axis_index(axis_md)
    count = lax.axis_size(axis_md)
    lane = lane_iota((height, LANES))
    outer = lane % 8 < HALO
    odd = lax.axis_index(axis_cd) % 2 == 1

    def from_left(c):
        return jnp.where(odd, near_second[c], near_first[c])

    def from_right(c):
        return jnp.where(odd, near_first[c], near_second[c])

    near = lane_iota((1, LANES)) < LANES // 2

    def feet(ref):
        far = jnp.where(near, feet_block(ref, md + 2, count), feet_block(ref, md - 2, count))
        blocks = [feet_block(ref, md + d, count) for d in (-1, 0, 1)]
        return jnp.concatenate(blocks + [far], axis=1)

    starts, ends, columns = feet(start), feet(end), feet(column)
    far = jnp.where((lane < LANES // 2) == odd, far_first[...], far_second[...])
    rates = jnp.concatenate(
        [from_left(NEEDLES), own[NEEDLES], from_right(NEEDLES), far], axis=1
    )
    needles = rates.shape[1]
    picked = jnp.where(row_iota((height, needles)) == columns, 1.0, 0.0)
    for part, value in enumerate(split_three(rates)):
        for z in range(layers):
            spread[part, z * height : (z + 1) * height] = (picked * value[z : z + 1]).astype(
                jnp.bfloat16
            )
    length = 2 * LANES
    cells = row_iota((length + LANES, needles))
    beyond = cells - length
    strip = jnp.where(beyond < 8, beyond - HALO, beyond - 8 + length - HALO)
    cells = jnp.where(cells < length, cells, strip) + md * length
    cover[...] = jnp.where((cells >= starts) & (cells < ends), 1.0, 0.0).astype(jnp.bfloat16)
    product = jnp.zeros((layers * height, length + LANES), F32)
    for part in range(3):
        product = product + lax.dot_general(
            spread[part], cover[...], (((1,), (1,)), ((), ())), preferred_element_type=F32
        )
    source[...] = (DT * product).reshape(source.shape)

    state = Field(field, strip_s0, joint)
    state.clear_strips()
    has_left, has_right = md > 0, md < count - 1
    for side in range(2):

        def raw(c):
            if side == 0:
                return jnp.where(outer, jnp.where(has_left, from_left(c), 0.0), own[c])
            return jnp.where(outer, own[c], jnp.where(has_right, from_right(c), 0.0))

        for c in range(5):
            strip_s0[c, side, OWN] = raw(S0 + c)
            strip_tgt[c, side] = raw(TGT + c)
        u = [DT * raw(VEL + d) for d in range(3)]
        turn = DT * raw(ROT)
        for key, value in gradient_parts(lambda i: raw(GRAD + i)).items():
            strip_coef[PLACE[key], side] = value
        strip_coef[SPREAD, side] = 2.0 * turn
        strip_coef[UX, side] = u[0]
        strip_coef[UZ, side] = u[2]
        strip_uy[side, 0:8] = jnp.zeros((8, LANES), F32)
        strip_uy[side, 24:32] = jnp.zeros((8, LANES), F32)
        strip_uy[side, OWN] = u[1]
        damp = 6.0 * turn + (jnp.abs(u[0]) + jnp.abs(u[1]) + jnp.abs(u[2]))
        taken = jnp.zeros((height, LANES), F32)
        for z in range(layers):
            moved = pltpu.roll(source[z, :, span(2)], (8 * z - 8 * side) % LANES, 1)
            taken = jnp.where(lane // 8 == z, moved, taken)
        strip_base[side] = damp + taken

    for side in range(2):
        m, damp = coefficients(strip_coef, strip_base, side)
        wind = (strip_coef[UX, side], strip_uy[side, OWN], strip_coef[UZ, side])
        a = [strip_s0[c, side, OWN] for c in range(5)]
        spin = strip_coef[SPREAD, side]
        out = forward(a, m, damp, spin, wind, state.strip_around(side))
        for c in range(5):
            strip_s1[c, side, OWN] = out[c]
    state.join()

    def put(z, tile, first, new, wind):
        def at(place):
            return line(z, tile * 11 + place, 22, layers)

        for c in range(5):
            up[at(c)] = first(c)[23:24]
            down[at(c)] = first(c)[8:9]
            up[at(5 + c)] = new(c)[23:24]
            down[at(5 + c)] = new(c)[8:9]
        up[at(10)] = -jnp.minimum(wind[23:24], 0.0)
        down[at(10)] = jnp.maximum(wind[8:9], 0.0)

    def mend(z, carry):
        for tile in range(2):
            gain = source[z, :, span(tile)]
            base[z + 1, tile] = base_in[z + 1, tile] + gain
            u = coef[UX, z + 1, tile]
            if tile == 0:
                weight, turn = jnp.where(lane == 0, jnp.maximum(u, 0.0), 0.0), 1
            else:
                weight, turn = jnp.where(lane == LANES - 1, -jnp.minimum(u, 0.0), 0.0), -1
            for c in range(5):
                edge = pltpu.roll(joint[c], (2 * LANES - HALO + turn - 8 * z) % LANES, 1)
                s1[c, z + 1, tile, OWN] = (
                    s1_in[c, z + 1, tile, OWN]
                    - gain * field[c, z + 1, tile, OWN]
                    + weight * edge
                )
            put(
                z,
                tile,
                lambda c: field.at[c, z + 1, tile],
                lambda c: s1.at[c, z + 1, tile],
                uy.at[z + 1, tile],
            )
        return carry

    clear_planes(s1)
    lax.fori_loop(0, layers, mend, 0)
    for side in range(2):
        put(
            None,
            side,
            lambda c: strip_s0.at[c, side],
            lambda c: strip_s1.at[c, side],
            strip_uy.at[side],
        )


def cd_flags(axis_cd):
    cd = lax.axis_index(axis_cd)
    return cd > 0, cd < lax.axis_size(axis_cd) - 1


def second_kernel(
    axis_cd,
    s1_in,
    strip_s1_in,
    coef,
    base,
    uy,
    tgt,
    strip_coef,
    strip_base,
    strip_uy,
    strip_tgt,
    own_up,
    own_down,
    from_below,
    from_above,
    s2,
    adj1,
    strip_adj1,
    dots,
    up,
    down,
    s1,
    strip_s1,
    adj2,
    strip_adj2,
    joint,
    joint2,
):
    layers = tgt.shape[1]
    has_below, has_above = cd_flags(axis_cd)

    def mend(target, wind, z, tile):
        def at(place):
            return line(z, tile * 11 + place, 22, layers)

        low_u, high_u = jnp.maximum(wind[8:9], 0.0), -jnp.minimum(wind[23:24], 0.0)
        low_n, high_n = from_below[at(10)], from_above[at(10)]
        for c in range(5):
            old, new = at(c), at(5 + c)
            ref = target(c)
            low = from_below[new] + low_n * own_down[old]
            high = from_above[new] + high_n * own_up[old]
            ref[7:8] = jnp.where(has_below, low, 0.0)
            ref[24:25] = jnp.where(has_above, high, 0.0)
            ref[8:9] = ref[8:9] + jnp.where(has_below, low_u * from_below[old], 0.0)
            ref[23:24] = ref[23:24] + jnp.where(has_above, high_u * from_above[old], 0.0)

    def mend_layer(z, carry):
        for tile in range(2):
            for c in range(5):
                s1[c, z + 1, tile, OWN] = s1_in[c, z + 1, tile, OWN]
            mend(lambda c: s1.at[c, z + 1, tile], uy.at[z + 1, tile], z, tile)
        return carry

    lax.fori_loop(0, layers, mend_layer, 0)
    clear_planes(s1)
    for side in range(2):
        for c in range(5):
            strip_s1[c, side, OWN] = strip_s1_in[c, side, OWN]
        mend(lambda c: strip_s1.at[c, side], strip_uy.at[side], None, side)

    state, delta = Field(s1, strip_s1, joint), Field(adj2, strip_adj2, joint2)
    state.join()
    delta.clear()
    delta.clear_strips()

    for side in range(2):
        m, damp = coefficients(strip_coef, strip_base, side)
        wind = (strip_coef[UX, side], strip_uy[side, OWN], strip_coef[UZ, side])
        a = [strip_s1[c, side, OWN] for c in range(5)]
        spin = strip_coef[SPREAD, side]
        out = forward(a, m, damp, spin, wind, state.strip_around(side))
        for c in range(5):
            strip_adj2[c, side, OWN] = out[c] - strip_tgt[c, side]
    delta.join()

    def advance(z, carry):
        for tile in range(2):
            at = (z + 1, tile)
            m, damp = coefficients(coef, base, *at)
            wind = (coef[(UX,) + at], uy[at + (OWN,)], coef[(UZ,) + at])
            a = [state.own(c, z, tile) for c in range(5)]
            out = forward(a, m, damp, coef[(SPREAD,) + at], wind, state.around(z, tile))
            total = 0.0
            for c in range(5):
                miss = out[c] - tgt[c, z, :, span(tile)]
                s2[c, z, :, span(tile)] = out[c]
                adj2[c, z + 1, tile, OWN] = miss
                total = total + miss * a[c]
            dots[z, :, span(tile)] = total
        return carry

    lax.fori_loop(0, layers, advance, 0)

    def put(z, tile, first, new, wind):
        def at(place):
            return line(z, tile * 10 + place, 20, layers)

        high, low = -jnp.minimum(wind[23:24], 0.0), jnp.maximum(wind[8:9], 0.0)
        for c in range(5):
            up[at(c)] = high * first(c)[23:24]
            down[at(c)] = low * first(c)[8:9]
            up[at(5 + c)] = high * new(c)[23:24]
            down[at(5 + c)] = low * new(c)[8:9]

    for side in range(2):
        m, damp = coefficients(strip_coef, strip_base, side)
        a = [strip_s1[c, side, OWN] for c in range(5)]
        b = [strip_adj2[c, side, OWN] for c in range(5)]
        wind = strip_back_wind(strip_coef, strip_uy, side)
        out = backward(b, a, m, damp, wind, delta.strip_around(side))
        for c in range(5):
            strip_adj1[c, side, OWN] = out[c]
        put(
            None,
            side,
            lambda c: strip_adj2.at[c, side],
            lambda c: strip_adj1.at[c, side],
            strip_uy.at[side],
        )
    edge_x = merged(strip_coef, UX, slice(None))

    def retreat(z, carry):
        for tile in range(2):
            at = (z + 1, tile)
            m, damp = coefficients(coef, base, *at)
            a = [state.own(c, z, tile) for c in range(5)]
            b = [delta.own(c, z, tile) for c in range(5)]
            wind = back_wind(coef, uy, edge_x, z, tile)
            out = backward(b, a, m, damp, wind, delta.around(z, tile))
            for c in range(5):
                adj1[c, z + 1, tile, OWN] = out[c]
            put(
                z,
                tile,
                lambda c: adj2.at[c, z + 1, tile],
                lambda c: adj1.at[c, z + 1, tile],
                uy.at[z + 1, tile],
            )
        return carry

    lax.fori_loop(0, layers, retreat, 0)


def third_kernel(
    axis_md,
    axis_cd,
    adj1_in,
    strip_adj1_in,
    dots,
    field,
    from_below,
    from_above,
    start,
    end,
    column,
    adj1,
    strip_adj1,
    first,
    kept,
    second,
    sens,
):
    layers, height, length = dots.shape
    md = lax.axis_index(axis_md)
    count = lax.axis_size(axis_md)
    has_below, has_above = cd_flags(axis_cd)
    odd = lax.axis_index(axis_cd) % 2 == 1

    row = row_iota((height, LANES))
    top = height - 1

    def mended(value, z, place):
        at = line(z, place, 20, layers)
        low = jnp.where(has_below, from_below[at], 0.0)
        high = jnp.where(has_above, from_above[at], 0.0)
        return value + jnp.where(row == 0, low, jnp.where(row == top, high, 0.0))

    for side in range(2):
        for c in range(5):
            value = strip_adj1_in[c, side, OWN]
            strip_adj1[c, side, OWN] = mended(value, None, side * 10 + c)
    Field(adj1, strip_adj1).clear()

    def weigh(z, carry):
        for tile in range(2):
            total = dots[z, :, span(tile)]
            for c in range(5):
                value = mended(adj1_in[c, z + 1, tile, OWN], z, tile * 10 + c)
                adj1[c, z + 1, tile, OWN] = value
                total = total + value * field[c, z + 1, tile, OWN]
            sens[z, :, span(tile)] = -DT * total
        return carry

    lax.fori_loop(0, layers, weigh, 0)

    def feet(ref):
        return jnp.concatenate([feet_block(ref, md + d, count) for d in (-1, 0, 1)], axis=1)

    starts, ends, columns = feet(start), feet(end), feet(column)
    needles = starts.shape[1]
    cells = row_iota((length, needles)) + md * length
    cover = jnp.where((cells >= starts) & (cells < ends), 1.0, 0.0).astype(jnp.bfloat16)
    product = jnp.zeros((layers * height, needles), F32)
    for part in split_three(sens[...].reshape(layers * height, length)):
        product = product + jnp.dot(
            part.astype(jnp.bfloat16), cover, preferred_element_type=F32
        )
    picked = jnp.where(row_iota((height, needles)) == columns, 1.0, 0.0)
    for z in range(layers):
        total = jnp.sum(
            product[z * height : (z + 1) * height] * picked, axis=0, keepdims=True
        )
        first[z : z + 1] = jnp.where(odd, total[:, span(0)], total[:, span(2)])
        kept[z : z + 1] = total[:, span(1)]
        second[z : z + 1] = jnp.where(odd, total[:, span(2)], total[:, span(0)])


def fourth_kernel(
    axis_cd,
    adj1,
    strip_adj1,
    field,
    coef,
    base,
    uy,
    strip_coef,
    weights_below,
    weights_above,
    own_up,
    own_down,
    from_below,
    from_above,
    adj0,
    joint,
):
    layers, height = adj0.shape[1], adj0.shape[2]
    top = height - 1
    has_below, has_above = cd_flags(axis_cd)
    delta = Field(adj1, strip_adj1, joint)
    delta.join()
    edge_x = merged(strip_coef, UX, slice(None))

    def retreat(z, carry):
        for tile in range(2):
            at = (z + 1, tile)
            m, damp = coefficients(coef, base, *at)
            a = [field[c, z + 1, tile, OWN] for c in range(5)]
            b = [delta.own(c, z, tile) for c in range(5)]
            wind = back_wind(coef, uy, edge_x, z, tile)
            out = backward(b, a, m, damp, wind, delta.around(z, tile))
            weight = line(z, tile * 11 + 10, 22, layers)
            low_n, high_n = weights_below[weight], weights_above[weight]
            lanes = span(tile)
            for c in range(5):
                old = line(z, tile * 10 + c, 20, layers)
                new = line(z, tile * 10 + 5 + c, 20, layers)
                low = from_below[new] + low_n * own_down[old]
                high = from_above[new] + high_n * own_up[old]
                low, high = jnp.where(has_below, low, 0.0), jnp.where(has_above, high, 0.0)
                adj0[c, z, :, lanes] = out[c]
                adj0[c, z, 0:1, lanes] = out[c][:1] + low
                adj0[c, z, top:, lanes] = out[c][top:] + high
        return carry

    lax.fori_loop(0, layers, retreat, 0)


def ring(value, axis, steps):
    count = lax.axis_size(axis)
    return lax.ppermute(value, axis, [(i, (i + steps) % count) for i in range(count)])


def winding(value, steps, turn):
    rows, columns = lax.axis_size("md"), lax.axis_size("cd")
    pairs = []
    for column in range(columns):
        for row in range(rows):
            target = row + (steps if column % 2 == turn else -steps)
            if 0 <= target < rows:
                pairs.append((row * columns + column, target * columns + column))
            else:
                pairs.append((row * columns + column, row * columns + (column ^ 1)))
    return lax.ppermute(value, ("md", "cd"), pairs)


def both_ways(value, steps):
    return winding(value, steps, 0), winding(value, steps, 1)


def shape_of(*dims, dtype=F32):
    return jax.ShapeDtypeStruct(dims, dtype)


def scratch(*dims, dtype=F32):
    return pltpu.VMEM(dims, dtype)


def cost(microseconds):
    return pl.CostEstimate(
        flops=int(microseconds * 1e6), bytes_accessed=int(microseconds * 3e6), transcendentals=0
    )


def params(mebibytes):
    return pltpu.CompilerParams(vmem_limit_bytes=mebibytes * 1024 * 1024)


def local(orientation, velocity, velocity_grad, rotary, target, needle_params, *feet):
    _, layers, height, length = orientation.shape
    rotary = rotary[None]
    rates = jnp.transpose(needle_params[:, 0, :])
    feet = [foot.reshape(1, -1) for foot in feet]
    padded = (layers + 2, 2, ROWS, LANES)
    plain = (layers + 2, 2, height, LANES)
    strip_padded, strip = (2, ROWS, LANES), (2, height, LANES)
    message, back_message = shape_of(22 * layers + 24, LANES), shape_of(20 * layers + 24, LANES)
    joint = scratch(5, height, LANES)

    hbm = pl.BlockSpec(memory_space=pltpu.HBM)
    blocks = 4
    packed = pl.pallas_call(
        pack_kernel,
        in_specs=[hbm] * 5 + [pl.BlockSpec(memory_space=pltpu.VMEM)],
        out_shape=shape_of(PLANES, height, LANES),
        scratch_shapes=[
            scratch(NEEDLES, layers, height, length),
            pltpu.SemaphoreType.DMA((blocks, 5)),
        ],
        compiler_params=params(62),
        cost_estimate=cost(4),
    )(orientation, velocity, velocity_grad, rotary, target, rates)
    far = both_ways(rates, 2)
    near = both_ways(packed, 1)

    field, coef, base, uy, s1 = pl.pallas_call(
        bulk_kernel,
        out_shape=[
            shape_of(5, *padded),
            shape_of(COEFS, *plain),
            shape_of(*plain),
            shape_of(*padded),
            shape_of(5, *padded),
        ],
        compiler_params=params(24),
        cost_estimate=cost(3),
    )(orientation, velocity, velocity_grad, rotary)

    s1, base, strip_s0, strip_coef, strip_base, strip_uy, strip_s1, strip_tgt, up, down = (
        pl.pallas_call(
            functools.partial(first_kernel, "md", "cd"),
            out_shape=[
                shape_of(5, *padded),
                shape_of(*plain),
                shape_of(5, *strip_padded),
                shape_of(COEFS, *strip),
                shape_of(*strip),
                shape_of(*strip_padded),
                shape_of(5, *strip_padded),
                shape_of(5, *strip),
                message,
                message,
            ],
            scratch_shapes=[
                scratch(3, layers * height, 4 * LANES, dtype=jnp.bfloat16),
                scratch(length + LANES, 4 * LANES, dtype=jnp.bfloat16),
                scratch(layers, height, length + LANES),
                joint,
            ],
            compiler_params=params(24),
        cost_estimate=cost(4),
        )(
            packed,
            *near,
            *far,
            *feet,
            field,
            coef,
            uy,
            base,
            s1,
        )
    )
    below = ring(up, "cd", 1)
    above = ring(down, "cd", -1)

    s2, adj1, strip_adj1, dots, back_up, back_down = pl.pallas_call(
        functools.partial(second_kernel, "cd"),
        out_shape=[
            shape_of(*orientation.shape),
            shape_of(5, *padded),
            shape_of(5, *strip_padded),
            shape_of(layers, height, length),
            back_message,
            back_message,
        ],
        scratch_shapes=[scratch(5, *padded), scratch(5, *strip_padded)] * 2 + [joint, joint],
        compiler_params=params(24),
        cost_estimate=cost(8),
    )(
        s1,
        strip_s1,
        coef,
        base,
        uy,
        target,
        strip_coef,
        strip_base,
        strip_uy,
        strip_tgt,
        up,
        down,
        below,
        above,
    )
    back_below = ring(back_up, "cd", 1)
    back_above = ring(back_down, "cd", -1)

    part = shape_of(*rates.shape)
    adj1, strip_adj1, part_first, part_own, part_second = pl.pallas_call(
        functools.partial(third_kernel, "md", "cd"),
        out_shape=[shape_of(5, *padded), shape_of(5, *strip_padded), part, part, part],
        scratch_shapes=[scratch(layers, height, length)],
        compiler_params=params(24),
        cost_estimate=cost(1),
    )(adj1, strip_adj1, dots, field, back_below, back_above, *feet)
    part_first = winding(part_first, 1, 0)
    part_second = winding(part_second, 1, 1)

    adj0 = pl.pallas_call(
        functools.partial(fourth_kernel, "cd"),
        out_shape=shape_of(*orientation.shape),
        scratch_shapes=[joint],
        compiler_params=params(24),
        cost_estimate=cost(4),
    )(
        adj1,
        strip_adj1,
        field,
        coef,
        base,
        uy,
        strip_coef,
        below,
        above,
        back_up,
        back_down,
        back_below,
        back_above,
    )
    gradient = part_own + part_first + part_second
    return s2, adj0, jnp.transpose(gradient)[:, None, :]


def solution(mesh):
    field = P(None, None, "cd", "md")
    feet = P(None, "cd")
    needles = P("md", "cd", None)
    return jax.shard_map(
        local,
        mesh=mesh,
        in_specs=(field, field, field, P(None, "cd", "md"), field, needles, feet, feet, feet),
        out_specs=(field, field, needles),
        check_vma=False,
    )
```

profile of v0, /device:TPU:105, one launch (start us, length us, event | category | flops | bytes accessed | tf_op | source)
XLA Modules:
  0.0 62.0 jit_solution(15297814242926436518)
XLA Ops:
  0.6 0.0 copy-start.9
  0.6 0.0 copy-start.1
  0.7 0.0 copy-start.4
  0.7 0.0 copy-start.6
  0.7 0.0 copy-start.7
  0.7 0.0 copy-start.8
  0.7 4.6 %shard_map.112.own = f32[24,16,128]{2,1,0:T(8,128)} custom-call(f32[5,16,16,256]{3,2,1,0:T(8,128)} %s0.3, f32[3,16,16,256]{3,2,1,0:T(8,128)} %vel.3, f32[9,16,16,256]{3,2,1,0:T(8,128)} %grad.3, f32[1,16,16,256]{3,2,1,0:T(8,128)} %bitcast.11, f32[5,16,16,256]{3,2,1,0:T(8,128)} %tgt.3, f32[16,128]{1,0:T(8,128)} %bitcast.19), custom_call_target="tpu_custom_call" | custom-call | flops 4000000 | bytes 12000000 | tf_op jit(solution)/shard_map/pallas_call | solution.py:817
  5.3 0.8 %collective-permute-start.1 = (f32[24,16,128]{2,1,0:T(8,128)}, f32[24,16,128]{2,1,0:T(8,128)S(1)}, u32[]{:S(2)}, u32[]{:S(2)}) collective-permute-start(f32[24,16,128]{2,1,0:T(8,128)} %shard_map.112.own), channel_id=1, source_target_pairs={{0,1},{8,0},{16,8},{24,16},{32,24},{40,32},{48,40},{56,48},{64,56}... | collective-permute-start | bytes 589832 | tf_op jit(solution)/shard_map/ppermute | solution.py:779
  6.1 3.2 %collective-permute-start = (f32[24,16,128]{2,1,0:T(8,128)}, f32[24,16,128]{2,1,0:T(8,128)S(1)}, u32[]{:S(2)}, u32[]{:S(2)}) collective-permute-start(f32[24,16,128]{2,1,0:T(8,128)} %shard_map.112.own), channel_id=1, source_target_pairs={{0,8},{8,16},{16,24},{24,32},{32,40},{40,48},{48,56},{56,64},{64,7... | collective-permute-start | bytes 589832 | tf_op jit(solution)/shard_map/ppermute | solution.py:779
  9.3 0.0 copy-done.9
  9.3 0.0 collective-permute-start.3
  9.3 3.6 %collective-permute-start.2 = (f32[16,128]{1,0:T(8,128)S(1)}, f32[16,128]{1,0:T(8,128)S(1)}, u32[]{:S(2)}, u32[]{:S(2)}) collective-permute-start(f32[16,128]{1,0:T(8,128)S(1)} %bitcast.21), channel_id=1, source_target_pairs={{0,16},{8,24},{16,32},{24,40},{32,48},{40,56},{48,64},{56,72},{64,... | collective-permute-start | bytes 24584 | tf_op jit(solution)/shard_map/ppermute | solution.py:779
  12.9 0.0 copy-done.1
  12.9 0.0 copy-done.4
  12.9 0.0 copy-start
  12.9 1.7 %copy-done = f32[9,16,16,256]{3,2,1,0:T(8,128)S(1)} copy-done((f32[9,16,16,256]{3,2,1,0:T(8,128)S(1)}, f32[9,16,16,256]{3,2,1,0:T(8,128)}, u32[]{:S(2)}) %copy-start) | copy-done | bytes 2359320
  14.5 0.0 copy-start.3
  14.5 1.1 %copy-done.3 = f32[3,16,16,256]{3,2,1,0:T(8,128)S(1)} copy-done((f32[3,16,16,256]{3,2,1,0:T(8,128)S(1)}, f32[3,16,16,256]{3,2,1,0:T(8,128)}, u32[]{:S(2)}) %copy-start.3) | copy-done | bytes 786456
  15.7 0.0 copy-start.5
  15.7 2.6 %shard_map.113 = (f32[5,18,2,32,128]{4,3,2,1,0:T(8,128)S(1)}, f32[11,18,2,16,128]{4,3,2,1,0:T(8,128)S(1)}, f32[18,2,16,128]{3,2,1,0:T(8,128)S(1)}, f32[18,2,32,1...) custom-call(f32[5,16,16,256]{3,2,1,0:T(8,128)S(1)} %copy-done.1, f32[3,16,16,256]{3,2,1,0:T(8,128)S(1)} %copy-done.3, ...), custom_call_target="tpu_custom_call" | custom-call | flops 3000000 | bytes 9000000 | tf_op jit(solution)/shard_map/pallas_call | solution.py:831
  18.2 0.0 collective-permute-done.3.far_second
  18.2 0.0 collective-permute-done.2.far_first
  18.3 0.0 collective-permute-done.1.near_second
  18.3 0.0 collective-permute-done.near_first
  18.3 0.0 copy-done.6
  18.3 0.0 copy-done.7
  18.3 0.0 copy-done.8
  18.3 0.0 copy-done.5
  18.3 0.0 copy-start.2
  18.3 3.1 %shard_map.114 = (f32[5,18,2,32,128]{4,3,2,1,0:T(8,128)S(1)}, f32[18,2,16,128]{3,2,1,0:T(8,128)S(1)}, f32[5,2,32,128]{3,2,1,0:T(8,128)}, f32[11,2,16,128]{3,2,1,...) custom-call(f32[24,16,128]{2,1,0:T(8,128)S(1)} %copy-done.5, ...), custom_call_target="tpu_custom_call" | custom-call | flops 4000000 | bytes 12000000 | tf_op jit(solution)/shard_map/pallas_call | solution.py:845
  21.5 0.2 collective-permute-start.4
  21.7 4.8 %collective-permute-start.5 = (f32[376,128]{1,0:T(8,128)S(1)}, f32[376,128]{1,0:T(8,128)S(1)}, u32[]{:S(2)}, u32[]{:S(2)}) collective-permute-start(f32[376,128]{1,0:T(8,128)S(1)} %get-tuple-element.41.own_down), channel_id=1, source_target_pairs={{0,7},{1,0},{2,1},{3,2},{4,3},{5,4},{6,5},{7,6},{8,15},{9,8},{10,9... | collective-permute-start | bytes 577544 | tf_op jit(solution)/shard_map/ppermute | solution.py:766
  26.5 5.3 %collective-permute-done.4.from_below.weights_below = f32[376,128]{1,0:T(8,128)S(1)} collective-permute-done((f32[376,128]{1,0:T(8,128)S(1)}, f32[376,128]{1,0:T(8,128)S(1)}, u32[]{:S(2)}, u32[]{:S(2)}) %collective-permute-start.4) | collective-permute-done | bytes 192544 | tf_op jit(solution)/shard_map/ppermute | solution.py:766
  31.9 1.6 %collective-permute-done.5.from_above.weights_above = f32[376,128]{1,0:T(8,128)S(1)} collective-permute-done((f32[376,128]{1,0:T(8,128)S(1)}, f32[376,128]{1,0:T(8,128)S(1)}, u32[]{:S(2)}, u32[]{:S(2)}) %collective-permute-start.5) | collective-permute-done | bytes 192544 | tf_op jit(solution)/shard_map/ppermute | solution.py:766
  33.5 0.0 copy-done.2
  33.5 8.2 %shard_map.115 = (f32[5,16,16,256]{3,2,1,0:T(8,128)}, f32[5,18,2,32,128]{4,3,2,1,0:T(8,128)S(1)}, f32[5,2,32,128]{3,2,1,0:T(8,128)S(1)}, f32[16,16,256]{2,1,0:T(...) custom-call(f32[5,18,2,32,128]{4,3,2,1,0:T(8,128)S(1)} %get-tuple-element.33.s1_in, ...), custom_call_target="tpu_custom_call" | custom-call | flops 8000000 | bytes 24000000 | tf_op jit(solution)/shard_map/pallas_call | solution.py:882
  41.7 0.3 collective-permute-start.6
  41.9 4.8 %collective-permute-start.7 = (f32[344,128]{1,0:T(8,128)S(1)}, f32[344,128]{1,0:T(8,128)S(1)}, u32[]{:S(2)}, u32[]{:S(2)}) collective-permute-start(f32[344,128]{1,0:T(8,128)S(1)} %get-tuple-element.47.own_down), channel_id=1, source_target_pairs={{0,7},{1,0},{2,1},{3,2},{4,3},{5,4},{6,5},{7,6},{8,15},{9,8},{10,9... | collective-permute-start | bytes 528392 | tf_op jit(solution)/shard_map/ppermute | solution.py:766
  46.7 2.9 %collective-permute-done.6.from_below = f32[344,128]{1,0:T(8,128)S(1)} collective-permute-done((f32[344,128]{1,0:T(8,128)S(1)}, f32[344,128]{1,0:T(8,128)S(1)}, u32[]{:S(2)}, u32[]{:S(2)}) %collective-permute-start.6) | collective-permute-done | bytes 176160 | tf_op jit(solution)/shard_map/ppermute | solution.py:766
  49.7 3.9 %collective-permute-done.7.from_above = f32[344,128]{1,0:T(8,128)S(1)} collective-permute-done((f32[344,128]{1,0:T(8,128)S(1)}, f32[344,128]{1,0:T(8,128)S(1)}, u32[]{:S(2)}, u32[]{:S(2)}) %collective-permute-start.7) | collective-permute-done | bytes 176160 | tf_op jit(solution)/shard_map/ppermute | solution.py:766
  53.6 1.0 %shard_map.116 = (f32[5,18,2,32,128]{4,3,2,1,0:T(8,128)S(1)}, f32[5,2,32,128]{3,2,1,0:T(8,128)S(1)}, f32[16,128]{1,0:T(8,128)S(1)}, f32[16,128]{1,0:T(8,128)S(1)}, f32[16,128]{1,0:T(8,128)S(1)}) custom-call(f32[5,18,2,32,128]{4,3,2,1,0:T(8,128)S(1)} %get-tuple-element.43.adj1_in, f32[5,2,32,128]{3,2,1,0:T(8,128)S(1)} %get-tuple-element.44.strip_adj1_in, ...), custom_call_target="tpu_custom_call" | custom-call | flops 1000000 | bytes 3000000 | tf_op jit(solution)/shard_map/pallas_call | solution.py:915
  54.5 1.7 %collective-permute-start.8 = (f32[16,128]{1,0:T(8,128)S(1)}, f32[16,128]{1,0:T(8,128)S(1)}, u32[]{:S(2)}, u32[]{:S(2)}) collective-permute-start(f32[16,128]{1,0:T(8,128)S(1)} %get-tuple-element.51), channel_id=1, source_target_pairs={{0,8},{8,16},{16,24},{24,32},{32,40},{40,48},{48,56},{56,64},{64,7... | collective-permute-start | bytes 24584 | tf_op jit(solution)/shard_map/ppermute | solution.py:779
  56.2 0.0 collective-permute-start.9
  56.2 4.4 %shard_map.117 = f32[5,16,16,256]{3,2,1,0:T(8,128)} custom-call(f32[5,18,2,32,128]{4,3,2,1,0:T(8,128)S(1)} %get-tuple-element.48.adj1, f32[5,2,32,128]{3,2,1,0:T(8,128)S(1)} %get-tuple-element.49.strip_adj1, f32[5,18,2,32,128]{4,3,2,1,0:T(8,128)S(1)} %get-tuple-element.28.field, f32[11,18,2,16,128]{4,3,2,1,0:T(8,128)S(1)} %get-tuple-element.29.coef, ...), custom_call_target="tpu_custom_call" | custom-call | flops 4000000 | bytes 12000000 | tf_op jit(solution)/shard_map/pallas_call | solution.py:925
  60.6 0.0 collective-permute-done.8
  60.6 0.8 %collective-permute-done.9 = f32[16,128]{1,0:T(8,128)S(1)} collective-permute-done((f32[16,128]{1,0:T(8,128)S(1)}, f32[16,128]{1,0:T(8,128)S(1)}, u32[]{:S(2)}, u32[]{:S(2)}) %collective-permute-start.9) | collective-permute-done | bytes 8224 | tf_op jit(solution)/shard_map/ppermute | solution.py:779
  61.4 0.6 add_bitcast_fusion
Async XLA Ops:
  0.6 8.7 %copy-start.9 = (f32[128,1,16]{0,2,1:T(8,128)S(1)}, f32[128,1,16]{0,2,1:T(8,128)}, u32[]{:S(2)}) copy-start(f32[128,1,16]{0,2,1:T(8,128)} %param.14) | copy-start | bytes 24580
  0.6 12.2 %copy-start.1 = (f32[5,16,16,256]{3,2,1,0:T(8,128)S(1)}, f32[5,16,16,256]{3,2,1,0:T(8,128)}, u32[]{:S(2)}) copy-start(f32[5,16,16,256]{3,2,1,0:T(8,128)} %s0.3) | copy-start | bytes 3932164
  0.7 12.2 %copy-start.4 = (f32[16,16,256]{2,1,0:T(8,128)S(1)}, f32[16,16,256]{2,1,0:T(8,128)}, u32[]{:S(2)}) copy-start(f32[16,16,256]{2,1,0:T(8,128)} %param.12) | copy-start | bytes 786436
  0.7 17.6 %copy-start.6 = (s32[4096,1]{0,1:T(1,128)S(1)}, s32[4096,1]{0,1:T(1,128)}, u32[]{:S(2)}) copy-start(s32[4096,1]{0,1:T(1,128)} %param.15) | copy-start | bytes 49156
  0.7 17.6 %copy-start.7 = (s32[4096,1]{0,1:T(1,128)S(1)}, s32[4096,1]{0,1:T(1,128)}, u32[]{:S(2)}) copy-start(s32[4096,1]{0,1:T(1,128)} %param.16) | copy-start | bytes 49156
  0.7 17.6 %copy-start.8 = (s32[4096,1]{0,1:T(1,128)S(1)}, s32[4096,1]{0,1:T(1,128)}, u32[]{:S(2)}) copy-start(s32[4096,1]{0,1:T(1,128)} %param.17) | copy-start | bytes 49156
  5.3 12.9 %collective-permute-start.1 = (f32[24,16,128]{2,1,0:T(8,128)}, f32[24,16,128]{2,1,0:T(8,128)S(1)}, u32[]{:S(2)}, u32[]{:S(2)}) collective-permute-start(f32[24,16,128]{2,1,0:T(8,128)} %shard_map.112.own), channel_id=1, source_target_pairs={{0,1},{8,0},{16,8},{24,16},{32,24},{40,32},{48,40},{56,48},{64,56}... | collective-permute-start | bytes 589832 | tf_op jit(solution)/shard_map/ppermute | solution.py:779
  6.1 12.2 %collective-permute-start = (f32[24,16,128]{2,1,0:T(8,128)}, f32[24,16,128]{2,1,0:T(8,128)S(1)}, u32[]{:S(2)}, u32[]{:S(2)}) collective-permute-start(f32[24,16,128]{2,1,0:T(8,128)} %shard_map.112.own), channel_id=1, source_target_pairs={{0,8},{8,16},{16,24},{24,32},{32,40},{40,48},{48,56},{56,64},{64,7... | collective-permute-start | bytes 589832 | tf_op jit(solution)/shard_map/ppermute | solution.py:779
  9.3 9.0 %collective-permute-start.3 = (f32[16,128]{1,0:T(8,128)S(1)}, f32[16,128]{1,0:T(8,128)S(1)}, u32[]{:S(2)}, u32[]{:S(2)}) collective-permute-start(f32[16,128]{1,0:T(8,128)S(1)} %bitcast.20), channel_id=1, source_target_pairs={{0,1},{8,9},{16,0},{24,8},{32,16},{40,24},{48,32},{56,40},{64,48},... | collective-permute-start | bytes 24584 | tf_op jit(solution)/shard_map/ppermute | solution.py:779
  9.3 9.0 %collective-permute-start.2 = (f32[16,128]{1,0:T(8,128)S(1)}, f32[16,128]{1,0:T(8,128)S(1)}, u32[]{:S(2)}, u32[]{:S(2)}) collective-permute-start(f32[16,128]{1,0:T(8,128)S(1)} %bitcast.21), channel_id=1, source_target_pairs={{0,16},{8,24},{16,32},{24,40},{32,48},{40,56},{48,64},{56,72},{64,... | collective-permute-start | bytes 24584 | tf_op jit(solution)/shard_map/ppermute | solution.py:779
  12.9 1.7 %copy-start = (f32[9,16,16,256]{3,2,1,0:T(8,128)S(1)}, f32[9,16,16,256]{3,2,1,0:T(8,128)}, u32[]{:S(2)}) copy-start(f32[9,16,16,256]{3,2,1,0:T(8,128)} %grad.3) | copy-start | bytes 7077892
  14.5 1.1 %copy-start.3 = (f32[3,16,16,256]{3,2,1,0:T(8,128)S(1)}, f32[3,16,16,256]{3,2,1,0:T(8,128)}, u32[]{:S(2)}) copy-start(f32[3,16,16,256]{3,2,1,0:T(8,128)} %vel.3) | copy-start | bytes 2359300
  15.7 2.6 %copy-start.5 = (f32[24,16,128]{2,1,0:T(8,128)S(1)}, f32[24,16,128]{2,1,0:T(8,128)}, u32[]{:S(2)}) copy-start(f32[24,16,128]{2,1,0:T(8,128)} %shard_map.112.own) | copy-start | bytes 589828
  18.3 15.2 %copy-start.2 = (f32[5,16,16,256]{3,2,1,0:T(8,128)S(1)}, f32[5,16,16,256]{3,2,1,0:T(8,128)}, u32[]{:S(2)}) copy-start(f32[5,16,16,256]{3,2,1,0:T(8,128)} %tgt.3) | copy-start | bytes 3932164
  21.5 10.4 %collective-permute-start.4 = (f32[376,128]{1,0:T(8,128)S(1)}, f32[376,128]{1,0:T(8,128)S(1)}, u32[]{:S(2)}, u32[]{:S(2)}) collective-permute-start(f32[376,128]{1,0:T(8,128)S(1)} %get-tuple-element.40.own_up), channel_id=1, source_target_pairs={{0,1},{1,2},{2,3},{3,4},{4,5},{5,6},{6,7},{7,0},{8,9},{9,10},{10,1... | collective-permute-start | bytes 577544 | tf_op jit(solution)/shard_map/ppermute | solution.py:766
  21.7 11.8 %collective-permute-start.5 = (f32[376,128]{1,0:T(8,128)S(1)}, f32[376,128]{1,0:T(8,128)S(1)}, u32[]{:S(2)}, u32[]{:S(2)}) collective-permute-start(f32[376,128]{1,0:T(8,128)S(1)} %get-tuple-element.41.own_down), channel_id=1, source_target_pairs={{0,7},{1,0},{2,1},{3,2},{4,3},{5,4},{6,5},{7,6},{8,15},{9,8},{10,9... | collective-permute-start | bytes 577544 | tf_op jit(solution)/shard_map/ppermute | solution.py:766
  41.7 8.0 %collective-permute-start.6 = (f32[344,128]{1,0:T(8,128)S(1)}, f32[344,128]{1,0:T(8,128)S(1)}, u32[]{:S(2)}, u32[]{:S(2)}) collective-permute-start(f32[344,128]{1,0:T(8,128)S(1)} %get-tuple-element.46.own_up), channel_id=1, source_target_pairs={{0,1},{1,2},{2,3},{3,4},{4,5},{5,6},{6,7},{7,0},{8,9},{9,10},{10,1... | collective-permute-start | bytes 528392 | tf_op jit(solution)/shard_map/ppermute | solution.py:766
  41.9 11.6 %collective-permute-start.7 = (f32[344,128]{1,0:T(8,128)S(1)}, f32[344,128]{1,0:T(8,128)S(1)}, u32[]{:S(2)}, u32[]{:S(2)}) collective-permute-start(f32[344,128]{1,0:T(8,128)S(1)} %get-tuple-element.47.own_down), channel_id=1, source_target_pairs={{0,7},{1,0},{2,1},{3,2},{4,3},{5,4},{6,5},{7,6},{8,15},{9,8},{10,9... | collective-permute-start | bytes 528392 | tf_op jit(solution)/shard_map/ppermute | solution.py:766
  54.5 6.0 %collective-permute-start.8 = (f32[16,128]{1,0:T(8,128)S(1)}, f32[16,128]{1,0:T(8,128)S(1)}, u32[]{:S(2)}, u32[]{:S(2)}) collective-permute-start(f32[16,128]{1,0:T(8,128)S(1)} %get-tuple-element.51), channel_id=1, source_target_pairs={{0,8},{8,16},{16,24},{24,32},{32,40},{40,48},{48,56},{56,64},{64,7... | collective-permute-start | bytes 24584 | tf_op jit(solution)/shard_map/ppermute | solution.py:779
  56.2 5.2 %collective-permute-start.9 = (f32[16,128]{1,0:T(8,128)S(1)}, f32[16,128]{1,0:T(8,128)S(1)}, u32[]{:S(2)}, u32[]{:S(2)}) collective-permute-start(f32[16,128]{1,0:T(8,128)S(1)} %get-tuple-element.52), channel_id=1, source_target_pairs={{0,1},{8,0},{16,8},{24,16},{32,24},{40,32},{48,40},{56,48},{64,56}... | collective-permute-start | bytes 24584 | tf_op jit(solution)/shard_map/ppermute | solution.py:779
where the time goes:
time: 62.5 us; the launch traced here: 62 us
  Pallas kernels  23.9 us (38%)
  starting transfers between devices  19.3 us (31%)
  waiting for transfers between devices  14.6 us (23%)
  local copies, waits for them, and re-layouts  2.83 us (5%)
  between operations  0.79 us (1%)
    ppermute x4, waiting for transfers between devices, ring(): lax.ppermute(value, axis, [(i, (i + steps) % count) for i in range(count)])  13.8 us
    ppermute x4, starting transfers between devices, ring(): lax.ppermute(value, axis, [(i, (i + steps) % count) for i in range(count)])  10.2 us
    ppermute x6, starting transfers between devices, winding(): return lax.ppermute(value, ('md', 'cd'), pairs)  9.16 us
    pallas_call x1, Pallas kernels, local(): pl.pallas_call(functools.partial(second_kernel, 'cd'), out_shape=[shape_o...  8.15 us
    pallas_call x1, Pallas kernels, local(): pl.pallas_call(pack_kernel, in_specs=[hbm] * 5 + [pl.BlockSpec(memory_spa...  4.65 us
    pallas_call x1, Pallas kernels, local(): pl.pallas_call(functools.partial(fourth_kernel, 'cd'), out_shape=shape_of...  4.39 us
    pallas_call x1, Pallas kernels, local(): pl.pallas_call(functools.partial(first_kernel, 'md', 'cd'), out_shape=[sh...  3.13 us
    unnamed x20, local copies, waits for them, and re-layouts  2.83 us
  transfers between devices with their start and end apart: 10, of which 5 were waited for; matrix products, arithmetic and copies ran while one was open for 0% of the time, Pallas kernels for 11%

commit v1 on v0

--- a/solution.py
+++ b/solution.py
@@ -207,6 +207,44 @@
     if z is None:
         return slice(count * layers + place, count * layers + place + 1)
     return pl.ds(place * layers + z, 1)
+
+
+def planes(place, layers):
+    return slice(place * layers, (place + 1) * layers)
+
+
+def row_place(ref, c, tile, row):
+    high, rows = ref.shape[-4], ref.shape[-2]
+    total = 1
+    for size in ref.shape[:-1]:
+        total *= size
+    at = ((c * high + 1) * 2 + tile) * rows + row
+    return ref.reshape(total, LANES), pl.ds(at, high - 2, stride=2 * rows)
+
+
+def row_of(ref, c, tile, row):
+    flat, place = row_place(ref, c, tile, row)
+    return flat[place, :]
+
+
+def set_row(ref, c, tile, row, value):
+    flat, place = row_place(ref, c, tile, row)
+    flat[place, :] = value
+
+
+def layer_pair(cur):
+    row, last = row_iota(cur.shape), cur.shape[0] - 1
+    behind = jnp.where(row == 0, 0.0, pltpu.roll(cur, 1, 0))
+    front = jnp.where(row == last, 0.0, pltpu.roll(cur, last, 0))
+    return behind, front
+
+
+def edge_column(left, right, layers):
+    shape = (layers, LANES)
+    lane, layer = lane_iota(shape), row_iota(shape)
+    low = jnp.sum(jnp.where(lane == 8 * layer + HALO - 1, left, 0.0), axis=1, keepdims=True)
+    high = jnp.sum(jnp.where(lane == 8 * layer + HALO, right, 0.0), axis=1, keepdims=True)
+    return jnp.where(lane == LANES - 1, low, jnp.where(lane == 0, high, 0.0))
 
 
 def back_wind(coef, uy, edge_x, z, tile):
@@ -438,15 +476,15 @@
             strip_s1[c, side, OWN] = out[c]
     state.join()
 
-    def put(z, tile, first, new, wind):
+    def put(side):
         def at(place):
-            return line(z, tile * 11 + place, 22, layers)
+            return line(None, side * 11 + place, 22, layers)
 
         for c in range(5):
-            up[at(c)] = first(c)[23:24]
-            down[at(c)] = first(c)[8:9]
-            up[at(5 + c)] = new(c)[23:24]
-            down[at(5 + c)] = new(c)[8:9]
+            first, new = strip_s0.at[c, side], strip_s1.at[c, side]
+            up[at(c)], down[at(c)] = first[23:24], first[8:9]
+            up[at(5 + c)], down[at(5 + c)] = new[23:24], new[8:9]
+        wind = strip_uy.at[side]
         up[at(10)] = -jnp.minimum(wind[23:24], 0.0)
         down[at(10)] = jnp.maximum(wind[8:9], 0.0)
 
@@ -466,25 +504,20 @@
                     - gain * field[c, z + 1, tile, OWN]
                     + weight * edge
                 )
-            put(
-                z,
-                tile,
-                lambda c: field.at[c, z + 1, tile],
-                lambda c: s1.at[c, z + 1, tile],
-                uy.at[z + 1, tile],
-            )
         return carry
 
     clear_planes(s1)
     lax.fori_loop(0, layers, mend, 0)
+    for tile in range(2):
+        for message, row in ((up, 23), (down, 8)):
+            for c in range(5):
+                message[planes(tile * 11 + c, layers)] = row_of(field, c, tile, row)
+                message[planes(tile * 11 + 5 + c, layers)] = row_of(s1, c, tile, row)
+        out, into = row_of(uy, 0, tile, 23), row_of(uy, 0, tile, 8)
+        up[planes(tile * 11 + 10, layers)] = -jnp.minimum(out, 0.0)
+        down[planes(tile * 11 + 10, layers)] = jnp.maximum(into, 0.0)
     for side in range(2):
-        put(
-            None,
-            side,
-            lambda c: strip_s0.at[c, side],
-            lambda c: strip_s1.at[c, side],
-            strip_uy.at[side],
-        )
+        put(side)
 
 
 def cd_flags(axis_cd):
@@ -492,14 +525,34 @@
     return cd > 0, cd < lax.axis_size(axis_cd) - 1
 
 
-def second_kernel(
+def advance_kernel(s1, strip_s1, coef, base, uy, tgt, s2, goal, joint):
+    layers = tgt.shape[1]
+    state = Field(s1, strip_s1, joint)
+    state.join()
+
+    def advance(z, carry):
+        for tile in range(2):
+            at = (z + 1, tile)
+            m, damp = coefficients(coef, base, *at)
+            wind = (coef[(UX,) + at], uy[at + (OWN,)], coef[(UZ,) + at])
+            a = [state.own(c, z, tile) for c in range(5)]
+            out = forward(a, m, damp, coef[(SPREAD,) + at], wind, state.around(z, tile))
+            for c in range(5):
+                s2[(c,) + at] = out[c]
+                goal[(c,) + at] = tgt[c, z, :, span(tile)]
+        return carry
+
+    lax.fori_loop(0, layers, advance, 0)
+
+
+def edge_kernel(
     axis_cd,
-    s1_in,
+    s1,
     strip_s1_in,
     coef,
     base,
     uy,
-    tgt,
+    goal,
     strip_coef,
     strip_base,
     strip_uy,
@@ -508,57 +561,37 @@
     own_down,
     from_below,
     from_above,
-    s2,
-    adj1,
+    s1_edge,
+    s2_edge,
+    strip_adj2,
     strip_adj1,
-    dots,
     up,
     down,
-    s1,
     strip_s1,
-    adj2,
-    strip_adj2,
-    joint,
-    joint2,
 ):
-    layers = tgt.shape[1]
+    layers = goal.shape[1] - 2
     has_below, has_above = cd_flags(axis_cd)
 
-    def mend(target, wind, z, tile):
+    state, delta = Field(s1, strip_s1), Field(s1, strip_adj2)
+    delta.clear_strips()
+    for side in range(2):
+
         def at(place):
-            return line(z, tile * 11 + place, 22, layers)
-
+            return line(None, side * 11 + place, 22, layers)
+
+        wind = strip_uy.at[side]
         low_u, high_u = jnp.maximum(wind[8:9], 0.0), -jnp.minimum(wind[23:24], 0.0)
         low_n, high_n = from_below[at(10)], from_above[at(10)]
         for c in range(5):
             old, new = at(c), at(5 + c)
-            ref = target(c)
+            ref = strip_s1.at[c, side]
+            ref[OWN] = strip_s1_in[c, side, OWN]
             low = from_below[new] + low_n * own_down[old]
             high = from_above[new] + high_n * own_up[old]
             ref[7:8] = jnp.where(has_below, low, 0.0)
             ref[24:25] = jnp.where(has_above, high, 0.0)
             ref[8:9] = ref[8:9] + jnp.where(has_below, low_u * from_below[old], 0.0)
             ref[23:24] = ref[23:24] + jnp.where(has_above, high_u * from_above[old], 0.0)
-
-    def mend_layer(z, carry):
-        for tile in range(2):
-            for c in range(5):
-                s1[c, z + 1, tile, OWN] = s1_in[c, z + 1, tile, OWN]
-            mend(lambda c: s1.at[c, z + 1, tile], uy.at[z + 1, tile], z, tile)
-        return carry
-
-    lax.fori_loop(0, layers, mend_layer, 0)
-    clear_planes(s1)
-    for side in range(2):
-        for c in range(5):
-            strip_s1[c, side, OWN] = strip_s1_in[c, side, OWN]
-        mend(lambda c: strip_s1.at[c, side], strip_uy.at[side], None, side)
-
-    state, delta = Field(s1, strip_s1, joint), Field(adj2, strip_adj2, joint2)
-    state.join()
-    delta.clear()
-    delta.clear_strips()
-
     for side in range(2):
         m, damp = coefficients(strip_coef, strip_base, side)
         wind = (strip_coef[UX, side], strip_uy[side, OWN], strip_coef[UZ, side])
@@ -567,71 +600,180 @@
         out = forward(a, m, damp, spin, wind, state.strip_around(side))
         for c in range(5):
             strip_adj2[c, side, OWN] = out[c] - strip_tgt[c, side]
-    delta.join()
-
-    def advance(z, carry):
-        for tile in range(2):
-            at = (z + 1, tile)
-            m, damp = coefficients(coef, base, *at)
-            wind = (coef[(UX,) + at], uy[at + (OWN,)], coef[(UZ,) + at])
-            a = [state.own(c, z, tile) for c in range(5)]
-            out = forward(a, m, damp, coef[(SPREAD,) + at], wind, state.around(z, tile))
-            total = 0.0
-            for c in range(5):
-                miss = out[c] - tgt[c, z, :, span(tile)]
-                s2[c, z, :, span(tile)] = out[c]
-                adj2[c, z + 1, tile, OWN] = miss
-                total = total + miss * a[c]
-            dots[z, :, span(tile)] = total
-        return carry
-
-    lax.fori_loop(0, layers, advance, 0)
-
-    def put(z, tile, first, new, wind):
+    for side in range(2):
+
         def at(place):
-            return line(z, tile * 10 + place, 20, layers)
-
-        high, low = -jnp.minimum(wind[23:24], 0.0), jnp.maximum(wind[8:9], 0.0)
-        for c in range(5):
-            up[at(c)] = high * first(c)[23:24]
-            down[at(c)] = low * first(c)[8:9]
-            up[at(5 + c)] = high * new(c)[23:24]
-            down[at(5 + c)] = low * new(c)[8:9]
-
-    for side in range(2):
+            return line(None, side * 10 + place, 20, layers)
+
         m, damp = coefficients(strip_coef, strip_base, side)
         a = [strip_s1[c, side, OWN] for c in range(5)]
         b = [strip_adj2[c, side, OWN] for c in range(5)]
         wind = strip_back_wind(strip_coef, strip_uy, side)
         out = backward(b, a, m, damp, wind, delta.strip_around(side))
+        high = -jnp.minimum(strip_uy[side, 23:24], 0.0)
+        low = jnp.maximum(strip_uy[side, 8:9], 0.0)
         for c in range(5):
             strip_adj1[c, side, OWN] = out[c]
-        put(
-            None,
-            side,
-            lambda c: strip_adj2.at[c, side],
-            lambda c: strip_adj1.at[c, side],
-            strip_uy.at[side],
-        )
+            up[at(c)] = high * b[c][-1:]
+            down[at(c)] = low * b[c][:1]
+            up[at(5 + c)] = high * out[c][-1:]
+            down[at(5 + c)] = low * out[c][:1]
+
+    def constants(tile, row):
+        m = {key: row_of(coef, place, tile, row) for key, place in PLACE.items()}
+        return m, row_of(base, 0, tile, row)
+
+    for number, (message, mine, valid, outgoing) in enumerate(
+        ((from_below, own_down, has_below, down), (from_above, own_up, has_above, up))
+    ):
+        rows = (0, 1, 2) if number == 0 else (15, 14, 13)
+        sides = (0, 1)
+
+        def plane(ref, place, tile):
+            return ref[planes(tile * 11 + place, layers)]
+
+        lines = [{}, {}, {}, {}]
+        for c in range(5):
+            for tile in range(2):
+                old, new = plane(message, c, tile), plane(message, 5 + c, tile)
+                weight = plane(message, 10, tile)
+                lines[0][c, tile] = jnp.where(
+                    valid, new + weight * plane(mine, c, tile), 0.0
+                )
+                lines[1][c, tile] = plane(mine, 5 + c, tile) + jnp.where(
+                    valid, plane(mine, 10, tile) * old, 0.0
+                )
+                s1_edge[c, number, tile] = lines[1][c, tile]
+                for k in (1, 2):
+                    lines[k + 1][c, tile] = row_of(s1, c, tile, 8 + rows[k])
+
+        def strip_edge(ref, c, row):
+            left, right = (ref[c, side, 8 + row : 9 + row] for side in sides)
+            return edge_column(left, right, layers)
+
+        def ordered(outer, inner):
+            return (outer, inner) if number == 0 else (inner, outer)
+
+        misses = [{}, {}]
+        for k in range(2):
+            row = rows[k]
+            edges = [strip_edge(strip_s1, c, row) for c in range(5)]
+            for tile in range(2):
+                m, damp = constants(tile, row)
+                wind = (
+                    row_of(coef, UX, tile, row),
+                    row_of(uy, 0, tile, 8 + row),
+                    row_of(coef, UZ, tile, row),
+                )
+                a = [lines[k + 1][c, tile] for c in range(5)]
+
+                def around(c):
+                    tiles = [lines[k + 1][c, t] for t in range(2)]
+                    return (
+                        x_pair(tiles, tile, edges[c]),
+                        ordered(lines[k][c, tile], lines[k + 2][c, tile]),
+                        layer_pair(a[c]),
+                    )
+
+                out = forward(a, m, damp, row_of(coef, SPREAD, tile, row), wind, around)
+                for c in range(5):
+                    s2_edge[c, 2 * number + k, tile] = out[c]
+                    misses[k][c, tile] = out[c] - row_of(goal, c, tile, row)
+
+        row = rows[0]
+        edges = [strip_edge(strip_adj2, c, row) for c in range(5)]
+        left, right = (strip_coef[UX, side, row : row + 1] for side in sides)
+        edge_x = edge_column(left, right, layers)
+        for tile in range(2):
+            m, damp = constants(tile, row)
+            a = [lines[1][c, tile] for c in range(5)]
+            b = [misses[0][c, tile] for c in range(5)]
+            zero = jnp.zeros_like(b[0])
+            wind = (
+                x_pair([row_of(coef, UX, t, row) for t in range(2)], tile, edge_x),
+                ordered(zero, row_of(uy, 0, tile, 8 + rows[1])),
+                layer_pair(row_of(coef, UZ, tile, row)),
+            )
+
+            def around(c):
+                tiles = [misses[0][c, t] for t in range(2)]
+                return (
+                    x_pair(tiles, tile, edges[c]),
+                    ordered(zero, misses[1][c, tile]),
+                    layer_pair(b[c]),
+                )
+
+            out = backward(b, a, m, damp, wind, around)
+            weight = plane(mine, 10, tile)
+            for c in range(5):
+                outgoing[planes(tile * 10 + c, layers)] = weight * b[c]
+                outgoing[planes(tile * 10 + 5 + c, layers)] = weight * out[c]
+
+
+def second_kernel(
+    s1_in,
+    s2_in,
+    goal,
+    s1_edge,
+    s2_edge,
+    coef,
+    base,
+    uy,
+    strip_coef,
+    strip_adj2,
+    s2_out,
+    adj1,
+    dots,
+    s1,
+    s2,
+    adj2,
+    joint,
+):
+    layers = goal.shape[1] - 2
+
+    def gather(z, carry):
+        for tile in range(2):
+            for c in range(5):
+                s1[c, z + 1, tile] = s1_in[c, z + 1, tile, OWN]
+                s2[c, z + 1, tile] = s2_in[c, z + 1, tile]
+        return carry
+
+    lax.fori_loop(0, layers, gather, 0)
+    for c in range(5):
+        for tile in range(2):
+            for number, row in enumerate((0, 15)):
+                set_row(s1, c, tile, row, s1_edge[c, number, tile])
+            for number, row in enumerate((0, 1, 15, 14)):
+                set_row(s2, c, tile, row, s2_edge[c, number, tile])
+
+    delta = Field(adj2, strip_adj2, joint)
+    delta.clear()
+    delta.join()
+
+    def compare(z, carry):
+        for tile in range(2):
+            total = 0.0
+            for c in range(5):
+                value = s2[c, z + 1, tile]
+                miss = value - goal[c, z + 1, tile]
+                s2_out[c, z, :, span(tile)] = value
+                adj2[c, z + 1, tile, OWN] = miss
+                total = total + miss * s1[c, z + 1, tile]
+            dots[z, :, span(tile)] = total
+        return carry
+
+    lax.fori_loop(0, layers, compare, 0)
     edge_x = merged(strip_coef, UX, slice(None))
 
     def retreat(z, carry):
         for tile in range(2):
-            at = (z + 1, tile)
-            m, damp = coefficients(coef, base, *at)
-            a = [state.own(c, z, tile) for c in range(5)]
+            m, damp = coefficients(coef, base, z + 1, tile)
+            a = [s1[c, z + 1, tile] for c in range(5)]
             b = [delta.own(c, z, tile) for c in range(5)]
             wind = back_wind(coef, uy, edge_x, z, tile)
             out = backward(b, a, m, damp, wind, delta.around(z, tile))
             for c in range(5):
                 adj1[c, z + 1, tile, OWN] = out[c]
-            put(
-                z,
-                tile,
-                lambda c: adj2.at[c, z + 1, tile],
-                lambda c: adj1.at[c, z + 1, tile],
-                uy.at[z + 1, tile],
-            )
         return carry
 
     lax.fori_loop(0, layers, retreat, 0)
@@ -879,26 +1021,33 @@
     below = ring(up, "cd", 1)
     above = ring(down, "cd", -1)
 
-    s2, adj1, strip_adj1, dots, back_up, back_down = pl.pallas_call(
-        functools.partial(second_kernel, "cd"),
+    s2_part, goal = pl.pallas_call(
+        advance_kernel,
+        out_shape=[shape_of(5, *plain), shape_of(5, *plain)],
+        scratch_shapes=[joint],
+        compiler_params=params(16),
+        cost_estimate=cost(4),
+    )(s1, strip_s1, coef, base, uy, target)
+    s1_edge, s2_edge, strip_adj2, strip_adj1, back_up, back_down = pl.pallas_call(
+        functools.partial(edge_kernel, "cd"),
         out_shape=[
-            shape_of(*orientation.shape),
-            shape_of(5, *padded),
+            shape_of(5, 2, 2, layers, LANES),
+            shape_of(5, 4, 2, layers, LANES),
             shape_of(5, *strip_padded),
-            shape_of(layers, height, length),
+            shape_of(5, *strip_padded),
             back_message,
             back_message,
         ],
-        scratch_shapes=[scratch(5, *padded), scratch(5, *strip_padded)] * 2 + [joint, joint],
-        compiler_params=params(24),
-        cost_estimate=cost(8),
+        scratch_shapes=[scratch(5, *strip_padded)],
+        compiler_params=params(16),
+        cost_estimate=cost(2),
     )(
         s1,
         strip_s1,
         coef,
         base,
         uy,
-        target,
+        goal,
         strip_coef,
         strip_base,
         strip_uy,
@@ -910,6 +1059,34 @@
     )
     back_below = ring(back_up, "cd", 1)
     back_above = ring(back_down, "cd", -1)
+
+    s2, adj1, dots = pl.pallas_call(
+        second_kernel,
+        out_shape=[
+            shape_of(*orientation.shape),
+            shape_of(5, *padded),
+            shape_of(layers, height, length),
+        ],
+        scratch_shapes=[
+            scratch(5, *plain),
+            scratch(5, *plain),
+            scratch(5, *padded),
+            joint,
+        ],
+        compiler_params=params(24),
+        cost_estimate=cost(6),
+    )(
+        s1,
+        s2_part,
+        goal,
+        s1_edge,
+        s2_edge,
+        coef,
+        base,
+        uy,
+        strip_coef,
+        strip_adj2,
+    )
 
     part = shape_of(*rates.shape)
     adj1, strip_adj1, part_first, part_own, part_second = pl.pallas_call(

time: 62.5 us -> 56.3 us (0.901)
  waiting for transfers between devices: 14.6 us -> 6.88 us
  Pallas kernels: 23.9 us -> 25.3 us
    ppermute x4, waiting for transfers between devices: 13.8 us -> 6.07 us  [ring(): lax.ppermute(value, axis, [(i, (i + steps) % count) for i in range(count)])]
    pallas_call x1 -> x3, Pallas kernels: 8.15 us -> 9.85 us  [the longest x1 4.89 us: local(): pl.pallas_call(second_kernel, out_shape=[shape_of(*orientation.shape), sh...]
  transfers between devices with their start and end apart: 10 -> 10, of which waited for: 5 -> 4; matrix products, arithmetic and copies ran while one was open for 0% -> 0% of each run, Pallas kernels for 11% -> 26%
where the time goes in v1:
time: 56.3 us; the launch traced here: 56.2 us
  Pallas kernels  25.3 us (45%)
  starting transfers between devices  19.8 us (35%)
  waiting for transfers between devices  6.88 us (12%)
  local copies, waits for them, and re-layouts  2.83 us (5%)
  between operations  0.8 us (1%)
  other arithmetic  0.6 us (1%)
    ppermute x4, starting transfers between devices, ring(): lax.ppermute(value, axis, [(i, (i + steps) % count) for i in range(count)])  10.2 us
    ppermute x6, starting transfers between devices, winding(): return lax.ppermute(value, ('md', 'cd'), pairs)  9.53 us
    ppermute x4, waiting for transfers between devices, ring(): lax.ppermute(value, axis, [(i, (i + steps) % count) for i in range(count)])  6.07 us
    pallas_call x1, Pallas kernels, local(): pl.pallas_call(second_kernel, out_shape=[shape_of(*orientation.shape), sh...  4.89 us
    pallas_call x1, Pallas kernels, local(): pl.pallas_call(pack_kernel, in_specs=[hbm] * 5 + [pl.BlockSpec(memory_spa...  4.65 us
    pallas_call x1, Pallas kernels, local(): pl.pallas_call(functools.partial(fourth_kernel, 'cd'), out_shape=shape_of...  4.38 us
    pallas_call x1, Pallas kernels, local(): pl.pallas_call(functools.partial(first_kernel, 'md', 'cd'), out_shape=[sh...  2.86 us
    unnamed x20, local copies, waits for them, and re-layouts  2.83 us
  transfers between devices with their start and end apart: 10, of which 4 were waited for; matrix products, arithmetic and copies ran while one was open for 0% of the time, Pallas kernels for 26%

profile of v1, /device:TPU:105, one launch (start us, length us, event | category | flops | bytes accessed | tf_op | source)
XLA Modules:
  0.0 56.2 jit_solution(2955280861178540075)
XLA Ops:
  0.6 0.0 copy-start.9
  0.6 0.0 copy-start.1
  0.7 0.0 copy-start.4
  0.7 0.0 copy-start.6
  0.7 0.0 copy-start.7
  0.7 0.0 copy-start.8
  0.7 4.6 %shard_map.112.own = f32[24,16,128]{2,1,0:T(8,128)} custom-call(f32[5,16,16,256]{3,2,1,0:T(8,128)} %s0.3, f32[3,16,16,256]{3,2,1,0:T(8,128)} %vel.3, f32[9,16,16,256]{3,2,1,0:T(8,128)} %grad.3, f32[1,16,16,256]{3,2,1,0:T(8,128)} %bitcast.11, f32[5,16,16,256]{3,2,1,0:T(8,128)} %tgt.3, f32[16,128]{1,0:T(8,128)} %bitcast.19), custom_call_target="tpu_custom_call" | custom-call | flops 4000000 | bytes 12000000 | tf_op jit(solution)/shard_map/pallas_call | solution.py:959
  5.3 0.8 %collective-permute-start.1 = (f32[24,16,128]{2,1,0:T(8,128)}, f32[24,16,128]{2,1,0:T(8,128)S(1)}, u32[]{:S(2)}, u32[]{:S(2)}) collective-permute-start(f32[24,16,128]{2,1,0:T(8,128)} %shard_map.112.own), channel_id=1, source_target_pairs={{0,1},{8,0},{16,8},{24,16},{32,24},{40,32},{48,40},{56,48},{64,56}... | collective-permute-start | bytes 589832 | tf_op jit(solution)/shard_map/ppermute | solution.py:921
  6.1 3.2 %collective-permute-start = (f32[24,16,128]{2,1,0:T(8,128)}, f32[24,16,128]{2,1,0:T(8,128)S(1)}, u32[]{:S(2)}, u32[]{:S(2)}) collective-permute-start(f32[24,16,128]{2,1,0:T(8,128)} %shard_map.112.own), channel_id=1, source_target_pairs={{0,8},{8,16},{16,24},{24,32},{32,40},{40,48},{48,56},{56,64},{64,7... | collective-permute-start | bytes 589832 | tf_op jit(solution)/shard_map/ppermute | solution.py:921
  9.3 0.0 copy-done.9
  9.3 0.0 collective-permute-start.3
  9.3 3.6 %collective-permute-start.2 = (f32[16,128]{1,0:T(8,128)S(1)}, f32[16,128]{1,0:T(8,128)S(1)}, u32[]{:S(2)}, u32[]{:S(2)}) collective-permute-start(f32[16,128]{1,0:T(8,128)S(1)} %bitcast.21), channel_id=1, source_target_pairs={{0,16},{8,24},{16,32},{24,40},{32,48},{40,56},{48,64},{56,72},{64,... | collective-permute-start | bytes 24584 | tf_op jit(solution)/shard_map/ppermute | solution.py:921
  12.9 0.0 copy-done.1
  12.9 0.0 copy-done.4
  12.9 0.0 copy-start
  12.9 1.7 %copy-done = f32[9,16,16,256]{3,2,1,0:T(8,128)S(1)} copy-done((f32[9,16,16,256]{3,2,1,0:T(8,128)S(1)}, f32[9,16,16,256]{3,2,1,0:T(8,128)}, u32[]{:S(2)}) %copy-start) | copy-done | bytes 2359320
  14.5 0.0 copy-start.3
  14.5 1.1 %copy-done.3 = f32[3,16,16,256]{3,2,1,0:T(8,128)S(1)} copy-done((f32[3,16,16,256]{3,2,1,0:T(8,128)S(1)}, f32[3,16,16,256]{3,2,1,0:T(8,128)}, u32[]{:S(2)}) %copy-start.3) | copy-done | bytes 786456
  15.7 2.6 %shard_map.113 = (f32[5,18,2,32,128]{4,3,2,1,0:T(8,128)S(1)}, f32[11,18,2,16,128]{4,3,2,1,0:T(8,128)S(1)}, f32[18,2,16,128]{3,2,1,0:T(8,128)S(1)}, f32[18,2,32,1...) custom-call(f32[5,16,16,256]{3,2,1,0:T(8,128)S(1)} %copy-done.1, f32[3,16,16,256]{3,2,1,0:T(8,128)S(1)} %copy-done.3, ...), custom_call_target="tpu_custom_call" | custom-call | flops 3000000 | bytes 9000000 | tf_op jit(solution)/shard_map/pallas_call | solution.py:973
  18.2 0.0 collective-permute-done.3.far_second
  18.2 0.0 collective-permute-done.2.far_first
  18.3 0.0 collective-permute-done.1.near_second
  18.3 0.0 collective-permute-done.near_first
  18.3 0.0 copy-done.6
  18.3 0.0 copy-done.7
  18.3 0.0 copy-done.8
  18.3 0.0 copy-done.5
  18.3 0.0 copy-start.2
  18.3 2.9 %shard_map.114 = (f32[5,18,2,32,128]{4,3,2,1,0:T(8,128)S(1)}, f32[18,2,16,128]{3,2,1,0:T(8,128)S(1)}, f32[5,2,32,128]{3,2,1,0:T(8,128)}, f32[11,2,16,128]{3,2,1,...) custom-call(f32[24,16,128]{2,1,0:T(8,128)S(1)} %copy-done.5, ...), custom_call_target="tpu_custom_call" | custom-call | flops 4000000 | bytes 12000000 | tf_op jit(solution)/shard_map/pallas_call | solution.py:987
  21.2 0.2 collective-permute-start.4
  21.4 4.8 %collective-permute-start.5 = (f32[376,128]{1,0:T(8,128)S(1)}, f32[376,128]{1,0:T(8,128)S(1)}, u32[]{:S(2)}, u32[]{:S(2)}) collective-permute-start(f32[376,128]{1,0:T(8,128)S(1)} %get-tuple-element.48.own_down), channel_id=1, source_target_pairs={{0,7},{1,0},{2,1},{3,2},{4,3},{5,4},{6,5},{7,6},{8,15},{9,8},{10,9... | collective-permute-start | bytes 577544 | tf_op jit(solution)/shard_map/ppermute | solution.py:908
  26.3 0.0 copy-done.2
  26.3 2.8 %shard_map.115 = (f32[5,18,2,16,128]{4,3,2,1,0:T(8,128)S(1)}, f32[5,18,2,16,128]{4,3,2,1,0:T(8,128)S(1)}) custom-call(f32[5,18,2,32,128]{4,3,2,1,0:T(8,128)S(1)} %get-tuple-element.38.s1.s1_in, f32[5,2,32,128]{3,2,1,0:T(8,128)S(1)} %get-tuple-element.39.strip_s1.strip_s1_in, f32[11,18,2,16,128]{4,3,2,1,0:T(8,128)S(1)} %get-tuple-element.34.coef, ...), custom_call_target="tpu_custom_call" | custom-call | flops 4000000 | bytes 12000000 | tf_op jit(solution)/shard_map/pallas_call | solution.py:1024
  29.1 2.5 %collective-permute-done.4.from_below.weights_below = f32[376,128]{1,0:T(8,128)S(1)} collective-permute-done((f32[376,128]{1,0:T(8,128)S(1)}, f32[376,128]{1,0:T(8,128)S(1)}, u32[]{:S(2)}, u32[]{:S(2)}) %collective-permute-start.4) | collective-permute-done | bytes 192544 | tf_op jit(solution)/shard_map/ppermute | solution.py:908
  31.6 1.6 %collective-permute-done.5.from_above.weights_above = f32[376,128]{1,0:T(8,128)S(1)} collective-permute-done((f32[376,128]{1,0:T(8,128)S(1)}, f32[376,128]{1,0:T(8,128)S(1)}, u32[]{:S(2)}, u32[]{:S(2)}) %collective-permute-start.5) | collective-permute-done | bytes 192544 | tf_op jit(solution)/shard_map/ppermute | solution.py:908
  33.2 2.2 %shard_map.116 = (f32[5,2,2,16,128]{4,3,2,1,0:T(8,128)S(1)}, f32[5,4,2,16,128]{4,3,2,1,0:T(8,128)S(1)}, f32[5,2,32,128]{3,2,1,0:T(8,128)S(1)}, f32[5,2,32,128]{3...) custom-call(f32[5,18,2,32,128]{4,3,2,1,0:T(8,128)S(1)} %get-tuple-element.38.s1.s1_in, ...), custom_call_target="tpu_custom_call" | custom-call | flops 2000000 | bytes 6000000 | tf_op jit(solution)/shard_map/pallas_call | solution.py:1031
  35.4 0.3 collective-permute-start.6
  35.7 4.8 %collective-permute-start.7 = (f32[344,128]{1,0:T(8,128)S(1)}, f32[344,128]{1,0:T(8,128)S(1)}, u32[]{:S(2)}, u32[]{:S(2)}) collective-permute-start(f32[344,128]{1,0:T(8,128)S(1)} %get-tuple-element.57.own_down), channel_id=1, source_target_pairs={{0,7},{1,0},{2,1},{3,2},{4,3},{5,4},{6,5},{7,6},{8,15},{9,8},{10,9... | collective-permute-start | bytes 528392 | tf_op jit(solution)/shard_map/ppermute | solution.py:908
  40.6 4.9 %shard_map.117 = (f32[5,16,16,256]{3,2,1,0:T(8,128)}, f32[5,18,2,32,128]{4,3,2,1,0:T(8,128)S(1)}, f32[16,16,256]{2,1,0:T(8,128)S(1)}) custom-call(f32[5,18,2,32,128]{4,3,2,1,0:T(8,128)S(1)} %get-tuple-element.38.s1.s1_in, f32[5,18,2,16,128]{4,3,2,1,0:T(8,128)S(1)} %get-tuple-element.41.s2_in, f32[5,18,2,16,128]{4,3,2,1,0:T(8,128)S(1)} %get-tuple-element.42.goal, ...), custom_call_target="tpu_custom_call" | custom-call | flops 6000000 | bytes 18000000 | tf_op jit(solution)/shard_map/pallas_call | solution.py:1063
  45.5 0.0 collective-permute-done.6.from_below
  45.5 1.9 %collective-permute-done.7.from_above = f32[344,128]{1,0:T(8,128)S(1)} collective-permute-done((f32[344,128]{1,0:T(8,128)S(1)}, f32[344,128]{1,0:T(8,128)S(1)}, u32[]{:S(2)}, u32[]{:S(2)}) %collective-permute-start.7) | collective-permute-done | bytes 176160 | tf_op jit(solution)/shard_map/ppermute | solution.py:908
  47.4 1.0 %shard_map.118 = (f32[5,18,2,32,128]{4,3,2,1,0:T(8,128)S(1)}, f32[5,2,32,128]{3,2,1,0:T(8,128)S(1)}, f32[16,128]{1,0:T(8,128)S(1)}, f32[16,128]{1,0:T(8,128)S(1)}, f32[16,128]{1,0:T(8,128)S(1)}) custom-call(f32[5,18,2,32,128]{4,3,2,1,0:T(8,128)S(1)} %get-tuple-element.53.adj1_in, f32[5,2,32,128]{3,2,1,0:T(8,128)S(1)} %get-tuple-element.54.strip_adj1_in, ...), custom_call_target="tpu_custom_call" | custom-call | flops 1000000 | bytes 3000000 | tf_op jit(solution)/shard_map/pallas_call | solution.py:1092
  48.4 2.0 %collective-permute-start.8 = (f32[16,128]{1,0:T(8,128)S(1)}, f32[16,128]{1,0:T(8,128)S(1)}, u32[]{:S(2)}, u32[]{:S(2)}) collective-permute-start(f32[16,128]{1,0:T(8,128)S(1)} %get-tuple-element.61), channel_id=1, source_target_pairs={{0,8},{8,16},{16,24},{24,32},{32,40},{40,48},{48,56},{56,64},{64,7... | collective-permute-start | bytes 24584 | tf_op jit(solution)/shard_map/ppermute | solution.py:921
  50.4 0.0 collective-permute-start.9
  50.4 4.4 %shard_map.119 = f32[5,16,16,256]{3,2,1,0:T(8,128)} custom-call(f32[5,18,2,32,128]{4,3,2,1,0:T(8,128)S(1)} %get-tuple-element.58.adj1, f32[5,2,32,128]{3,2,1,0:T(8,128)S(1)} %get-tuple-element.59.strip_adj1, f32[5,18,2,32,128]{4,3,2,1,0:T(8,128)S(1)} %get-tuple-element.33.field, f32[11,18,2,16,128]{4,3,2,1,0:T(8,128)S(1)} %get-tuple-element.34.coef, ...), custom_call_target="tpu_custom_call" | custom-call | flops 4000000 | bytes 12000000 | tf_op jit(solution)/shard_map/pallas_call | solution.py:1102
  54.8 0.0 collective-permute-done.8
  54.8 0.8 %collective-permute-done.9 = f32[16,128]{1,0:T(8,128)S(1)} collective-permute-done((f32[16,128]{1,0:T(8,128)S(1)}, f32[16,128]{1,0:T(8,128)S(1)}, u32[]{:S(2)}, u32[]{:S(2)}) %collective-permute-start.9) | collective-permute-done | bytes 8224 | tf_op jit(solution)/shard_map/ppermute | solution.py:921
  55.6 0.6 %add_bitcast_fusion = f32[128,1,16]{0,2,1:T(8,128)} fusion(f32[16,128]{1,0:T(8,128)S(1)} %collective-permute-done.9, f32[16,128]{1,0:T(8,128)S(1)} %get-tuple-element.60, f32[16,128]{1,0:T(8,128)S(1)} %collective-permute-done.8), kind=kLoop, calls=%fused_computation | loop fusion | flops 4096 | bytes 32768 | tf_op jit(solution)/shard_map/broadcast_in_dim | solution.py:1124
  (1 shorter events, 0.0 us)
Async XLA Ops:
  0.6 8.7 %copy-start.9 = (f32[128,1,16]{0,2,1:T(8,128)S(1)}, f32[128,1,16]{0,2,1:T(8,128)}, u32[]{:S(2)}) copy-start(f32[128,1,16]{0,2,1:T(8,128)} %param.14) | copy-start | bytes 24580
  0.6 12.2 %copy-start.1 = (f32[5,16,16,256]{3,2,1,0:T(8,128)S(1)}, f32[5,16,16,256]{3,2,1,0:T(8,128)}, u32[]{:S(2)}) copy-start(f32[5,16,16,256]{3,2,1,0:T(8,128)} %s0.3) | copy-start | bytes 3932164
  0.7 12.2 %copy-start.4 = (f32[16,16,256]{2,1,0:T(8,128)S(1)}, f32[16,16,256]{2,1,0:T(8,128)}, u32[]{:S(2)}) copy-start(f32[16,16,256]{2,1,0:T(8,128)} %param.12) | copy-start | bytes 786436
  0.7 17.6 %copy-start.6 = (s32[4096,1]{0,1:T(1,128)S(1)}, s32[4096,1]{0,1:T(1,128)}, u32[]{:S(2)}) copy-start(s32[4096,1]{0,1:T(1,128)} %param.15) | copy-start | bytes 49156
  0.7 17.6 %copy-start.7 = (s32[4096,1]{0,1:T(1,128)S(1)}, s32[4096,1]{0,1:T(1,128)}, u32[]{:S(2)}) copy-start(s32[4096,1]{0,1:T(1,128)} %param.16) | copy-start | bytes 49156
  0.7 17.6 %copy-start.8 = (s32[4096,1]{0,1:T(1,128)S(1)}, s32[4096,1]{0,1:T(1,128)}, u32[]{:S(2)}) copy-start(s32[4096,1]{0,1:T(1,128)} %param.17) | copy-start | bytes 49156
  5.3 12.9 %collective-permute-start.1 = (f32[24,16,128]{2,1,0:T(8,128)}, f32[24,16,128]{2,1,0:T(8,128)S(1)}, u32[]{:S(2)}, u32[]{:S(2)}) collective-permute-start(f32[24,16,128]{2,1,0:T(8,128)} %shard_map.112.own), channel_id=1, source_target_pairs={{0,1},{8,0},{16,8},{24,16},{32,24},{40,32},{48,40},{56,48},{64,56}... | collective-permute-start | bytes 589832 | tf_op jit(solution)/shard_map/ppermute | solution.py:921
  6.1 12.2 %collective-permute-start = (f32[24,16,128]{2,1,0:T(8,128)}, f32[24,16,128]{2,1,0:T(8,128)S(1)}, u32[]{:S(2)}, u32[]{:S(2)}) collective-permute-start(f32[24,16,128]{2,1,0:T(8,128)} %shard_map.112.own), channel_id=1, source_target_pairs={{0,8},{8,16},{16,24},{24,32},{32,40},{40,48},{48,56},{56,64},{64,7... | collective-permute-start | bytes 589832 | tf_op jit(solution)/shard_map/ppermute | solution.py:921
  9.3 9.0 %collective-permute-start.3 = (f32[16,128]{1,0:T(8,128)S(1)}, f32[16,128]{1,0:T(8,128)S(1)}, u32[]{:S(2)}, u32[]{:S(2)}) collective-permute-start(f32[16,128]{1,0:T(8,128)S(1)} %bitcast.20), channel_id=1, source_target_pairs={{0,1},{8,9},{16,0},{24,8},{32,16},{40,24},{48,32},{56,40},{64,48},... | collective-permute-start | bytes 24584 | tf_op jit(solution)/shard_map/ppermute | solution.py:921
  9.3 9.0 %collective-permute-start.2 = (f32[16,128]{1,0:T(8,128)S(1)}, f32[16,128]{1,0:T(8,128)S(1)}, u32[]{:S(2)}, u32[]{:S(2)}) collective-permute-start(f32[16,128]{1,0:T(8,128)S(1)} %bitcast.21), channel_id=1, source_target_pairs={{0,16},{8,24},{16,32},{24,40},{32,48},{40,56},{48,64},{56,72},{64,... | collective-permute-start | bytes 24584 | tf_op jit(solution)/shard_map/ppermute | solution.py:921
  12.9 1.7 %copy-start = (f32[9,16,16,256]{3,2,1,0:T(8,128)S(1)}, f32[9,16,16,256]{3,2,1,0:T(8,128)}, u32[]{:S(2)}) copy-start(f32[9,16,16,256]{3,2,1,0:T(8,128)} %grad.3) | copy-start | bytes 7077892
  14.5 1.1 %copy-start.3 = (f32[3,16,16,256]{3,2,1,0:T(8,128)S(1)}, f32[3,16,16,256]{3,2,1,0:T(8,128)}, u32[]{:S(2)}) copy-start(f32[3,16,16,256]{3,2,1,0:T(8,128)} %vel.3) | copy-start | bytes 2359300
  15.7 2.6 %copy-start.5 = (f32[24,16,128]{2,1,0:T(8,128)S(1)}, f32[24,16,128]{2,1,0:T(8,128)}, u32[]{:S(2)}) copy-start(f32[24,16,128]{2,1,0:T(8,128)} %shard_map.112.own) | copy-start | bytes 589828
  18.3 8.0 %copy-start.2 = (f32[5,16,16,256]{3,2,1,0:T(8,128)S(1)}, f32[5,16,16,256]{3,2,1,0:T(8,128)}, u32[]{:S(2)}) copy-start(f32[5,16,16,256]{3,2,1,0:T(8,128)} %tgt.3) | copy-start | bytes 3932164
  21.2 10.4 %collective-permute-start.4 = (f32[376,128]{1,0:T(8,128)S(1)}, f32[376,128]{1,0:T(8,128)S(1)}, u32[]{:S(2)}, u32[]{:S(2)}) collective-permute-start(f32[376,128]{1,0:T(8,128)S(1)} %get-tuple-element.47.own_up), channel_id=1, source_target_pairs={{0,1},{1,2},{2,3},{3,4},{4,5},{5,6},{6,7},{7,0},{8,9},{9,10},{10,1... | collective-permute-start | bytes 577544 | tf_op jit(solution)/shard_map/ppermute | solution.py:908
  21.4 11.8 %collective-permute-start.5 = (f32[376,128]{1,0:T(8,128)S(1)}, f32[376,128]{1,0:T(8,128)S(1)}, u32[]{:S(2)}, u32[]{:S(2)}) collective-permute-start(f32[376,128]{1,0:T(8,128)S(1)} %get-tuple-element.48.own_down), channel_id=1, source_target_pairs={{0,7},{1,0},{2,1},{3,2},{4,3},{5,4},{6,5},{7,6},{8,15},{9,8},{10,9... | collective-permute-start | bytes 577544 | tf_op jit(solution)/shard_map/ppermute | solution.py:908
  35.4 10.1 %collective-permute-start.6 = (f32[344,128]{1,0:T(8,128)S(1)}, f32[344,128]{1,0:T(8,128)S(1)}, u32[]{:S(2)}, u32[]{:S(2)}) collective-permute-start(f32[344,128]{1,0:T(8,128)S(1)} %get-tuple-element.56.own_up), channel_id=1, source_target_pairs={{0,1},{1,2},{2,3},{3,4},{4,5},{5,6},{6,7},{7,0},{8,9},{9,10},{10,1... | collective-permute-start | bytes 528392 | tf_op jit(solution)/shard_map/ppermute | solution.py:908
  35.7 11.6 %collective-permute-start.7 = (f32[344,128]{1,0:T(8,128)S(1)}, f32[344,128]{1,0:T(8,128)S(1)}, u32[]{:S(2)}, u32[]{:S(2)}) collective-permute-start(f32[344,128]{1,0:T(8,128)S(1)} %get-tuple-element.57.own_down), channel_id=1, source_target_pairs={{0,7},{1,0},{2,1},{3,2},{4,3},{5,4},{6,5},{7,6},{8,15},{9,8},{10,9... | collective-permute-start | bytes 528392 | tf_op jit(solution)/shard_map/ppermute | solution.py:908
  48.4 6.4 %collective-permute-start.8 = (f32[16,128]{1,0:T(8,128)S(1)}, f32[16,128]{1,0:T(8,128)S(1)}, u32[]{:S(2)}, u32[]{:S(2)}) collective-permute-start(f32[16,128]{1,0:T(8,128)S(1)} %get-tuple-element.61), channel_id=1, source_target_pairs={{0,8},{8,16},{16,24},{24,32},{32,40},{40,48},{48,56},{56,64},{64,7... | collective-permute-start | bytes 24584 | tf_op jit(solution)/shard_map/ppermute | solution.py:921
  50.4 5.2 %collective-permute-start.9 = (f32[16,128]{1,0:T(8,128)S(1)}, f32[16,128]{1,0:T(8,128)S(1)}, u32[]{:S(2)}, u32[]{:S(2)}) collective-permute-start(f32[16,128]{1,0:T(8,128)S(1)} %get-tuple-element.62), channel_id=1, source_target_pairs={{0,1},{8,0},{16,8},{24,16},{32,24},{40,32},{48,40},{56,48},{64,56}... | collective-permute-start | bytes 24584 | tf_op jit(solution)/shard_map/ppermute | solution.py:921

commit v2 on v1

--- a/solution.py
+++ b/solution.py
@@ -12,7 +12,8 @@
 LANES = 128
 F32 = jnp.float32
 HALO = 4
-S0, VEL, GRAD, ROT, TGT, NEEDLES, PLANES = 0, 5, 8, 17, 18, 23, 24
+S0, VEL, GRAD, ROT, TGT, NEEDLES = 0, 5, 8, 17, 18, 23
+PAIRS = 12
 PLACE = {(0, 0): 0, (1, 1): 1, (0, 1): 2, (1, 0): 3, (0, 2): 4, (2, 0): 5, (1, 2): 6, (2, 1): 7}
 SPREAD, UX, UZ, COEFS = 8, 9, 10, 11
 ROWS = 32
@@ -264,7 +265,24 @@
     )
 
 
-def pack_kernel(s0, vel, grad, rot, tgt, needle, out, stage, sems):
+def pack_kernel(
+    axis_cd,
+    s0,
+    vel,
+    grad,
+    rot,
+    tgt,
+    needle,
+    out,
+    first,
+    second,
+    field,
+    coef,
+    base,
+    uy,
+    stage,
+    sems,
+):
     layers = stage.shape[1]
     blocks = sems.shape[0]
     deep = layers // blocks
@@ -284,8 +302,29 @@
     for block in range(blocks):
         for copy in copies(block):
             copy.start()
-    out[NEEDLES] = needle[...]
     lane = lane_iota(out.shape[1:])
+    Field(field, None).clear()
+    clear_planes(coef, [UZ])
+
+    def load(z, carry):
+        zero = jnp.zeros((8, LANES), F32)
+        for tile in range(2):
+            for c in range(5):
+                field[c, z + 1, tile, OWN] = stage[c, z, :, span(tile)]
+            u = [DT * stage[VEL + d, z, :, span(tile)] for d in range(3)]
+            turn = DT * stage[ROT, z, :, span(tile)]
+            parts = gradient_parts(lambda i: stage[GRAD + i, z, :, span(tile)])
+            for key, value in parts.items():
+                coef[PLACE[key], z + 1, tile] = value
+            coef[SPREAD, z + 1, tile] = 2.0 * turn
+            coef[UX, z + 1, tile] = u[0]
+            coef[UZ, z + 1, tile] = u[2]
+            uy[z + 1, tile, 0:8] = zero
+            uy[z + 1, tile, 24:32] = zero
+            uy[z + 1, tile, OWN] = u[1]
+            base[z + 1, tile] = 6.0 * turn + (jnp.abs(u[0]) + jnp.abs(u[1]) + jnp.abs(u[2]))
+        return carry
+
 
     def step(block, carry):
         for copy in copies(block):
@@ -299,36 +338,26 @@
                 moved = pltpu.roll(both, (8 * z + HALO) % LANES, 1)
                 total = jnp.where(lane // 8 == z, moved, total)
             out[c] = total
+        lax.fori_loop(block * deep, (block + 1) * deep, load, 0)
         return carry
 
     lax.fori_loop(0, blocks, step, 0)
 
-
-def bulk_kernel(s0, vel, grad, rot, field, coef, base, uy, s1):
-    layers = s0.shape[1]
+    odd = lax.axis_index(axis_cd) % 2 == 1
+    outer = lane % 8 < HALO
+    first[PAIRS] = needle[...]
+    second[PAIRS] = needle[...]
+    for c in range(PAIRS):
+        here, other = out[c], out[min(c + PAIRS, NEEDLES - 1)]
+        to_right = jnp.where(outer, here, pltpu.roll(other, HALO, 1))
+        to_left = jnp.where(outer, pltpu.roll(other, LANES - HALO, 1), here)
+        first[c] = jnp.where(odd, to_left, to_right)
+        second[c] = jnp.where(odd, to_right, to_left)
+
+
+def bulk_kernel(field, coef, base, uy, s1):
+    layers = field.shape[1] - 2
     state = Field(field, None)
-    state.clear()
-    clear_planes(coef, [UZ])
-
-    def load(z, carry):
-        zero = jnp.zeros((8, LANES), F32)
-        for tile in range(2):
-            for c in range(5):
-                field[c, z + 1, tile, OWN] = s0[c, z, :, span(tile)]
-            u = [DT * vel[d, z, :, span(tile)] for d in range(3)]
-            turn = DT * rot[0, z, :, span(tile)]
-            for key, value in gradient_parts(lambda i: grad[i, z, :, span(tile)]).items():
-                coef[PLACE[key], z + 1, tile] = value
-            coef[SPREAD, z + 1, tile] = 2.0 * turn
-            coef[UX, z + 1, tile] = u[0]
-            coef[UZ, z + 1, tile] = u[2]
-            uy[z + 1, tile, 0:8] = zero
-            uy[z + 1, tile, 24:32] = zero
-            uy[z + 1, tile, OWN] = u[1]
-            base[z + 1, tile] = 6.0 * turn + (jnp.abs(u[0]) + jnp.abs(u[1]) + jnp.abs(u[2]))
-        return carry
-
-    lax.fori_loop(0, layers, load, 0)
 
     def advance(z, carry):
         for tile in range(2):
@@ -363,6 +392,7 @@
     axis_md,
     axis_cd,
     own,
+    needle,
     near_first,
     near_second,
     far_first,
@@ -404,6 +434,9 @@
     def from_right(c):
         return jnp.where(odd, near_first[c], near_second[c])
 
+    def half(take, c, turn):
+        return take(c) if c < PAIRS else pltpu.roll(take(c - PAIRS), turn, 1)
+
     near = lane_iota((1, LANES)) < LANES // 2
 
     def feet(ref):
@@ -414,7 +447,7 @@
     starts, ends, columns = feet(start), feet(end), feet(column)
     far = jnp.where((lane < LANES // 2) == odd, far_first[...], far_second[...])
     rates = jnp.concatenate(
-        [from_left(NEEDLES), own[NEEDLES], from_right(NEEDLES), far], axis=1
+        [from_left(PAIRS), needle[...], from_right(PAIRS), far], axis=1
     )
     needles = rates.shape[1]
     picked = jnp.where(row_iota((height, needles)) == columns, 1.0, 0.0)
@@ -443,8 +476,8 @@
 
         def raw(c):
             if side == 0:
-                return jnp.where(outer, jnp.where(has_left, from_left(c), 0.0), own[c])
-            return jnp.where(outer, own[c], jnp.where(has_right, from_right(c), 0.0))
+                return jnp.where(outer, jnp.where(has_left, half(from_left, c, LANES - HALO), 0.0), own[c])
+            return jnp.where(outer, own[c], jnp.where(has_right, half(from_right, c, HALO), 0.0))
 
         for c in range(5):
             strip_s0[c, side, OWN] = raw(S0 + c)
@@ -956,32 +989,40 @@
 
     hbm = pl.BlockSpec(memory_space=pltpu.HBM)
     blocks = 4
-    packed = pl.pallas_call(
-        pack_kernel,
+    packed, first, second, field, coef, base, uy = pl.pallas_call(
+        functools.partial(pack_kernel, "cd"),
         in_specs=[hbm] * 5 + [pl.BlockSpec(memory_space=pltpu.VMEM)],
-        out_shape=shape_of(PLANES, height, LANES),
+        out_shape=[
+            shape_of(NEEDLES, height, LANES),
+            shape_of(PAIRS + 1, height, LANES),
+            shape_of(PAIRS + 1, height, LANES),
+            shape_of(5, *padded),
+            shape_of(COEFS, *plain),
+            shape_of(*plain),
+            shape_of(*padded),
+        ],
         scratch_shapes=[
             scratch(NEEDLES, layers, height, length),
             pltpu.SemaphoreType.DMA((blocks, 5)),
         ],
-        compiler_params=params(62),
+        compiler_params=params(20),
         cost_estimate=cost(4),
-    )(orientation, velocity, velocity_grad, rotary, target, rates)
+    )(
+        *(
+            pltpu.with_memory_space_constraint(field, pltpu.HBM)
+            for field in (orientation, velocity, velocity_grad, rotary, target)
+        ),
+        rates,
+    )
     far = both_ways(rates, 2)
-    near = both_ways(packed, 1)
-
-    field, coef, base, uy, s1 = pl.pallas_call(
+    near = winding(first, 1, 0), winding(second, 1, 1)
+
+    s1 = pl.pallas_call(
         bulk_kernel,
-        out_shape=[
-            shape_of(5, *padded),
-            shape_of(COEFS, *plain),
-            shape_of(*plain),
-            shape_of(*padded),
-            shape_of(5, *padded),
-        ],
-        compiler_params=params(24),
-        cost_estimate=cost(3),
-    )(orientation, velocity, velocity_grad, rotary)
+        out_shape=shape_of(5, *padded),
+        compiler_params=params(16),
+        cost_estimate=cost(2),
+    )(field, coef, base, uy)
 
     s1, base, strip_s0, strip_coef, strip_base, strip_uy, strip_s1, strip_tgt, up, down = (
         pl.pallas_call(
@@ -1008,6 +1049,7 @@
         cost_estimate=cost(4),
         )(
             packed,
+            rates,
             *near,
             *far,
             *feet,

time: 56.3 us -> 54.8 us (0.973)
  local copies, waits for them, and re-layouts: 2.83 us -> 0.71 us
  Pallas kernels: 25.3 us -> 23.4 us
  waiting for transfers between devices: 6.88 us -> 8.25 us
  starting transfers between devices: 19.8 us -> 20.9 us
    unnamed x20 -> x12, local copies, waits for them, and re-layouts: 2.83 us -> 0.71 us
    pallas_call x2, Pallas kernels: 7.21 us -> 5.35 us  [the longest x1 3.46 us: local(): pl.pallas_call(functools.partial(pack_kernel, 'cd'), in_specs=[hbm] * 5 +...]
    ppermute x6, starting transfers between devices: 9.53 us -> 10.7 us  [winding(): return lax.ppermute(value, ('md', 'cd'), pairs)]
    ppermute x4, waiting for transfers between devices: 6.07 us -> 6.76 us  [ring(): lax.ppermute(value, axis, [(i, (i + steps) % count) for i in range(count)])]
    ppermute x6, waiting for transfers between devices: 0.81 us -> 1.49 us  [winding(): return lax.ppermute(value, ('md', 'cd'), pairs)]
  transfers between devices with their start and end apart: 10 -> 10, of which waited for: 4 -> 5; matrix products, arithmetic and copies ran while one was open for 0% -> 0% of each run, Pallas kernels for 26% -> 26%
where the time goes in v2:
time: 54.8 us; the launch traced here: 54.7 us
  Pallas kernels  23.4 us (43%)
  starting transfers between devices  20.9 us (38%)
  waiting for transfers between devices  8.25 us (15%)
  between operations  0.74 us (1%)
  local copies, waits for them, and re-layouts  0.71 us (1%)
  other arithmetic  0.6 us (1%)
    ppermute x6, starting transfers between devices, winding(): return lax.ppermute(value, ('md', 'cd'), pairs)  10.7 us
    ppermute x4, starting transfers between devices, ring(): lax.ppermute(value, axis, [(i, (i + steps) % count) for i in range(count)])  10.2 us
    ppermute x4, waiting for transfers between devices, ring(): lax.ppermute(value, axis, [(i, (i + steps) % count) for i in range(count)])  6.76 us
    pallas_call x1, Pallas kernels, local(): pl.pallas_call(second_kernel, out_shape=[shape_of(*orientation.shape), sh...  4.88 us
    pallas_call x1, Pallas kernels, local(): pl.pallas_call(functools.partial(fourth_kernel, 'cd'), out_shape=shape_of...  4.39 us
    pallas_call x1, Pallas kernels, local(): pl.pallas_call(functools.partial(pack_kernel, 'cd'), in_specs=[hbm] * 5 +...  3.46 us
    pallas_call x1, Pallas kernels, local(): pl.pallas_call(functools.partial(first_kernel, 'md', 'cd'), out_shape=[sh...  2.87 us
    pallas_call x1, Pallas kernels, local(): pl.pallas_call(advance_kernel, out_shape=[shape_of(5, *plain), shape_of(5...  2.8 us
  transfers between devices with their start and end apart: 10, of which 5 were waited for; matrix products, arithmetic and copies ran while one was open for 0% of the time, Pallas kernels for 26%

profile of v2, /device:TPU:105, one launch (start us, length us, event | category | flops | bytes accessed | tf_op | source)
XLA Modules:
  0.0 54.7 jit_solution(1726460807818958902)
XLA Ops:
  0.6 0.0 copy-start.4
  0.6 0.7 %copy-done.4 = f32[128,1,16]{0,2,1:T(8,128)S(1)} copy-done((f32[128,1,16]{0,2,1:T(8,128)S(1)}, f32[128,1,16]{0,2,1:T(8,128)}, u32[]{:S(2)}) %copy-start.4) | copy-done | bytes 8216
  1.3 3.5 %shard_map.112 = (f32[23,16,128]{2,1,0:T(8,128)S(1)}, f32[13,16,128]{2,1,0:T(8,128)S(1)}, f32[13,16,128]{2,1,0:T(8,128)S(1)}, f32[5,18,2,32,128]{4,3,2,1,0:T(8,1...) custom-call(f32[5,16,16,256]{3,2,1,0:T(8,128)} %s0.1, ...), custom_call_target="tpu_custom_call" | custom-call | flops 4000000 | bytes 12000000 | tf_op jit(solution)/shard_map/pallas_call | solution.py:992
  4.8 3.4 %collective-permute-start = (f32[13,16,128]{2,1,0:T(8,128)S(1)}, f32[13,16,128]{2,1,0:T(8,128)S(1)}, u32[]{:S(2)}, u32[]{:S(2)}) collective-permute-start(f32[13,16,128]{2,1,0:T(8,128)S(1)} %get-tuple-element.36), channel_id=1, source_target_pairs={{0,8},{8,16},{16,24},{24,32},{32,40},{40,48},{48,56},{56,64},{64,7... | collective-permute-start | bytes 319496 | tf_op jit(solution)/shard_map/ppermute | solution.py:954
  8.2 0.0 collective-permute-start.1
  8.2 0.0 collective-permute-start.3
  8.2 3.6 %collective-permute-start.2 = (f32[16,128]{1,0:T(8,128)S(1)}, f32[16,128]{1,0:T(8,128)S(1)}, u32[]{:S(2)}, u32[]{:S(2)}) collective-permute-start(f32[16,128]{1,0:T(8,128)S(1)} %bitcast.19), channel_id=1, source_target_pairs={{0,16},{8,24},{16,32},{24,40},{32,48},{40,56},{48,64},{56,72},{64,... | collective-permute-start | bytes 24584 | tf_op jit(solution)/shard_map/ppermute | solution.py:954
  11.8 0.0 copy-start.1
  11.8 0.0 copy-start.2
  11.8 0.0 copy-start.3
  11.8 0.0 copy-start.5
  11.8 1.9 %shard_map.113.s1_in = f32[5,18,2,32,128]{4,3,2,1,0:T(8,128)S(1)} custom-call(f32[5,18,2,32,128]{4,3,2,1,0:T(8,128)S(1)} %get-tuple-element.38.field, f32[11,18,2,16,128]{4,3,2,1,0:T(8,128)S(1)} %get-tuple-element.39.coef, f32[18,2,16,128]{3,2,1,0:T(8,128)S(1)} %get-tuple-element.41.base.base_in, f32[18,2,32,128]{3,2,1,0:T(8,128)S(1)} %get-tuple-element.40.uy), custom_call_target="tpu_custom_call" | custom-call | flops 2000000 | bytes 6000000 | tf_op jit(solution)/shard_map/pallas_call | solution.py:1020
  13.7 0.0 collective-permute-done.3.far_second
  13.7 0.0 collective-permute-done.2.far_first
  13.7 0.0 collective-permute-done.near_first
  13.7 0.7 %collective-permute-done.1.near_second = f32[13,16,128]{2,1,0:T(8,128)S(1)} collective-permute-done((f32[13,16,128]{2,1,0:T(8,128)S(1)}, f32[13,16,128]{2,1,0:T(8,128)S(1)}, u32[]{:S(2)}, u32[]{:S(2)}) %collective-permute-start.1) | collective-permute-done | bytes 106528 | tf_op jit(solution)/shard_map/ppermute | solution.py:954
  14.4 0.0 copy-done.1
  14.4 0.0 copy-done.2
  14.4 0.0 copy-done.3
  14.4 0.0 copy-done.5
  14.4 0.0 copy-start
  14.4 2.9 %shard_map.114 = (f32[5,18,2,32,128]{4,3,2,1,0:T(8,128)S(1)}, f32[18,2,16,128]{3,2,1,0:T(8,128)S(1)}, f32[5,2,32,128]{3,2,1,0:T(8,128)}, f32[11,2,16,128]{3,2,1,...) custom-call(f32[23,16,128]{2,1,0:T(8,128)S(1)} %get-tuple-element.35, ...), custom_call_target="tpu_custom_call" | custom-call | flops 4000000 | bytes 12000000 | tf_op jit(solution)/shard_map/pallas_call | solution.py:1028
  17.3 1.9 %collective-permute-start.4 = (f32[376,128]{1,0:T(8,128)S(1)}, f32[376,128]{1,0:T(8,128)S(1)}, u32[]{:S(2)}, u32[]{:S(2)}) collective-permute-start(f32[376,128]{1,0:T(8,128)S(1)} %get-tuple-element.51.own_up), channel_id=1, source_target_pairs={{0,1},{1,2},{2,3},{3,4},{4,5},{5,6},{6,7},{7,0},{8,9},{9,10},{10,1... | collective-permute-start | bytes 577544 | tf_op jit(solution)/shard_map/ppermute | solution.py:941
  19.2 3.2 %collective-permute-start.5 = (f32[376,128]{1,0:T(8,128)S(1)}, f32[376,128]{1,0:T(8,128)S(1)}, u32[]{:S(2)}, u32[]{:S(2)}) collective-permute-start(f32[376,128]{1,0:T(8,128)S(1)} %get-tuple-element.52.own_down), channel_id=1, source_target_pairs={{0,7},{1,0},{2,1},{3,2},{4,3},{5,4},{6,5},{7,6},{8,15},{9,8},{10,9... | collective-permute-start | bytes 577544 | tf_op jit(solution)/shard_map/ppermute | solution.py:941
  22.4 0.0 copy-done
  22.4 2.8 %shard_map.115 = (f32[5,18,2,16,128]{4,3,2,1,0:T(8,128)S(1)}, f32[5,18,2,16,128]{4,3,2,1,0:T(8,128)S(1)}) custom-call(f32[5,18,2,32,128]{4,3,2,1,0:T(8,128)S(1)} %get-tuple-element.42.s1.s1_in, f32[5,2,32,128]{3,2,1,0:T(8,128)S(1)} %get-tuple-element.43.strip_s1.strip_s1_in, f32[11,18,2,16,128]{4,3,2,1,0:T(8,128)S(1)} %get-tuple-element.39.coef, ...), custom_call_target="tpu_custom_call" | custom-call | flops 4000000 | bytes 12000000 | tf_op jit(solution)/shard_map/pallas_call | solution.py:1066
  25.2 1.3 %collective-permute-done.4.from_below.weights_below = f32[376,128]{1,0:T(8,128)S(1)} collective-permute-done((f32[376,128]{1,0:T(8,128)S(1)}, f32[376,128]{1,0:T(8,128)S(1)}, u32[]{:S(2)}, u32[]{:S(2)}) %collective-permute-start.4) | collective-permute-done | bytes 192544 | tf_op jit(solution)/shard_map/ppermute | solution.py:941
  26.5 4.8 %collective-permute-done.5.from_above.weights_above = f32[376,128]{1,0:T(8,128)S(1)} collective-permute-done((f32[376,128]{1,0:T(8,128)S(1)}, f32[376,128]{1,0:T(8,128)S(1)}, u32[]{:S(2)}, u32[]{:S(2)}) %collective-permute-start.5) | collective-permute-done | bytes 192544 | tf_op jit(solution)/shard_map/ppermute | solution.py:941
  31.3 2.2 %shard_map.116 = (f32[5,2,2,16,128]{4,3,2,1,0:T(8,128)S(1)}, f32[5,4,2,16,128]{4,3,2,1,0:T(8,128)S(1)}, f32[5,2,32,128]{3,2,1,0:T(8,128)S(1)}, f32[5,2,32,128]{3...) custom-call(f32[5,18,2,32,128]{4,3,2,1,0:T(8,128)S(1)} %get-tuple-element.42.s1.s1_in, ...), custom_call_target="tpu_custom_call" | custom-call | flops 2000000 | bytes 6000000 | tf_op jit(solution)/shard_map/pallas_call | solution.py:1073
  33.5 0.1 collective-permute-start.6
  33.6 5.1 %collective-permute-start.7 = (f32[344,128]{1,0:T(8,128)S(1)}, f32[344,128]{1,0:T(8,128)S(1)}, u32[]{:S(2)}, u32[]{:S(2)}) collective-permute-start(f32[344,128]{1,0:T(8,128)S(1)} %get-tuple-element.61.own_down), channel_id=1, source_target_pairs={{0,7},{1,0},{2,1},{3,2},{4,3},{5,4},{6,5},{7,6},{8,15},{9,8},{10,9... | collective-permute-start | bytes 528392 | tf_op jit(solution)/shard_map/ppermute | solution.py:941
  38.7 4.9 %shard_map.117 = (f32[5,16,16,256]{3,2,1,0:T(8,128)}, f32[5,18,2,32,128]{4,3,2,1,0:T(8,128)S(1)}, f32[16,16,256]{2,1,0:T(8,128)S(1)}) custom-call(f32[5,18,2,32,128]{4,3,2,1,0:T(8,128)S(1)} %get-tuple-element.42.s1.s1_in, f32[5,18,2,16,128]{4,3,2,1,0:T(8,128)S(1)} %get-tuple-element.45.s2_in, f32[5,18,2,16,128]{4,3,2,1,0:T(8,128)S(1)} %get-tuple-element.46.goal, ...), custom_call_target="tpu_custom_call" | custom-call | flops 6000000 | bytes 18000000 | tf_op jit(solution)/shard_map/pallas_call | solution.py:1105
  43.6 0.0 collective-permute-done.6.from_below
  43.6 0.6 %collective-permute-done.7.from_above = f32[344,128]{1,0:T(8,128)S(1)} collective-permute-done((f32[344,128]{1,0:T(8,128)S(1)}, f32[344,128]{1,0:T(8,128)S(1)}, u32[]{:S(2)}, u32[]{:S(2)}) %collective-permute-start.7) | collective-permute-done | bytes 176160 | tf_op jit(solution)/shard_map/ppermute | solution.py:941
  44.2 1.0 %shard_map.118 = (f32[5,18,2,32,128]{4,3,2,1,0:T(8,128)S(1)}, f32[5,2,32,128]{3,2,1,0:T(8,128)S(1)}, f32[16,128]{1,0:T(8,128)S(1)}, f32[16,128]{1,0:T(8,128)S(1)}, f32[16,128]{1,0:T(8,128)S(1)}) custom-call(f32[5,18,2,32,128]{4,3,2,1,0:T(8,128)S(1)} %get-tuple-element.57.adj1_in, f32[5,2,32,128]{3,2,1,0:T(8,128)S(1)} %get-tuple-element.58.strip_adj1_in, ...), custom_call_target="tpu_custom_call" | custom-call | flops 1000000 | bytes 3000000 | tf_op jit(solution)/shard_map/pallas_call | solution.py:1134
  45.2 3.7 %collective-permute-start.8 = (f32[16,128]{1,0:T(8,128)S(1)}, f32[16,128]{1,0:T(8,128)S(1)}, u32[]{:S(2)}, u32[]{:S(2)}) collective-permute-start(f32[16,128]{1,0:T(8,128)S(1)} %get-tuple-element.65), channel_id=1, source_target_pairs={{0,8},{8,16},{16,24},{24,32},{32,40},{40,48},{48,56},{56,64},{64,7... | collective-permute-start | bytes 24584 | tf_op jit(solution)/shard_map/ppermute | solution.py:954
  48.9 0.0 collective-permute-start.9
  48.9 4.4 %shard_map.119 = f32[5,16,16,256]{3,2,1,0:T(8,128)} custom-call(f32[5,18,2,32,128]{4,3,2,1,0:T(8,128)S(1)} %get-tuple-element.62.adj1, f32[5,2,32,128]{3,2,1,0:T(8,128)S(1)} %get-tuple-element.63.strip_adj1, f32[5,18,2,32,128]{4,3,2,1,0:T(8,128)S(1)} %get-tuple-element.38.field, f32[11,18,2,16,128]{4,3,2,1,0:T(8,128)S(1)} %get-tuple-element.39.coef, ...), custom_call_target="tpu_custom_call" | custom-call | flops 4000000 | bytes 12000000 | tf_op jit(solution)/shard_map/pallas_call | solution.py:1144
  53.3 0.0 collective-permute-done.8
  53.3 0.8 %collective-permute-done.9 = f32[16,128]{1,0:T(8,128)S(1)} collective-permute-done((f32[16,128]{1,0:T(8,128)S(1)}, f32[16,128]{1,0:T(8,128)S(1)}, u32[]{:S(2)}, u32[]{:S(2)}) %collective-permute-start.9) | collective-permute-done | bytes 8224 | tf_op jit(solution)/shard_map/ppermute | solution.py:954
  54.1 0.6 %add_bitcast_fusion = f32[128,1,16]{0,2,1:T(8,128)} fusion(f32[16,128]{1,0:T(8,128)S(1)} %collective-permute-done.9, f32[16,128]{1,0:T(8,128)S(1)} %get-tuple-element.64, f32[16,128]{1,0:T(8,128)S(1)} %collective-permute-done.8), kind=kLoop, calls=%fused_computation | loop fusion | flops 4096 | bytes 32768 | tf_op jit(solution)/shard_map/broadcast_in_dim | solution.py:1166
Async XLA Ops:
  0.6 0.7 %copy-start.4 = (f32[128,1,16]{0,2,1:T(8,128)S(1)}, f32[128,1,16]{0,2,1:T(8,128)}, u32[]{:S(2)}) copy-start(f32[128,1,16]{0,2,1:T(8,128)} %param.14) | copy-start | bytes 24580
  4.8 8.9 %collective-permute-start = (f32[13,16,128]{2,1,0:T(8,128)S(1)}, f32[13,16,128]{2,1,0:T(8,128)S(1)}, u32[]{:S(2)}, u32[]{:S(2)}) collective-permute-start(f32[13,16,128]{2,1,0:T(8,128)S(1)} %get-tuple-element.36), channel_id=1, source_target_pairs={{0,8},{8,16},{16,24},{24,32},{32,40},{40,48},{48,56},{56,64},{64,7... | collective-permute-start | bytes 319496 | tf_op jit(solution)/shard_map/ppermute | solution.py:954
  8.2 6.2 %collective-permute-start.1 = (f32[13,16,128]{2,1,0:T(8,128)S(1)}, f32[13,16,128]{2,1,0:T(8,128)S(1)}, u32[]{:S(2)}, u32[]{:S(2)}) collective-permute-start(f32[13,16,128]{2,1,0:T(8,128)S(1)} %get-tuple-element.37), channel_id=1, source_target_pairs={{0,1},{8,0},{16,8},{24,16},{32,24},{40,32},{48,40},{56,48},{64,56}... | collective-permute-start | bytes 319496 | tf_op jit(solution)/shard_map/ppermute | solution.py:954
  8.2 5.5 %collective-permute-start.3 = (f32[16,128]{1,0:T(8,128)S(1)}, f32[16,128]{1,0:T(8,128)S(1)}, u32[]{:S(2)}, u32[]{:S(2)}) collective-permute-start(f32[16,128]{1,0:T(8,128)S(1)} %bitcast.18), channel_id=1, source_target_pairs={{0,1},{8,9},{16,0},{24,8},{32,16},{40,24},{48,32},{56,40},{64,48},... | collective-permute-start | bytes 24584 | tf_op jit(solution)/shard_map/ppermute | solution.py:954
  8.2 5.5 %collective-permute-start.2 = (f32[16,128]{1,0:T(8,128)S(1)}, f32[16,128]{1,0:T(8,128)S(1)}, u32[]{:S(2)}, u32[]{:S(2)}) collective-permute-start(f32[16,128]{1,0:T(8,128)S(1)} %bitcast.19), channel_id=1, source_target_pairs={{0,16},{8,24},{16,32},{24,40},{32,48},{40,56},{48,64},{56,72},{64,... | collective-permute-start | bytes 24584 | tf_op jit(solution)/shard_map/ppermute | solution.py:954
  11.8 2.6 %copy-start.1 = (s32[4096,1]{0,1:T(1,128)S(1)}, s32[4096,1]{0,1:T(1,128)}, u32[]{:S(2)}) copy-start(s32[4096,1]{0,1:T(1,128)} %param.15) | copy-start | bytes 49156
  11.8 2.6 %copy-start.2 = (s32[4096,1]{0,1:T(1,128)S(1)}, s32[4096,1]{0,1:T(1,128)}, u32[]{:S(2)}) copy-start(s32[4096,1]{0,1:T(1,128)} %param.16) | copy-start | bytes 49156
  11.8 2.6 %copy-start.3 = (s32[4096,1]{0,1:T(1,128)S(1)}, s32[4096,1]{0,1:T(1,128)}, u32[]{:S(2)}) copy-start(s32[4096,1]{0,1:T(1,128)} %param.17) | copy-start | bytes 49156
  11.8 2.6 %copy-start.5 = (f32[128,1,16]{0,2,1:T(8,128)S(1)}, f32[128,1,16]{0,2,1:T(8,128)}, u32[]{:S(2)}) copy-start(f32[128,1,16]{0,2,1:T(8,128)} %param.14) | copy-start | bytes 24580
  14.4 8.0 %copy-start = (f32[5,16,16,256]{3,2,1,0:T(8,128)S(1)}, f32[5,16,16,256]{3,2,1,0:T(8,128)}, u32[]{:S(2)}) copy-start(f32[5,16,16,256]{3,2,1,0:T(8,128)} %tgt.3) | copy-start | bytes 3932164
  17.3 9.2 %collective-permute-start.4 = (f32[376,128]{1,0:T(8,128)S(1)}, f32[376,128]{1,0:T(8,128)S(1)}, u32[]{:S(2)}, u32[]{:S(2)}) collective-permute-start(f32[376,128]{1,0:T(8,128)S(1)} %get-tuple-element.51.own_up), channel_id=1, source_target_pairs={{0,1},{1,2},{2,3},{3,4},{4,5},{5,6},{6,7},{7,0},{8,9},{9,10},{10,1... | collective-permute-start | bytes 577544 | tf_op jit(solution)/shard_map/ppermute | solution.py:941
  19.2 12.1 %collective-permute-start.5 = (f32[376,128]{1,0:T(8,128)S(1)}, f32[376,128]{1,0:T(8,128)S(1)}, u32[]{:S(2)}, u32[]{:S(2)}) collective-permute-start(f32[376,128]{1,0:T(8,128)S(1)} %get-tuple-element.52.own_down), channel_id=1, source_target_pairs={{0,7},{1,0},{2,1},{3,2},{4,3},{5,4},{6,5},{7,6},{8,15},{9,8},{10,9... | collective-permute-start | bytes 577544 | tf_op jit(solution)/shard_map/ppermute | solution.py:941
  33.5 10.0 %collective-permute-start.6 = (f32[344,128]{1,0:T(8,128)S(1)}, f32[344,128]{1,0:T(8,128)S(1)}, u32[]{:S(2)}, u32[]{:S(2)}) collective-permute-start(f32[344,128]{1,0:T(8,128)S(1)} %get-tuple-element.60.own_up), channel_id=1, source_target_pairs={{0,1},{1,2},{2,3},{3,4},{4,5},{5,6},{6,7},{7,0},{8,9},{9,10},{10,1... | collective-permute-start | bytes 528392 | tf_op jit(solution)/shard_map/ppermute | solution.py:941
  33.6 10.6 %collective-permute-start.7 = (f32[344,128]{1,0:T(8,128)S(1)}, f32[344,128]{1,0:T(8,128)S(1)}, u32[]{:S(2)}, u32[]{:S(2)}) collective-permute-start(f32[344,128]{1,0:T(8,128)S(1)} %get-tuple-element.61.own_down), channel_id=1, source_target_pairs={{0,7},{1,0},{2,1},{3,2},{4,3},{5,4},{6,5},{7,6},{8,15},{9,8},{10,9... | collective-permute-start | bytes 528392 | tf_op jit(solution)/shard_map/ppermute | solution.py:941
  45.2 8.1 %collective-permute-start.8 = (f32[16,128]{1,0:T(8,128)S(1)}, f32[16,128]{1,0:T(8,128)S(1)}, u32[]{:S(2)}, u32[]{:S(2)}) collective-permute-start(f32[16,128]{1,0:T(8,128)S(1)} %get-tuple-element.65), channel_id=1, source_target_pairs={{0,8},{8,16},{16,24},{24,32},{32,40},{40,48},{48,56},{56,64},{64,7... | collective-permute-start | bytes 24584 | tf_op jit(solution)/shard_map/ppermute | solution.py:954
  48.9 5.2 %collective-permute-start.9 = (f32[16,128]{1,0:T(8,128)S(1)}, f32[16,128]{1,0:T(8,128)S(1)}, u32[]{:S(2)}, u32[]{:S(2)}) collective-permute-start(f32[16,128]{1,0:T(8,128)S(1)} %get-tuple-element.66), channel_id=1, source_target_pairs={{0,1},{8,0},{16,8},{24,16},{32,24},{40,32},{48,40},{56,48},{64,56}... | collective-permute-start | bytes 24584 | tf_op jit(solution)/shard_map/ppermute | solution.py:954

commit v3 on v2

--- a/solution.py
+++ b/solution.py
@@ -743,26 +743,56 @@
                 outgoing[planes(tile * 10 + 5 + c, layers)] = weight * out[c]
 
 
+def needle_feet(ref, md, count):
+    return jnp.concatenate([feet_block(ref, md + d, count) for d in (-1, 0, 1)], axis=1)
+
+
+def own_cover(md, length, starts, ends):
+    cells = row_iota((length, starts.shape[1])) + md * length
+    return jnp.where((cells >= starts) & (cells < ends), 1.0, 0.0).astype(jnp.bfloat16)
+
+
+def covered_sum(values, cover):
+    product = jnp.zeros((values.shape[0], cover.shape[1]), F32)
+    for part in split_three(values):
+        product = product + jnp.dot(
+            part.astype(jnp.bfloat16), cover, preferred_element_type=F32
+        )
+    return product
+
+
 def second_kernel(
+    axis_md,
     s1_in,
     s2_in,
     goal,
     s1_edge,
     s2_edge,
+    field,
     coef,
     base,
     uy,
     strip_coef,
     strip_adj2,
+    strip_adj1,
+    start,
+    end,
+    column,
     s2_out,
+    adj0,
+    gained,
     adj1,
     dots,
     s1,
     s2,
     adj2,
     joint,
+    joint1,
 ):
-    layers = goal.shape[1] - 2
+    layers, height = goal.shape[1] - 2, goal.shape[3]
+    length = 2 * LANES
+    md = lax.axis_index(axis_md)
+    count = lax.axis_size(axis_md)
 
     def gather(z, carry):
         for tile in range(2):
@@ -809,87 +839,80 @@
                 adj1[c, z + 1, tile, OWN] = out[c]
         return carry
 
+    last_delta = Field(adj1, strip_adj1, joint1)
+    last_delta.clear()
+    last_delta.join()
     lax.fori_loop(0, layers, retreat, 0)
+
+    def finish(z, carry):
+        for tile in range(2):
+            m, damp = coefficients(coef, base, z + 1, tile)
+            a = [field[c, z + 1, tile, OWN] for c in range(5)]
+            b = [last_delta.own(c, z, tile) for c in range(5)]
+            wind = back_wind(coef, uy, edge_x, z, tile)
+            out = backward(b, a, m, damp, wind, last_delta.around(z, tile))
+            total = dots[z, :, span(tile)]
+            for c in range(5):
+                adj0[c, z + 1, tile] = out[c]
+                total = total + a[c] * b[c]
+            dots[z, :, span(tile)] = -DT * total
+        return carry
+
+    lax.fori_loop(0, layers, finish, 0)
+    starts, ends, columns = (needle_feet(ref, md, count) for ref in (start, end, column))
+    cover = own_cover(md, length, starts, ends)
+    product = covered_sum(dots[...].reshape(layers * height, length), cover)
+    picked = jnp.where(row_iota((height, starts.shape[1])) == columns, 1.0, 0.0)
+    for z in range(layers):
+        gained[z : z + 1] = jnp.sum(
+            product[z * height : (z + 1) * height] * picked, axis=0, keepdims=True
+        )
 
 
 def third_kernel(
     axis_md,
     axis_cd,
-    adj1_in,
-    strip_adj1_in,
-    dots,
+    gained,
     field,
     from_below,
     from_above,
     start,
     end,
     column,
-    adj1,
-    strip_adj1,
     first,
     kept,
     second,
-    sens,
 ):
-    layers, height, length = dots.shape
+    layers = field.shape[1] - 2
+    length = 2 * LANES
     md = lax.axis_index(axis_md)
     count = lax.axis_size(axis_md)
-    has_below, has_above = cd_flags(axis_cd)
     odd = lax.axis_index(axis_cd) % 2 == 1
-
-    row = row_iota((height, LANES))
-    top = height - 1
-
-    def mended(value, z, place):
-        at = line(z, place, 20, layers)
-        low = jnp.where(has_below, from_below[at], 0.0)
-        high = jnp.where(has_above, from_above[at], 0.0)
-        return value + jnp.where(row == 0, low, jnp.where(row == top, high, 0.0))
-
-    for side in range(2):
-        for c in range(5):
-            value = strip_adj1_in[c, side, OWN]
-            strip_adj1[c, side, OWN] = mended(value, None, side * 10 + c)
-    Field(adj1, strip_adj1).clear()
-
-    def weigh(z, carry):
-        for tile in range(2):
-            total = dots[z, :, span(tile)]
-            for c in range(5):
-                value = mended(adj1_in[c, z + 1, tile, OWN], z, tile * 10 + c)
-                adj1[c, z + 1, tile, OWN] = value
-                total = total + value * field[c, z + 1, tile, OWN]
-            sens[z, :, span(tile)] = -DT * total
-        return carry
-
-    lax.fori_loop(0, layers, weigh, 0)
-
-    def feet(ref):
-        return jnp.concatenate([feet_block(ref, md + d, count) for d in (-1, 0, 1)], axis=1)
-
-    starts, ends, columns = feet(start), feet(end), feet(column)
-    needles = starts.shape[1]
-    cells = row_iota((length, needles)) + md * length
-    cover = jnp.where((cells >= starts) & (cells < ends), 1.0, 0.0).astype(jnp.bfloat16)
-    product = jnp.zeros((layers * height, needles), F32)
-    for part in split_three(sens[...].reshape(layers * height, length)):
-        product = product + jnp.dot(
-            part.astype(jnp.bfloat16), cover, preferred_element_type=F32
-        )
-    picked = jnp.where(row_iota((height, needles)) == columns, 1.0, 0.0)
-    for z in range(layers):
-        total = jnp.sum(
-            product[z * height : (z + 1) * height] * picked, axis=0, keepdims=True
-        )
-        first[z : z + 1] = jnp.where(odd, total[:, span(0)], total[:, span(2)])
-        kept[z : z + 1] = total[:, span(1)]
-        second[z : z + 1] = jnp.where(odd, total[:, span(2)], total[:, span(0)])
+    lines = []
+    for message, valid, row in zip((from_below, from_above), cd_flags(axis_cd), (8, 23)):
+        parts = []
+        for tile in range(2):
+            total = 0.0
+            for c in range(5):
+                brought = message[planes(tile * 10 + c, layers)]
+                total = total + brought * row_of(field, c, tile, row)
+            parts.append(jnp.where(valid, -DT * total, 0.0))
+        lines.append(jnp.concatenate(parts, axis=1))
+    starts, ends, columns = (needle_feet(ref, md, count) for ref in (start, end, column))
+    cover = own_cover(md, length, starts, ends)
+    product = covered_sum(jnp.concatenate(lines, axis=0), cover)
+    total = gained[...]
+    for number, row in enumerate((0, 15)):
+        here = product[number * layers : (number + 1) * layers]
+        total = total + jnp.where(columns == row, here, 0.0)
+    first[...] = jnp.where(odd, total[:, span(0)], total[:, span(2)])
+    kept[...] = total[:, span(1)]
+    second[...] = jnp.where(odd, total[:, span(2)], total[:, span(0)])
 
 
 def fourth_kernel(
     axis_cd,
-    adj1,
-    strip_adj1,
+    adj0_in,
     field,
     coef,
     base,
@@ -901,39 +924,71 @@
     own_down,
     from_below,
     from_above,
+    out_field,
     adj0,
-    joint,
 ):
-    layers, height = adj0.shape[1], adj0.shape[2]
-    top = height - 1
+    layers = field.shape[1] - 2
     has_below, has_above = cd_flags(axis_cd)
-    delta = Field(adj1, strip_adj1, joint)
-    delta.join()
-    edge_x = merged(strip_coef, UX, slice(None))
-
-    def retreat(z, carry):
-        for tile in range(2):
-            at = (z + 1, tile)
-            m, damp = coefficients(coef, base, *at)
-            a = [field[c, z + 1, tile, OWN] for c in range(5)]
-            b = [delta.own(c, z, tile) for c in range(5)]
-            wind = back_wind(coef, uy, edge_x, z, tile)
-            out = backward(b, a, m, damp, wind, delta.around(z, tile))
-            weight = line(z, tile * 11 + 10, 22, layers)
-            low_n, high_n = weights_below[weight], weights_above[weight]
-            lanes = span(tile)
-            for c in range(5):
-                old = line(z, tile * 10 + c, 20, layers)
-                new = line(z, tile * 10 + 5 + c, 20, layers)
-                low = from_below[new] + low_n * own_down[old]
-                high = from_above[new] + high_n * own_up[old]
-                low, high = jnp.where(has_below, low, 0.0), jnp.where(has_above, high, 0.0)
-                adj0[c, z, :, lanes] = out[c]
-                adj0[c, z, 0:1, lanes] = out[c][:1] + low
-                adj0[c, z, top:, lanes] = out[c][top:] + high
+
+    def gather(z, carry):
+        for tile in range(2):
+            for c in range(5):
+                adj0[c, z + 1, tile] = adj0_in[c, z + 1, tile]
         return carry
 
-    lax.fori_loop(0, layers, retreat, 0)
+    lax.fori_loop(0, layers, gather, 0)
+
+    for number, (weights, message, mine, valid) in enumerate(
+        (
+            (weights_below, from_below, own_down, has_below),
+            (weights_above, from_above, own_up, has_above),
+        )
+    ):
+        row, inner = ((0, 1), (15, 14))[number]
+        brought = {}
+        for c in range(5):
+            for tile in range(2):
+                value = message[planes(tile * 10 + c, layers)]
+                brought[c, tile] = jnp.where(valid, value, 0.0)
+        edges = []
+        for c in range(5):
+            left, right = (message[line(None, side * 10 + c, 20, layers)] for side in (0, 1))
+            edges.append(jnp.where(valid, edge_column(left, right, layers), 0.0))
+        left, right = (strip_coef[UX, side, row : row + 1] for side in (0, 1))
+        edge_x = edge_column(left, right, layers)
+        for tile in range(2):
+            m = {key: row_of(coef, place, tile, row) for key, place in PLACE.items()}
+            damp = row_of(base, 0, tile, row)
+            a = [row_of(field, c, tile, 8 + row) for c in range(5)]
+            b = [brought[c, tile] for c in range(5)]
+            wind = (
+                x_pair([row_of(coef, UX, t, row) for t in range(2)], tile, edge_x),
+                layer_pair(row_of(coef, UZ, tile, row)),
+            )
+
+            def around(c):
+                tiles = [brought[c, t] for t in range(2)]
+                return x_pair(tiles, tile, edges[c]), layer_pair(b[c])
+
+            out = backward(b, a, m, damp, wind, around)
+            speed = row_of(uy, 0, tile, 8 + row)
+            inward = -jnp.minimum(speed, 0.0) if number == 0 else jnp.maximum(speed, 0.0)
+            weight = weights[planes(tile * 11 + 10, layers)]
+            for c in range(5):
+                own = mine[planes(tile * 10 + c, layers)]
+                far = message[planes(tile * 10 + 5 + c, layers)] + weight * own
+                total = out[c] + jnp.where(valid, far, 0.0)
+                set_row(adj0, c, tile, row, row_of(adj0, c, tile, row) + total)
+                more = inward * b[c]
+                set_row(adj0, c, tile, inner, row_of(adj0, c, tile, inner) + more)
+
+    def scatter(z, carry):
+        for tile in range(2):
+            for c in range(5):
+                out_field[c, z, :, span(tile)] = adj0[c, z + 1, tile]
+        return carry
+
+    lax.fori_loop(0, layers, scatter, 0)
 
 
 def ring(value, axis, steps):
@@ -1102,54 +1157,58 @@
     back_below = ring(back_up, "cd", 1)
     back_above = ring(back_down, "cd", -1)
 
-    s2, adj1, dots = pl.pallas_call(
-        second_kernel,
+    part = shape_of(*rates.shape)
+    s2, adj0_part, gained = pl.pallas_call(
+        functools.partial(second_kernel, "md"),
         out_shape=[
             shape_of(*orientation.shape),
-            shape_of(5, *padded),
-            shape_of(layers, height, length),
+            shape_of(5, *plain),
+            shape_of(layers, 3 * LANES),
         ],
         scratch_shapes=[
+            scratch(5, *padded),
+            scratch(layers, height, length),
             scratch(5, *plain),
             scratch(5, *plain),
             scratch(5, *padded),
             joint,
+            joint,
         ],
         compiler_params=params(24),
-        cost_estimate=cost(6),
+        cost_estimate=cost(9),
     )(
         s1,
         s2_part,
         goal,
         s1_edge,
         s2_edge,
+        field,
         coef,
         base,
         uy,
         strip_coef,
         strip_adj2,
+        strip_adj1,
+        *feet,
     )
 
-    part = shape_of(*rates.shape)
-    adj1, strip_adj1, part_first, part_own, part_second = pl.pallas_call(
+    part_first, part_own, part_second = pl.pallas_call(
         functools.partial(third_kernel, "md", "cd"),
-        out_shape=[shape_of(5, *padded), shape_of(5, *strip_padded), part, part, part],
-        scratch_shapes=[scratch(layers, height, length)],
-        compiler_params=params(24),
+        out_shape=[part, part, part],
+        compiler_params=params(16),
         cost_estimate=cost(1),
-    )(adj1, strip_adj1, dots, field, back_below, back_above, *feet)
+    )(gained, field, back_below, back_above, *feet)
     part_first = winding(part_first, 1, 0)
     part_second = winding(part_second, 1, 1)
 
     adj0 = pl.pallas_call(
         functools.partial(fourth_kernel, "cd"),
         out_shape=shape_of(*orientation.shape),
-        scratch_shapes=[joint],
-        compiler_params=params(24),
-        cost_estimate=cost(4),
+        scratch_shapes=[scratch(5, *plain)],
+        compiler_params=params(16),
+        cost_estimate=cost(2),
     )(
-        adj1,
-        strip_adj1,
+        adj0_part,
         field,
         coef,
         base,

time: 54.8 us -> 55.8 us (1.018)
  waiting for transfers between devices: 8.25 us -> 9.87 us
  starting transfers between devices: 20.9 us -> 20 us
    pallas_call x2, Pallas kernels: 5.87 us -> 8.46 us  [the longest x1 8.05 us: local(): pl.pallas_call(functools.partial(second_kernel, 'md'), out_shape=[shape_o...]
    pallas_call x1, Pallas kernels: 4.39 us -> 2.24 us  [local(): pl.pallas_call(functools.partial(fourth_kernel, 'cd'), out_shape=shape_of...]
    ppermute x6, waiting for transfers between devices: 1.49 us -> 3.63 us  [winding(): return lax.ppermute(value, ('md', 'cd'), pairs)]
    ppermute x6, starting transfers between devices: 10.7 us -> 9.75 us  [winding(): return lax.ppermute(value, ('md', 'cd'), pairs)]
  transfers between devices with their start and end apart: 10 -> 10, of which waited for: 5 -> 4; matrix products, arithmetic and copies ran while one was open for 0% -> 0% of each run, Pallas kernels for 26% -> 27%
where the time goes in v3:
time: 55.8 us; the launch traced here: 55.7 us
  Pallas kernels  23.8 us (43%)
  starting transfers between devices  20 us (36%)
  waiting for transfers between devices  9.87 us (18%)
  between operations  0.74 us (1%)
  local copies, waits for them, and re-layouts  0.71 us (1%)
  other arithmetic  0.6 us (1%)
    ppermute x4, starting transfers between devices, ring(): lax.ppermute(value, axis, [(i, (i + steps) % count) for i in range(count)])  10.2 us
    ppermute x6, starting transfers between devices, winding(): return lax.ppermute(value, ('md', 'cd'), pairs)  9.75 us
    pallas_call x1, Pallas kernels, local(): pl.pallas_call(functools.partial(second_kernel, 'md'), out_shape=[shape_o...  8.05 us
    ppermute x4, waiting for transfers between devices, ring(): lax.ppermute(value, axis, [(i, (i + steps) % count) for i in range(count)])  6.23 us
    ppermute x6, waiting for transfers between devices, winding(): return lax.ppermute(value, ('md', 'cd'), pairs)  3.63 us
    pallas_call x1, Pallas kernels, local(): pl.pallas_call(functools.partial(pack_kernel, 'cd'), in_specs=[hbm] * 5 +...  3.46 us
    pallas_call x1, Pallas kernels, local(): pl.pallas_call(functools.partial(first_kernel, 'md', 'cd'), out_shape=[sh...  2.87 us
    pallas_call x1, Pallas kernels, local(): pl.pallas_call(advance_kernel, out_shape=[shape_of(5, *plain), shape_of(5...  2.71 us
  transfers between devices with their start and end apart: 10, of which 4 were waited for; matrix products, arithmetic and copies ran while one was open for 0% of the time, Pallas kernels for 27%

profile of v3, /device:TPU:105, one launch (start us, length us, event | category | flops | bytes accessed | tf_op | source)
XLA Modules:
  0.0 55.7 jit_solution(5761881517800806314)
XLA Ops:
  0.6 0.0 copy-start.4
  0.6 0.7 %copy-done.4 = f32[128,1,16]{0,2,1:T(8,128)S(1)} copy-done((f32[128,1,16]{0,2,1:T(8,128)S(1)}, f32[128,1,16]{0,2,1:T(8,128)}, u32[]{:S(2)}) %copy-start.4) | copy-done | bytes 8216
  1.3 3.5 %shard_map.112 = (f32[23,16,128]{2,1,0:T(8,128)S(1)}, f32[13,16,128]{2,1,0:T(8,128)S(1)}, f32[13,16,128]{2,1,0:T(8,128)S(1)}, f32[5,18,2,32,128]{4,3,2,1,0:T(8,1...) custom-call(f32[5,16,16,256]{3,2,1,0:T(8,128)} %s0.1, ...), custom_call_target="tpu_custom_call" | custom-call | flops 4000000 | bytes 12000000 | tf_op jit(solution)/shard_map/pallas_call | solution.py:1047
  4.8 3.4 %collective-permute-start = (f32[13,16,128]{2,1,0:T(8,128)S(1)}, f32[13,16,128]{2,1,0:T(8,128)S(1)}, u32[]{:S(2)}, u32[]{:S(2)}) collective-permute-start(f32[13,16,128]{2,1,0:T(8,128)S(1)} %get-tuple-element.34), channel_id=1, source_target_pairs={{0,8},{8,16},{16,24},{24,32},{32,40},{40,48},{48,56},{56,64},{64,7... | collective-permute-start | bytes 319496 | tf_op jit(solution)/shard_map/ppermute | solution.py:1009
  8.2 0.0 collective-permute-start.1
  8.2 0.0 collective-permute-start.3
  8.2 3.6 %collective-permute-start.2 = (f32[16,128]{1,0:T(8,128)S(1)}, f32[16,128]{1,0:T(8,128)S(1)}, u32[]{:S(2)}, u32[]{:S(2)}) collective-permute-start(f32[16,128]{1,0:T(8,128)S(1)} %bitcast.22), channel_id=1, source_target_pairs={{0,16},{8,24},{16,32},{24,40},{32,48},{40,56},{48,64},{56,72},{64,... | collective-permute-start | bytes 24584 | tf_op jit(solution)/shard_map/ppermute | solution.py:1009
  11.8 0.0 copy-start.1
  11.8 0.0 copy-start.2
  11.8 0.0 copy-start.3
  11.8 0.0 copy-start.5
  11.8 1.9 %shard_map.113.s1_in = f32[5,18,2,32,128]{4,3,2,1,0:T(8,128)S(1)} custom-call(f32[5,18,2,32,128]{4,3,2,1,0:T(8,128)S(1)} %get-tuple-element.36.field, f32[11,18,2,16,128]{4,3,2,1,0:T(8,128)S(1)} %get-tuple-element.37.coef, f32[18,2,16,128]{3,2,1,0:T(8,128)S(1)} %get-tuple-element.39.base.base_in, f32[18,2,32,128]{3,2,1,0:T(8,128)S(1)} %get-tuple-element.38.uy), custom_call_target="tpu_custom_call" | custom-call | flops 2000000 | bytes 6000000 | tf_op jit(solution)/shard_map/pallas_call | solution.py:1075
  13.7 0.0 collective-permute-done.3.far_second
  13.7 0.0 collective-permute-done.2.far_first
  13.7 0.0 collective-permute-done.near_first
  13.7 0.7 %collective-permute-done.1.near_second = f32[13,16,128]{2,1,0:T(8,128)S(1)} collective-permute-done((f32[13,16,128]{2,1,0:T(8,128)S(1)}, f32[13,16,128]{2,1,0:T(8,128)S(1)}, u32[]{:S(2)}, u32[]{:S(2)}) %collective-permute-start.1) | collective-permute-done | bytes 106528 | tf_op jit(solution)/shard_map/ppermute | solution.py:1009
  14.4 0.0 copy-done.1
  14.4 0.0 copy-done.2
  14.4 0.0 copy-done.3
  14.4 0.0 copy-done.5
  14.4 0.0 copy-start
  14.4 2.9 %shard_map.114 = (f32[5,18,2,32,128]{4,3,2,1,0:T(8,128)S(1)}, f32[18,2,16,128]{3,2,1,0:T(8,128)S(1)}, f32[5,2,32,128]{3,2,1,0:T(8,128)}, f32[11,2,16,128]{3,2,1,...) custom-call(f32[23,16,128]{2,1,0:T(8,128)S(1)} %get-tuple-element.33, ...), custom_call_target="tpu_custom_call" | custom-call | flops 4000000 | bytes 12000000 | tf_op jit(solution)/shard_map/pallas_call | solution.py:1083
  17.3 1.9 %collective-permute-start.4 = (f32[376,128]{1,0:T(8,128)S(1)}, f32[376,128]{1,0:T(8,128)S(1)}, u32[]{:S(2)}, u32[]{:S(2)}) collective-permute-start(f32[376,128]{1,0:T(8,128)S(1)} %get-tuple-element.49.own_up), channel_id=1, source_target_pairs={{0,1},{1,2},{2,3},{3,4},{4,5},{5,6},{6,7},{7,0},{8,9},{9,10},{10,1... | collective-permute-start | bytes 577544 | tf_op jit(solution)/shard_map/ppermute | solution.py:996
  19.2 3.2 %collective-permute-start.5 = (f32[376,128]{1,0:T(8,128)S(1)}, f32[376,128]{1,0:T(8,128)S(1)}, u32[]{:S(2)}, u32[]{:S(2)}) collective-permute-start(f32[376,128]{1,0:T(8,128)S(1)} %get-tuple-element.50.own_down), channel_id=1, source_target_pairs={{0,7},{1,0},{2,1},{3,2},{4,3},{5,4},{6,5},{7,6},{8,15},{9,8},{10,9... | collective-permute-start | bytes 577544 | tf_op jit(solution)/shard_map/ppermute | solution.py:996
  22.4 0.0 copy-done
  22.4 2.7 %shard_map.115 = (f32[5,18,2,16,128]{4,3,2,1,0:T(8,128)S(1)}, f32[5,18,2,16,128]{4,3,2,1,0:T(8,128)S(1)}) custom-call(f32[5,18,2,32,128]{4,3,2,1,0:T(8,128)S(1)} %get-tuple-element.40.s1.s1_in, f32[5,2,32,128]{3,2,1,0:T(8,128)S(1)} %get-tuple-element.41.strip_s1.strip_s1_in, f32[11,18,2,16,128]{4,3,2,1,0:T(8,128)S(1)} %get-tuple-element.37.coef, ...), custom_call_target="tpu_custom_call" | custom-call | flops 4000000 | bytes 12000000 | tf_op jit(solution)/shard_map/pallas_call | solution.py:1121
  25.1 1.4 %collective-permute-done.4.from_below.weights_below = f32[376,128]{1,0:T(8,128)S(1)} collective-permute-done((f32[376,128]{1,0:T(8,128)S(1)}, f32[376,128]{1,0:T(8,128)S(1)}, u32[]{:S(2)}, u32[]{:S(2)}) %collective-permute-start.4) | collective-permute-done | bytes 192544 | tf_op jit(solution)/shard_map/ppermute | solution.py:996
  26.5 4.8 %collective-permute-done.5.from_above.weights_above = f32[376,128]{1,0:T(8,128)S(1)} collective-permute-done((f32[376,128]{1,0:T(8,128)S(1)}, f32[376,128]{1,0:T(8,128)S(1)}, u32[]{:S(2)}, u32[]{:S(2)}) %collective-permute-start.5) | collective-permute-done | bytes 192544 | tf_op jit(solution)/shard_map/ppermute | solution.py:996
  31.3 2.1 %shard_map.116 = (f32[5,2,2,16,128]{4,3,2,1,0:T(8,128)S(1)}, f32[5,4,2,16,128]{4,3,2,1,0:T(8,128)S(1)}, f32[5,2,32,128]{3,2,1,0:T(8,128)S(1)}, f32[5,2,32,128]{3...) custom-call(f32[5,18,2,32,128]{4,3,2,1,0:T(8,128)S(1)} %get-tuple-element.40.s1.s1_in, ...), custom_call_target="tpu_custom_call" | custom-call | flops 2000000 | bytes 6000000 | tf_op jit(solution)/shard_map/pallas_call | solution.py:1128
  33.5 0.1 collective-permute-start.6
  33.6 5.1 %collective-permute-start.7 = (f32[344,128]{1,0:T(8,128)S(1)}, f32[344,128]{1,0:T(8,128)S(1)}, u32[]{:S(2)}, u32[]{:S(2)}) collective-permute-start(f32[344,128]{1,0:T(8,128)S(1)} %get-tuple-element.58.own_down), channel_id=1, source_target_pairs={{0,7},{1,0},{2,1},{3,2},{4,3},{5,4},{6,5},{7,6},{8,15},{9,8},{10,9... | collective-permute-start | bytes 528392 | tf_op jit(solution)/shard_map/ppermute | solution.py:996
  38.6 8.1 %shard_map.117 = (f32[5,16,16,256]{3,2,1,0:T(8,128)}, f32[5,18,2,16,128]{4,3,2,1,0:T(8,128)S(1)}, f32[16,384]{1,0:T(8,128)S(1)}) custom-call(f32[5,18,2,32,128]{4,3,2,1,0:T(8,128)S(1)} %get-tuple-element.40.s1.s1_in, f32[5,18,2,16,128]{4,3,2,1,0:T(8,128)S(1)} %get-tuple-element.43.s2_in, f32[5,18,2,16,128]{4,3,2,1,0:T(8,128)S(1)} %get-tuple-element.44.goal, ...), custom_call_target="tpu_custom_call" | custom-call | flops 9000000 | bytes 27000000 | tf_op jit(solution)/shard_map/pallas_call | solution.py:1161
  46.7 0.0 collective-permute-done.6.from_below
  46.7 0.0 collective-permute-done.7.from_above
  46.7 0.4 shard_map.119
  47.1 2.8 %collective-permute-start.8 = (f32[16,128]{1,0:T(8,128)S(1)}, f32[16,128]{1,0:T(8,128)S(1)}, u32[]{:S(2)}, u32[]{:S(2)}) collective-permute-start(f32[16,128]{1,0:T(8,128)S(1)} %get-tuple-element.61), channel_id=1, source_target_pairs={{0,8},{8,16},{16,24},{24,32},{32,40},{40,48},{48,56},{56,64},{64,7... | collective-permute-start | bytes 24584 | tf_op jit(solution)/shard_map/ppermute | solution.py:1009
  49.9 0.0 collective-permute-start.9
  49.9 2.2 %shard_map.118 = f32[5,16,16,256]{3,2,1,0:T(8,128)} custom-call(f32[5,18,2,16,128]{4,3,2,1,0:T(8,128)S(1)} %get-tuple-element.56.adj0_in, f32[5,18,2,32,128]{4,3,2,1,0:T(8,128)S(1)} %get-tuple-element.36.field, f32[11,18,2,16,128]{4,3,2,1,0:T(8,128)S(1)} %get-tuple-element.37.coef, f32[18,2,16,128]{3,2,1,0:T(8,128)S(1)} %get-tuple-element.42.base, ...), custom_call_target="tpu_custom_call" | custom-call | flops 2000000 | bytes 6000000 | tf_op jit(solution)/shard_map/pallas_call | solution.py:1204
  52.1 0.0 collective-permute-done.8
  52.1 2.9 %collective-permute-done.9 = f32[16,128]{1,0:T(8,128)S(1)} collective-permute-done((f32[16,128]{1,0:T(8,128)S(1)}, f32[16,128]{1,0:T(8,128)S(1)}, u32[]{:S(2)}, u32[]{:S(2)}) %collective-permute-start.9) | collective-permute-done | bytes 8224 | tf_op jit(solution)/shard_map/ppermute | solution.py:1009
  55.1 0.6 %add_bitcast_fusion = f32[128,1,16]{0,2,1:T(8,128)} fusion(f32[16,128]{1,0:T(8,128)S(1)} %collective-permute-done.9, f32[16,128]{1,0:T(8,128)S(1)} %get-tuple-element.60, f32[16,128]{1,0:T(8,128)S(1)} %collective-permute-done.8), kind=kLoop, calls=%fused_computation | loop fusion | flops 4096 | bytes 32768 | tf_op jit(solution)/shard_map/broadcast_in_dim | solution.py:1225
Async XLA Ops:
  0.6 0.7 %copy-start.4 = (f32[128,1,16]{0,2,1:T(8,128)S(1)}, f32[128,1,16]{0,2,1:T(8,128)}, u32[]{:S(2)}) copy-start(f32[128,1,16]{0,2,1:T(8,128)} %param.14) | copy-start | bytes 24580
  4.8 8.9 %collective-permute-start = (f32[13,16,128]{2,1,0:T(8,128)S(1)}, f32[13,16,128]{2,1,0:T(8,128)S(1)}, u32[]{:S(2)}, u32[]{:S(2)}) collective-permute-start(f32[13,16,128]{2,1,0:T(8,128)S(1)} %get-tuple-element.34), channel_id=1, source_target_pairs={{0,8},{8,16},{16,24},{24,32},{32,40},{40,48},{48,56},{56,64},{64,7... | collective-permute-start | bytes 319496 | tf_op jit(solution)/shard_map/ppermute | solution.py:1009
  8.2 6.2 %collective-permute-start.1 = (f32[13,16,128]{2,1,0:T(8,128)S(1)}, f32[13,16,128]{2,1,0:T(8,128)S(1)}, u32[]{:S(2)}, u32[]{:S(2)}) collective-permute-start(f32[13,16,128]{2,1,0:T(8,128)S(1)} %get-tuple-element.35), channel_id=1, source_target_pairs={{0,1},{8,0},{16,8},{24,16},{32,24},{40,32},{48,40},{56,48},{64,56}... | collective-permute-start | bytes 319496 | tf_op jit(solution)/shard_map/ppermute | solution.py:1009
  8.2 5.5 %collective-permute-start.3 = (f32[16,128]{1,0:T(8,128)S(1)}, f32[16,128]{1,0:T(8,128)S(1)}, u32[]{:S(2)}, u32[]{:S(2)}) collective-permute-start(f32[16,128]{1,0:T(8,128)S(1)} %bitcast.21), channel_id=1, source_target_pairs={{0,1},{8,9},{16,0},{24,8},{32,16},{40,24},{48,32},{56,40},{64,48},... | collective-permute-start | bytes 24584 | tf_op jit(solution)/shard_map/ppermute | solution.py:1009
  8.2 5.5 %collective-permute-start.2 = (f32[16,128]{1,0:T(8,128)S(1)}, f32[16,128]{1,0:T(8,128)S(1)}, u32[]{:S(2)}, u32[]{:S(2)}) collective-permute-start(f32[16,128]{1,0:T(8,128)S(1)} %bitcast.22), channel_id=1, source_target_pairs={{0,16},{8,24},{16,32},{24,40},{32,48},{40,56},{48,64},{56,72},{64,... | collective-permute-start | bytes 24584 | tf_op jit(solution)/shard_map/ppermute | solution.py:1009
  11.8 2.6 %copy-start.1 = (s32[4096,1]{0,1:T(1,128)S(1)}, s32[4096,1]{0,1:T(1,128)}, u32[]{:S(2)}) copy-start(s32[4096,1]{0,1:T(1,128)} %param.15) | copy-start | bytes 49156
  11.8 2.6 %copy-start.2 = (s32[4096,1]{0,1:T(1,128)S(1)}, s32[4096,1]{0,1:T(1,128)}, u32[]{:S(2)}) copy-start(s32[4096,1]{0,1:T(1,128)} %param.16) | copy-start | bytes 49156
  11.8 2.6 %copy-start.3 = (s32[4096,1]{0,1:T(1,128)S(1)}, s32[4096,1]{0,1:T(1,128)}, u32[]{:S(2)}) copy-start(s32[4096,1]{0,1:T(1,128)} %param.17) | copy-start | bytes 49156
  11.8 2.6 %copy-start.5 = (f32[128,1,16]{0,2,1:T(8,128)S(1)}, f32[128,1,16]{0,2,1:T(8,128)}, u32[]{:S(2)}) copy-start(f32[128,1,16]{0,2,1:T(8,128)} %param.14) | copy-start | bytes 24580
  14.4 8.0 %copy-start = (f32[5,16,16,256]{3,2,1,0:T(8,128)S(1)}, f32[5,16,16,256]{3,2,1,0:T(8,128)}, u32[]{:S(2)}) copy-start(f32[5,16,16,256]{3,2,1,0:T(8,128)} %tgt.3) | copy-start | bytes 3932164
  17.3 9.2 %collective-permute-start.4 = (f32[376,128]{1,0:T(8,128)S(1)}, f32[376,128]{1,0:T(8,128)S(1)}, u32[]{:S(2)}, u32[]{:S(2)}) collective-permute-start(f32[376,128]{1,0:T(8,128)S(1)} %get-tuple-element.49.own_up), channel_id=1, source_target_pairs={{0,1},{1,2},{2,3},{3,4},{4,5},{5,6},{6,7},{7,0},{8,9},{9,10},{10,1... | collective-permute-start | bytes 577544 | tf_op jit(solution)/shard_map/ppermute | solution.py:996
  19.2 12.1 %collective-permute-start.5 = (f32[376,128]{1,0:T(8,128)S(1)}, f32[376,128]{1,0:T(8,128)S(1)}, u32[]{:S(2)}, u32[]{:S(2)}) collective-permute-start(f32[376,128]{1,0:T(8,128)S(1)} %get-tuple-element.50.own_down), channel_id=1, source_target_pairs={{0,7},{1,0},{2,1},{3,2},{4,3},{5,4},{6,5},{7,6},{8,15},{9,8},{10,9... | collective-permute-start | bytes 577544 | tf_op jit(solution)/shard_map/ppermute | solution.py:996
  33.5 13.2 %collective-permute-start.6 = (f32[344,128]{1,0:T(8,128)S(1)}, f32[344,128]{1,0:T(8,128)S(1)}, u32[]{:S(2)}, u32[]{:S(2)}) collective-permute-start(f32[344,128]{1,0:T(8,128)S(1)} %get-tuple-element.57.own_up), channel_id=1, source_target_pairs={{0,1},{1,2},{2,3},{3,4},{4,5},{5,6},{6,7},{7,0},{8,9},{9,10},{10,1... | collective-permute-start | bytes 528392 | tf_op jit(solution)/shard_map/ppermute | solution.py:996
  33.6 13.1 %collective-permute-start.7 = (f32[344,128]{1,0:T(8,128)S(1)}, f32[344,128]{1,0:T(8,128)S(1)}, u32[]{:S(2)}, u32[]{:S(2)}) collective-permute-start(f32[344,128]{1,0:T(8,128)S(1)} %get-tuple-element.58.own_down), channel_id=1, source_target_pairs={{0,7},{1,0},{2,1},{3,2},{4,3},{5,4},{6,5},{7,6},{8,15},{9,8},{10,9... | collective-permute-start | bytes 528392 | tf_op jit(solution)/shard_map/ppermute | solution.py:996
  47.1 5.0 %collective-permute-start.8 = (f32[16,128]{1,0:T(8,128)S(1)}, f32[16,128]{1,0:T(8,128)S(1)}, u32[]{:S(2)}, u32[]{:S(2)}) collective-permute-start(f32[16,128]{1,0:T(8,128)S(1)} %get-tuple-element.61), channel_id=1, source_target_pairs={{0,8},{8,16},{16,24},{24,32},{32,40},{40,48},{48,56},{56,64},{64,7... | collective-permute-start | bytes 24584 | tf_op jit(solution)/shard_map/ppermute | solution.py:1009
  49.9 5.2 %collective-permute-start.9 = (f32[16,128]{1,0:T(8,128)S(1)}, f32[16,128]{1,0:T(8,128)S(1)}, u32[]{:S(2)}, u32[]{:S(2)}) collective-permute-start(f32[16,128]{1,0:T(8,128)S(1)} %get-tuple-element.62), channel_id=1, source_target_pairs={{0,1},{8,0},{16,8},{24,16},{32,24},{40,32},{48,40},{56,48},{64,56}... | collective-permute-start | bytes 24584 | tf_op jit(solution)/shard_map/ppermute | solution.py:1009

commit v4 on v3

--- a/solution.py
+++ b/solution.py
@@ -281,7 +281,9 @@
     base,
     uy,
     stage,
+    needle_stage,
     sems,
+    needle_sem,
 ):
     layers = stage.shape[1]
     blocks = sems.shape[0]
@@ -302,6 +304,8 @@
     for block in range(blocks):
         for copy in copies(block):
             copy.start()
+    needle_copy = pltpu.make_async_copy(needle, needle_stage, needle_sem)
+    needle_copy.start()
     lane = lane_iota(out.shape[1:])
     Field(field, None).clear()
     clear_planes(coef, [UZ])
@@ -345,8 +349,9 @@
 
     odd = lax.axis_index(axis_cd) % 2 == 1
     outer = lane % 8 < HALO
-    first[PAIRS] = needle[...]
-    second[PAIRS] = needle[...]
+    needle_copy.wait()
+    first[PAIRS] = needle_stage[...]
+    second[PAIRS] = needle_stage[...]
     for c in range(PAIRS):
         here, other = out[c], out[min(c + PAIRS, NEEDLES - 1)]
         to_right = jnp.where(outer, here, pltpu.roll(other, HALO, 1))
@@ -403,10 +408,8 @@
     field,
     coef,
     uy,
-    base_in,
-    s1_in,
     s1,
-    base,
+    gain,
     strip_s0,
     strip_coef,
     strip_base,
@@ -418,7 +421,6 @@
     spread,
     cover,
     source,
-    joint,
 ):
     layers = field.shape[1] - 2
     height = own.shape[1]
@@ -467,9 +469,12 @@
         product = product + lax.dot_general(
             spread[part], cover[...], (((1,), (1,)), ((), ())), preferred_element_type=F32
         )
-    source[...] = (DT * product).reshape(source.shape)
-
-    state = Field(field, strip_s0, joint)
+    product = DT * product
+    for tile in range(2):
+        gain[1 : layers + 1, tile] = product[:, span(tile)].reshape(layers, height, LANES)
+    source[...] = product[:, span(2)].reshape(source.shape)
+
+    state = Field(field, strip_s0)
     state.clear_strips()
     has_left, has_right = md > 0, md < count - 1
     for side in range(2):
@@ -495,7 +500,7 @@
         damp = 6.0 * turn + (jnp.abs(u[0]) + jnp.abs(u[1]) + jnp.abs(u[2]))
         taken = jnp.zeros((height, LANES), F32)
         for z in range(layers):
-            moved = pltpu.roll(source[z, :, span(2)], (8 * z - 8 * side) % LANES, 1)
+            moved = pltpu.roll(source[z], (8 * z - 8 * side) % LANES, 1)
             taken = jnp.where(lane // 8 == z, moved, taken)
         strip_base[side] = damp + taken
 
@@ -507,7 +512,6 @@
         out = forward(a, m, damp, spin, wind, state.strip_around(side))
         for c in range(5):
             strip_s1[c, side, OWN] = out[c]
-    state.join()
 
     def put(side):
         def at(place):
@@ -521,10 +525,83 @@
         up[at(10)] = -jnp.minimum(wind[23:24], 0.0)
         down[at(10)] = jnp.maximum(wind[8:9], 0.0)
 
+    for message, row in ((up, 15), (down, 0)):
+        for tile in range(2):
+            u = row_of(coef, UX, tile, row)
+            if tile == 0:
+                weight, turn = jnp.where(lane == 0, jnp.maximum(u, 0.0), 0.0), 1
+            else:
+                weight = jnp.where(lane == LANES - 1, -jnp.minimum(u, 0.0), 0.0)
+                turn = LANES - 1
+            gained = row_of(gain, 0, tile, row)
+            for c in range(5):
+                left, right = (strip_s0[c, side, 8 + row : 9 + row] for side in (0, 1))
+                edge = pltpu.roll(edge_column(left, right, layers), turn, 1)
+                old = row_of(field, c, tile, 8 + row)
+                new = row_of(s1, c, tile, 8 + row) - gained * old + weight * edge
+                message[planes(tile * 11 + c, layers)] = old
+                message[planes(tile * 11 + 5 + c, layers)] = new
+            speed = row_of(uy, 0, tile, 8 + row)
+            outward = -jnp.minimum(speed, 0.0) if row else jnp.maximum(speed, 0.0)
+            message[planes(tile * 11 + 10, layers)] = outward
+    for side in range(2):
+        put(side)
+
+
+def cd_flags(axis_cd):
+    cd = lax.axis_index(axis_cd)
+    return cd > 0, cd < lax.axis_size(axis_cd) - 1
+
+
+def advance_kernel(
+    s1_in,
+    field,
+    gain,
+    coef,
+    base_in,
+    uy,
+    tgt,
+    strip_s0,
+    strip_s1,
+    strip_coef,
+    strip_base,
+    strip_uy,
+    strip_tgt,
+    s1,
+    base,
+    s2,
+    goal,
+    adj1,
+    dots,
+    adj2,
+    strip_adj2,
+    joint,
+    joint1,
+    joint2,
+):
+    layers, height = tgt.shape[1], tgt.shape[2]
+    lane = lane_iota((height, LANES))
+    start = Field(field, strip_s0, joint)
+    state = Field(s1, strip_s1, joint1)
+    delta = Field(adj2, strip_adj2, joint2)
+    start.join()
+    state.join()
+    clear_planes(s1)
+    clear_planes(adj2)
+    for side in range(2):
+        m, damp = coefficients(strip_coef, strip_base, side)
+        wind = (strip_coef[UX, side], strip_uy[side, OWN], strip_coef[UZ, side])
+        a = [strip_s1[c, side, OWN] for c in range(5)]
+        spin = strip_coef[SPREAD, side]
+        out = forward(a, m, damp, spin, wind, state.strip_around(side))
+        for c in range(5):
+            strip_adj2[c, side, OWN] = out[c] - strip_tgt[c, side]
+    delta.join()
+
     def mend(z, carry):
         for tile in range(2):
-            gain = source[z, :, span(tile)]
-            base[z + 1, tile] = base_in[z + 1, tile] + gain
+            gained = gain[z + 1, tile]
+            base[z + 1, tile] = base_in[z + 1, tile] + gained
             u = coef[UX, z + 1, tile]
             if tile == 0:
                 weight, turn = jnp.where(lane == 0, jnp.maximum(u, 0.0), 0.0), 1
@@ -534,34 +611,12 @@
                 edge = pltpu.roll(joint[c], (2 * LANES - HALO + turn - 8 * z) % LANES, 1)
                 s1[c, z + 1, tile, OWN] = (
                     s1_in[c, z + 1, tile, OWN]
-                    - gain * field[c, z + 1, tile, OWN]
+                    - gained * field[c, z + 1, tile, OWN]
                     + weight * edge
                 )
         return carry
 
-    clear_planes(s1)
     lax.fori_loop(0, layers, mend, 0)
-    for tile in range(2):
-        for message, row in ((up, 23), (down, 8)):
-            for c in range(5):
-                message[planes(tile * 11 + c, layers)] = row_of(field, c, tile, row)
-                message[planes(tile * 11 + 5 + c, layers)] = row_of(s1, c, tile, row)
-        out, into = row_of(uy, 0, tile, 23), row_of(uy, 0, tile, 8)
-        up[planes(tile * 11 + 10, layers)] = -jnp.minimum(out, 0.0)
-        down[planes(tile * 11 + 10, layers)] = jnp.maximum(into, 0.0)
-    for side in range(2):
-        put(side)
-
-
-def cd_flags(axis_cd):
-    cd = lax.axis_index(axis_cd)
-    return cd > 0, cd < lax.axis_size(axis_cd) - 1
-
-
-def advance_kernel(s1, strip_s1, coef, base, uy, tgt, s2, goal, joint):
-    layers = tgt.shape[1]
-    state = Field(s1, strip_s1, joint)
-    state.join()
 
     def advance(z, carry):
         for tile in range(2):
@@ -570,12 +625,32 @@
             wind = (coef[(UX,) + at], uy[at + (OWN,)], coef[(UZ,) + at])
             a = [state.own(c, z, tile) for c in range(5)]
             out = forward(a, m, damp, coef[(SPREAD,) + at], wind, state.around(z, tile))
-            for c in range(5):
+            total = 0.0
+            for c in range(5):
+                wanted = tgt[c, z, :, span(tile)]
+                miss = out[c] - wanted
                 s2[(c,) + at] = out[c]
-                goal[(c,) + at] = tgt[c, z, :, span(tile)]
+                goal[(c,) + at] = wanted
+                adj2[(c,) + at + (OWN,)] = miss
+                total = total + miss * a[c]
+            dots[at] = total
         return carry
 
     lax.fori_loop(0, layers, advance, 0)
+    edge_x = merged(strip_coef, UX, slice(None))
+
+    def retreat(z, carry):
+        for tile in range(2):
+            m, damp = coefficients(coef, base, z + 1, tile)
+            a = [state.own(c, z, tile) for c in range(5)]
+            b = [delta.own(c, z, tile) for c in range(5)]
+            wind = back_wind(coef, uy, edge_x, z, tile)
+            out = backward(b, a, m, damp, wind, delta.around(z, tile))
+            for c in range(5):
+                adj1[c, z + 1, tile] = out[c]
+        return carry
+
+    lax.fori_loop(0, layers, retreat, 0)
 
 
 def edge_kernel(
@@ -594,8 +669,10 @@
     own_down,
     from_below,
     from_above,
-    s1_edge,
     s2_edge,
+    adj2_edge,
+    adj1_edge,
+    dots_edge,
     strip_adj2,
     strip_adj1,
     up,
@@ -676,7 +753,6 @@
                 lines[1][c, tile] = plane(mine, 5 + c, tile) + jnp.where(
                     valid, plane(mine, 10, tile) * old, 0.0
                 )
-                s1_edge[c, number, tile] = lines[1][c, tile]
                 for k in (1, 2):
                     lines[k + 1][c, tile] = row_of(s1, c, tile, 8 + rows[k])
 
@@ -709,9 +785,14 @@
                     )
 
                 out = forward(a, m, damp, row_of(coef, SPREAD, tile, row), wind, around)
+                total = 0.0
                 for c in range(5):
+                    miss = out[c] - row_of(goal, c, tile, row)
                     s2_edge[c, 2 * number + k, tile] = out[c]
-                    misses[k][c, tile] = out[c] - row_of(goal, c, tile, row)
+                    adj2_edge[c, 2 * number + k, tile] = miss
+                    misses[k][c, tile] = miss
+                    total = total + miss * a[c]
+                dots_edge[2 * number + k, tile] = total
 
         row = rows[0]
         edges = [strip_edge(strip_adj2, c, row) for c in range(5)]
@@ -741,6 +822,7 @@
             for c in range(5):
                 outgoing[planes(tile * 10 + c, layers)] = weight * b[c]
                 outgoing[planes(tile * 10 + 5 + c, layers)] = weight * out[c]
+                adj1_edge[c, number, tile] = out[c]
 
 
 def needle_feet(ref, md, count):
@@ -763,11 +845,15 @@
 
 def second_kernel(
     axis_md,
-    s1_in,
+    s1,
     s2_in,
     goal,
-    s1_edge,
+    adj1_in,
+    dots_in,
     s2_edge,
+    adj2_edge,
+    adj1_edge,
+    dots_edge,
     field,
     coef,
     base,
@@ -783,11 +869,9 @@
     gained,
     adj1,
     dots,
-    s1,
+    sens,
     s2,
-    adj2,
     joint,
-    joint1,
 ):
     layers, height = goal.shape[1] - 2, goal.shape[3]
     length = 2 * LANES
@@ -796,53 +880,76 @@
 
     def gather(z, carry):
         for tile in range(2):
-            for c in range(5):
-                s1[c, z + 1, tile] = s1_in[c, z + 1, tile, OWN]
+            dots[z + 1, tile] = dots_in[z + 1, tile]
+            for c in range(5):
                 s2[c, z + 1, tile] = s2_in[c, z + 1, tile]
+                adj1[c, z + 1, tile, OWN] = adj1_in[c, z + 1, tile]
         return carry
 
     lax.fori_loop(0, layers, gather, 0)
-    for c in range(5):
-        for tile in range(2):
-            for number, row in enumerate((0, 15)):
-                set_row(s1, c, tile, row, s1_edge[c, number, tile])
-            for number, row in enumerate((0, 1, 15, 14)):
+    for tile in range(2):
+        for number, row in enumerate((0, 1, 15, 14)):
+            set_row(dots, 0, tile, row, dots_edge[number, tile])
+            for c in range(5):
                 set_row(s2, c, tile, row, s2_edge[c, number, tile])
-
-    delta = Field(adj2, strip_adj2, joint)
-    delta.clear()
-    delta.join()
-
-    def compare(z, carry):
-        for tile in range(2):
-            total = 0.0
-            for c in range(5):
-                value = s2[c, z + 1, tile]
-                miss = value - goal[c, z + 1, tile]
-                s2_out[c, z, :, span(tile)] = value
-                adj2[c, z + 1, tile, OWN] = miss
-                total = total + miss * s1[c, z + 1, tile]
-            dots[z, :, span(tile)] = total
+        for number, row in enumerate((0, 15)):
+            for c in range(5):
+                set_row(adj1, c, tile, 8 + row, adj1_edge[c, number, tile])
+
+    for number, rows in enumerate(((0, 1, 2, 3), (15, 14, 13, 12))):
+        lines = [{}, {}, {}, {}]
+        for c in range(5):
+            for tile in range(2):
+                for k in (0, 1):
+                    lines[k][c, tile] = adj2_edge[c, 2 * number + k, tile]
+                for k in (2, 3):
+                    state = row_of(s2_in, c, tile, rows[k])
+                    lines[k][c, tile] = state - row_of(goal, c, tile, rows[k])
+
+        def ordered(outer, inner):
+            return (outer, inner) if number == 0 else (inner, outer)
+
+        for k in (1, 2):
+            row = rows[k]
+            edges = []
+            for c in range(5):
+                left, right = (strip_adj2[c, side, 8 + row : 9 + row] for side in (0, 1))
+                edges.append(edge_column(left, right, layers))
+            left, right = (strip_coef[UX, side, row : row + 1] for side in (0, 1))
+            edge = edge_column(left, right, layers)
+            for tile in range(2):
+                m = {key: row_of(coef, place, tile, row) for key, place in PLACE.items()}
+                damp = row_of(base, 0, tile, row)
+                a = [row_of(s1, c, tile, 8 + row) for c in range(5)]
+                b = [lines[k][c, tile] for c in range(5)]
+                wind = (
+                    x_pair([row_of(coef, UX, t, row) for t in range(2)], tile, edge),
+                    ordered(*(row_of(uy, 0, tile, 8 + rows[i]) for i in (k - 1, k + 1))),
+                    layer_pair(row_of(coef, UZ, tile, row)),
+                )
+
+                def around(c):
+                    return (
+                        x_pair([lines[k][c, t] for t in range(2)], tile, edges[c]),
+                        ordered(lines[k - 1][c, tile], lines[k + 1][c, tile]),
+                        layer_pair(b[c]),
+                    )
+
+                out = backward(b, a, m, damp, wind, around)
+                for c in range(5):
+                    set_row(adj1, c, tile, 8 + row, out[c])
+
+    def write(z, carry):
+        for tile in range(2):
+            for c in range(5):
+                s2_out[c, z, :, span(tile)] = s2[c, z + 1, tile]
         return carry
 
-    lax.fori_loop(0, layers, compare, 0)
+    lax.fori_loop(0, layers, write, 0)
     edge_x = merged(strip_coef, UX, slice(None))
-
-    def retreat(z, carry):
-        for tile in range(2):
-            m, damp = coefficients(coef, base, z + 1, tile)
-            a = [s1[c, z + 1, tile] for c in range(5)]
-            b = [delta.own(c, z, tile) for c in range(5)]
-            wind = back_wind(coef, uy, edge_x, z, tile)
-            out = backward(b, a, m, damp, wind, delta.around(z, tile))
-            for c in range(5):
-                adj1[c, z + 1, tile, OWN] = out[c]
-        return carry
-
-    last_delta = Field(adj1, strip_adj1, joint1)
+    last_delta = Field(adj1, strip_adj1, joint)
     last_delta.clear()
     last_delta.join()
-    lax.fori_loop(0, layers, retreat, 0)
 
     def finish(z, carry):
         for tile in range(2):
@@ -851,17 +958,17 @@
             b = [last_delta.own(c, z, tile) for c in range(5)]
             wind = back_wind(coef, uy, edge_x, z, tile)
             out = backward(b, a, m, damp, wind, last_delta.around(z, tile))
-            total = dots[z, :, span(tile)]
+            total = dots[z + 1, tile]
             for c in range(5):
                 adj0[c, z + 1, tile] = out[c]
                 total = total + a[c] * b[c]
-            dots[z, :, span(tile)] = -DT * total
+            sens[z, :, span(tile)] = -DT * total
         return carry
 
     lax.fori_loop(0, layers, finish, 0)
     starts, ends, columns = (needle_feet(ref, md, count) for ref in (start, end, column))
     cover = own_cover(md, length, starts, ends)
-    product = covered_sum(dots[...].reshape(layers * height, length), cover)
+    product = covered_sum(sens[...].reshape(layers * height, length), cover)
     picked = jnp.where(row_iota((height, starts.shape[1])) == columns, 1.0, 0.0)
     for z in range(layers):
         gained[z : z + 1] = jnp.sum(
@@ -1046,7 +1153,7 @@
     blocks = 4
     packed, first, second, field, coef, base, uy = pl.pallas_call(
         functools.partial(pack_kernel, "cd"),
-        in_specs=[hbm] * 5 + [pl.BlockSpec(memory_space=pltpu.VMEM)],
+        in_specs=[hbm] * 6,
         out_shape=[
             shape_of(NEEDLES, height, LANES),
             shape_of(PAIRS + 1, height, LANES),
@@ -1058,16 +1165,17 @@
         ],
         scratch_shapes=[
             scratch(NEEDLES, layers, height, length),
+            scratch(*rates.shape),
             pltpu.SemaphoreType.DMA((blocks, 5)),
+            pltpu.SemaphoreType.DMA,
         ],
         compiler_params=params(20),
         cost_estimate=cost(4),
     )(
         *(
             pltpu.with_memory_space_constraint(field, pltpu.HBM)
-            for field in (orientation, velocity, velocity_grad, rotary, target)
-        ),
-        rates,
+            for field in (orientation, velocity, velocity_grad, rotary, target, rates)
+        )
     )
     far = both_ways(rates, 2)
     near = winding(first, 1, 0), winding(second, 1, 1)
@@ -1079,11 +1187,10 @@
         cost_estimate=cost(2),
     )(field, coef, base, uy)
 
-    s1, base, strip_s0, strip_coef, strip_base, strip_uy, strip_s1, strip_tgt, up, down = (
+    gain, strip_s0, strip_coef, strip_base, strip_uy, strip_s1, strip_tgt, up, down = (
         pl.pallas_call(
             functools.partial(first_kernel, "md", "cd"),
             out_shape=[
-                shape_of(5, *padded),
                 shape_of(*plain),
                 shape_of(5, *strip_padded),
                 shape_of(COEFS, *strip),
@@ -1097,62 +1204,76 @@
             scratch_shapes=[
                 scratch(3, layers * height, 4 * LANES, dtype=jnp.bfloat16),
                 scratch(length + LANES, 4 * LANES, dtype=jnp.bfloat16),
-                scratch(layers, height, length + LANES),
-                joint,
+                scratch(layers, height, LANES),
             ],
             compiler_params=params(24),
-        cost_estimate=cost(4),
-        )(
-            packed,
-            rates,
-            *near,
-            *far,
-            *feet,
-            field,
-            coef,
-            uy,
-            base,
-            s1,
-        )
+            cost_estimate=cost(3),
+        )(packed, rates, *near, *far, *feet, field, coef, uy, s1)
     )
     below = ring(up, "cd", 1)
     above = ring(down, "cd", -1)
 
-    s2_part, goal = pl.pallas_call(
+    s1, base, s2_part, goal, adj1_part, dots = pl.pallas_call(
         advance_kernel,
-        out_shape=[shape_of(5, *plain), shape_of(5, *plain)],
-        scratch_shapes=[joint],
+        out_shape=[
+            shape_of(5, *padded),
+            shape_of(*plain),
+            shape_of(5, *plain),
+            shape_of(5, *plain),
+            shape_of(5, *plain),
+            shape_of(*plain),
+        ],
+        scratch_shapes=[scratch(5, *padded), scratch(5, *strip_padded), joint, joint, joint],
         compiler_params=params(16),
-        cost_estimate=cost(4),
-    )(s1, strip_s1, coef, base, uy, target)
-    s1_edge, s2_edge, strip_adj2, strip_adj1, back_up, back_down = pl.pallas_call(
-        functools.partial(edge_kernel, "cd"),
-        out_shape=[
-            shape_of(5, 2, 2, layers, LANES),
-            shape_of(5, 4, 2, layers, LANES),
-            shape_of(5, *strip_padded),
-            shape_of(5, *strip_padded),
-            back_message,
-            back_message,
-        ],
-        scratch_shapes=[scratch(5, *strip_padded)],
-        compiler_params=params(16),
-        cost_estimate=cost(2),
+        cost_estimate=cost(8),
     )(
         s1,
-        strip_s1,
+        field,
+        gain,
         coef,
         base,
         uy,
-        goal,
+        target,
+        strip_s0,
+        strip_s1,
         strip_coef,
         strip_base,
         strip_uy,
         strip_tgt,
-        up,
-        down,
-        below,
-        above,
+    )
+    edge_row = (2, layers, LANES)
+    s2_edge, adj2_edge, adj1_edge, dots_edge, strip_adj2, strip_adj1, back_up, back_down = (
+        pl.pallas_call(
+            functools.partial(edge_kernel, "cd"),
+            out_shape=[
+                shape_of(5, 4, *edge_row),
+                shape_of(5, 4, *edge_row),
+                shape_of(5, 2, *edge_row),
+                shape_of(4, *edge_row),
+                shape_of(5, *strip_padded),
+                shape_of(5, *strip_padded),
+                back_message,
+                back_message,
+            ],
+            scratch_shapes=[scratch(5, *strip_padded)],
+            compiler_params=params(16),
+            cost_estimate=cost(2),
+        )(
+            s1,
+            strip_s1,
+            coef,
+            base,
+            uy,
+            goal,
+            strip_coef,
+            strip_base,
+            strip_uy,
+            strip_tgt,
+            up,
+            down,
+            below,
+            above,
+        )
     )
     back_below = ring(back_up, "cd", 1)
     back_above = ring(back_down, "cd", -1)
@@ -1167,21 +1288,23 @@
         ],
         scratch_shapes=[
             scratch(5, *padded),
+            scratch(*plain),
             scratch(layers, height, length),
             scratch(5, *plain),
-            scratch(5, *plain),
-            scratch(5, *padded),
-            joint,
             joint,
         ],
         compiler_params=params(24),
-        cost_estimate=cost(9),
+        cost_estimate=cost(6),
     )(
         s1,
         s2_part,
         goal,
-        s1_edge,
+        adj1_part,
+        dots,
         s2_edge,
+        adj2_edge,
+        adj1_edge,
+        dots_edge,
         field,
         coef,
         base,

time: 55.8 us -> 53.8 us (0.964)
  waiting for transfers between devices: 9.87 us -> 6.01 us
  Pallas kernels: 23.8 us -> 26.4 us
  local copies, waits for them, and re-layouts: 0.71 us -> 0.02 us
    ppermute x4, waiting for transfers between devices: 6.23 us -> 0.21 us  [ring(): lax.ppermute(value, axis, [(i, (i + steps) % count) for i in range(count)])]
    pallas_call x2, Pallas kernels: 6.17 us -> 11.1 us  [the longest x1 7.64 us: local(): pl.pallas_call(advance_kernel, out_shape=[shape_of(5, *padded), shape_of(...]
    ppermute x6, waiting for transfers between devices: 3.63 us -> 5.8 us  [winding(): return lax.ppermute(value, ('md', 'cd'), pairs)]
    pallas_call x1, Pallas kernels: 8.05 us -> 6.6 us  [local(): pl.pallas_call(functools.partial(second_kernel, 'md'), out_shape=[shape_o...]
    pallas_call x1, Pallas kernels: 2.87 us -> 2.03 us  [local(): pl.pallas_call(functools.partial(first_kernel, 'md', 'cd'), out_shape=[sh...]
    unnamed x12 -> x10, local copies, waits for them, and re-layouts: 0.71 us -> 0.02 us
  transfers between devices with their start and end apart: 10 -> 10, of which waited for: 4 -> 4; matrix products, arithmetic and copies ran while one was open for 0% -> 0% of each run, Pallas kernels for 27% -> 34%
where the time goes in v4:
time: 53.8 us; the launch traced here: 53.7 us
  Pallas kernels  26.4 us (49%)
  starting transfers between devices  19.9 us (37%)
  waiting for transfers between devices  6.01 us (11%)
  between operations  0.72 us (1%)
  other arithmetic  0.6 us (1%)
    ppermute x4, starting transfers between devices, ring(): lax.ppermute(value, axis, [(i, (i + steps) % count) for i in range(count)])  10.3 us
    ppermute x6, starting transfers between devices, winding(): return lax.ppermute(value, ('md', 'cd'), pairs)  9.66 us
    pallas_call x1, Pallas kernels, local(): pl.pallas_call(advance_kernel, out_shape=[shape_of(5, *padded), shape_of(...  7.64 us
    pallas_call x1, Pallas kernels, local(): pl.pallas_call(functools.partial(second_kernel, 'md'), out_shape=[shape_o...  6.6 us
    ppermute x6, waiting for transfers between devices, winding(): return lax.ppermute(value, ('md', 'cd'), pairs)  5.8 us
    pallas_call x1, Pallas kernels, local(): pl.pallas_call(functools.partial(pack_kernel, 'cd'), in_specs=[hbm] * 6,...  3.47 us
    pallas_call x1, Pallas kernels, local(): pl.pallas_call(functools.partial(fourth_kernel, 'cd'), out_shape=shape_of...  2.24 us
    pallas_call x1, Pallas kernels, local(): pl.pallas_call(functools.partial(edge_kernel, 'cd'), out_shape=[shape_of(...  2.14 us
  transfers between devices with their start and end apart: 10, of which 4 were waited for; matrix products, arithmetic and copies ran while one was open for 0% of the time, Pallas kernels for 34%

profile of v4, /device:TPU:105, one launch (start us, length us, event | category | flops | bytes accessed | tf_op | source)
XLA Modules:
  0.0 53.7 jit_solution(5994325659013302094)
XLA Ops:
  0.6 0.0 copy-start.4
  0.6 3.5 %shard_map.112 = (f32[23,16,128]{2,1,0:T(8,128)S(1)}, f32[13,16,128]{2,1,0:T(8,128)S(1)}, f32[13,16,128]{2,1,0:T(8,128)S(1)}, f32[5,18,2,32,128]{4,3,2,1,0:T(8,1...) custom-call(f32[5,16,16,256]{3,2,1,0:T(8,128)} %s0.1, ...), custom_call_target="tpu_custom_call" | custom-call | flops 4000000 | bytes 12000000 | tf_op jit(solution)/shard_map/pallas_call | solution.py:1154
  4.1 3.4 %collective-permute-start = (f32[13,16,128]{2,1,0:T(8,128)S(1)}, f32[13,16,128]{2,1,0:T(8,128)S(1)}, u32[]{:S(2)}, u32[]{:S(2)}) collective-permute-start(f32[13,16,128]{2,1,0:T(8,128)S(1)} %get-tuple-element.44), channel_id=1, source_target_pairs={{0,8},{8,16},{16,24},{24,32},{32,40},{40,48},{48,56},{56,64},{64,7... | collective-permute-start | bytes 319496 | tf_op jit(solution)/shard_map/ppermute | solution.py:1116
  7.5 0.0 collective-permute-start.1
  7.5 0.0 copy-done.4
  7.5 1.3 %collective-permute-start.2 = (f32[16,128]{1,0:T(8,128)S(1)}, f32[16,128]{1,0:T(8,128)S(1)}, u32[]{:S(2)}, u32[]{:S(2)}) collective-permute-start(f32[16,128]{1,0:T(8,128)S(1)} %bitcast.21), channel_id=1, source_target_pairs={{0,16},{8,24},{16,32},{24,40},{32,48},{40,56},{48,64},{56,72},{64,... | collective-permute-start | bytes 24584 | tf_op jit(solution)/shard_map/ppermute | solution.py:1116
  8.8 0.2 collective-permute-start.3
  9.0 0.0 copy-start.1
  9.0 0.0 copy-start.2
  9.0 0.0 copy-start.3
  9.0 1.9 %shard_map.113.s1.s1_in = f32[5,18,2,32,128]{4,3,2,1,0:T(8,128)S(1)} custom-call(f32[5,18,2,32,128]{4,3,2,1,0:T(8,128)S(1)} %get-tuple-element.39.field, f32[11,18,2,16,128]{4,3,2,1,0:T(8,128)S(1)} %get-tuple-element.40.coef, f32[18,2,16,128]{3,2,1,0:T(8,128)S(1)} %get-tuple-element.41.base.base_in, f32[18,2,32,128]{3,2,1,0:T(8,128)S(1)} %get-tuple-element.42.uy), custom_call_target="tpu_custom_call" | custom-call | flops 2000000 | bytes 6000000 | tf_op jit(solution)/shard_map/pallas_call | solution.py:1183
  10.9 0.0 collective-permute-done.2.far_first
  10.9 2.6 %collective-permute-done.3.far_second = f32[16,128]{1,0:T(8,128)S(1)} collective-permute-done((f32[16,128]{1,0:T(8,128)S(1)}, f32[16,128]{1,0:T(8,128)S(1)}, u32[]{:S(2)}, u32[]{:S(2)}) %collective-permute-start.3) | collective-permute-done | bytes 8224 | tf_op jit(solution)/shard_map/ppermute | solution.py:1116
  13.5 0.0 collective-permute-done.near_first
  13.5 0.4 collective-permute-done.1.near_second
  13.8 0.0 copy-done.1
  13.8 0.0 copy-done.2
  13.8 0.0 copy-done.3
  13.8 0.0 copy-start
  13.8 2.0 %shard_map.114 = (f32[18,2,16,128]{3,2,1,0:T(8,128)S(1)}, f32[5,2,32,128]{3,2,1,0:T(8,128)S(1)}, f32[11,2,16,128]{3,2,1,0:T(8,128)S(1)}, f32[2,16,128]{2,1,0:T(8...) custom-call(f32[23,16,128]{2,1,0:T(8,128)S(1)} %get-tuple-element.43, ...), custom_call_target="tpu_custom_call" | custom-call | flops 3000000 | bytes 9000000 | tf_op jit(solution)/shard_map/pallas_call | solution.py:1191
  15.9 1.8 %collective-permute-start.4 = (f32[376,128]{1,0:T(8,128)S(1)}, f32[376,128]{1,0:T(8,128)S(1)}, u32[]{:S(2)}, u32[]{:S(2)}) collective-permute-start(f32[376,128]{1,0:T(8,128)S(1)} %get-tuple-element.59.own_up), channel_id=1, source_target_pairs={{0,1},{1,2},{2,3},{3,4},{4,5},{5,6},{6,7},{7,0},{8,9},{9,10},{10,1... | collective-permute-start | bytes 577544 | tf_op jit(solution)/shard_map/ppermute | solution.py:1103
  17.7 3.3 %collective-permute-start.5 = (f32[376,128]{1,0:T(8,128)S(1)}, f32[376,128]{1,0:T(8,128)S(1)}, u32[]{:S(2)}, u32[]{:S(2)}) collective-permute-start(f32[376,128]{1,0:T(8,128)S(1)} %get-tuple-element.60.own_down), channel_id=1, source_target_pairs={{0,7},{1,0},{2,1},{3,2},{4,3},{5,4},{6,5},{7,6},{8,15},{9,8},{10,9... | collective-permute-start | bytes 577544 | tf_op jit(solution)/shard_map/ppermute | solution.py:1103
  21.0 0.0 copy-done
  21.0 7.6 %shard_map.115 = (f32[5,18,2,32,128]{4,3,2,1,0:T(8,128)S(1)}, f32[18,2,16,128]{3,2,1,0:T(8,128)S(1)}, f32[5,18,2,16,128]{4,3,2,1,0:T(8,128)S(1)}, f32[5,18,2,16,...) custom-call(f32[5,18,2,32,128]{4,3,2,1,0:T(8,128)S(1)} %shard_map.113.s1.s1_in, ...), custom_call_target="tpu_custom_call" | custom-call | flops 8000000 | bytes 24000000 | tf_op jit(solution)/shard_map/pallas_call | solution.py:1216
  28.7 0.0 collective-permute-done.4.from_below.weights_below
  28.7 0.2 collective-permute-done.5.from_above.weights_above
  28.9 2.1 %shard_map.116 = (f32[5,4,2,16,128]{4,3,2,1,0:T(8,128)S(1)}, f32[5,4,2,16,128]{4,3,2,1,0:T(8,128)S(1)}, f32[5,2,2,16,128]{4,3,2,1,0:T(8,128)S(1)}, f32[4,2,16,12...) custom-call(f32[5,18,2,32,128]{4,3,2,1,0:T(8,128)S(1)} %get-tuple-el, ...), custom_call_target="tpu_custom_call" | custom-call | flops 2000000 | bytes 6000000 | tf_op jit(solution)/shard_map/pallas_call | solution.py:1246
  31.0 0.1 collective-permute-start.6
  31.1 5.1 %collective-permute-start.7 = (f32[344,128]{1,0:T(8,128)S(1)}, f32[344,128]{1,0:T(8,128)S(1)}, u32[]{:S(2)}, u32[]{:S(2)}) collective-permute-start(f32[344,128]{1,0:T(8,128)S(1)} %get-tuple-element.70.own_down), channel_id=1, source_target_pairs={{0,7},{1,0},{2,1},{3,2},{4,3},{5,4},{6,5},{7,6},{8,15},{9,8},{10,9... | collective-permute-start | bytes 528392 | tf_op jit(solution)/shard_map/ppermute | solution.py:1103
  36.2 6.6 %shard_map.117 = (f32[5,16,16,256]{3,2,1,0:T(8,128)}, f32[5,18,2,16,128]{4,3,2,1,0:T(8,128)S(1)}, f32[16,384]{1,0:T(8,128)S(1)}) custom-call(f32[5,18,2,32,128]{4,3,2,1,0:T(8,128)S(1)} %get-tuple-element.53.s1, f32[5,18,2,16,128]{4,3,2,1,0:T(8,128)S(1)} %get-tuple-element.54.s2_in, f32[5,18,2,16,128]{4,3,2,1,0:T(8,128)S(1)} %get-tuple-element.55.goal, ...), custom_call_target="tpu_custom_call" | custom-call | flops 6000000 | bytes 18000000 | tf_op jit(solution)/shard_map/pallas_call | solution.py:1282
  42.8 0.0 collective-permute-done.6.from_below
  42.8 0.0 collective-permute-done.7.from_above
  42.8 0.4 shard_map.119
  43.2 4.7 %collective-permute-start.8 = (f32[16,128]{1,0:T(8,128)S(1)}, f32[16,128]{1,0:T(8,128)S(1)}, u32[]{:S(2)}, u32[]{:S(2)}) collective-permute-start(f32[16,128]{1,0:T(8,128)S(1)} %get-tuple-element.73), channel_id=1, source_target_pairs={{0,8},{8,16},{16,24},{24,32},{32,40},{40,48},{48,56},{56,64},{64,7... | collective-permute-start | bytes 24584 | tf_op jit(solution)/shard_map/ppermute | solution.py:1116
  47.9 0.1 collective-permute-start.9
  48.0 2.2 %shard_map.118 = f32[5,16,16,256]{3,2,1,0:T(8,128)} custom-call(f32[5,18,2,16,128]{4,3,2,1,0:T(8,128)S(1)} %get-tuple-element.68.adj0_in, f32[5,18,2,32,128]{4,3,2,1,0:T(8,128)S(1)} %get-tuple-element.39.field, f32[11,18,2,16,128]{4,3,2,1,0:T(8,128)S(1)} %get-tuple-element.40.coef, f32[18,2,16,128]{3,2,1,0:T(8,128)S(1)} %get-tuple-element.58.base, ...), custom_call_target="tpu_custom_call" | custom-call | flops 2000000 | bytes 6000000 | tf_op jit(solution)/shard_map/pallas_call | solution.py:1327
  50.2 0.0 collective-permute-done.8
  50.2 2.9 %collective-permute-done.9 = f32[16,128]{1,0:T(8,128)S(1)} collective-permute-done((f32[16,128]{1,0:T(8,128)S(1)}, f32[16,128]{1,0:T(8,128)S(1)}, u32[]{:S(2)}, u32[]{:S(2)}) %collective-permute-start.9) | collective-permute-done | bytes 8224 | tf_op jit(solution)/shard_map/ppermute | solution.py:1116
  53.1 0.6 %add_bitcast_fusion = f32[128,1,16]{0,2,1:T(8,128)} fusion(f32[16,128]{1,0:T(8,128)S(1)} %collective-permute-done.9, f32[16,128]{1,0:T(8,128)S(1)} %get-tuple-element.72, f32[16,128]{1,0:T(8,128)S(1)} %collective-permute-done.8), kind=kLoop, calls=%fused_computation | loop fusion | flops 4096 | bytes 32768 | tf_op jit(solution)/shard_map/broadcast_in_dim | solution.py:1348
Async XLA Ops:
  0.6 6.9 %copy-start.4 = (f32[128,1,16]{0,2,1:T(8,128)S(1)}, f32[128,1,16]{0,2,1:T(8,128)}, u32[]{:S(2)}) copy-start(f32[128,1,16]{0,2,1:T(8,128)} %param.14) | copy-start | bytes 24580
  4.1 9.3 %collective-permute-start = (f32[13,16,128]{2,1,0:T(8,128)S(1)}, f32[13,16,128]{2,1,0:T(8,128)S(1)}, u32[]{:S(2)}, u32[]{:S(2)}) collective-permute-start(f32[13,16,128]{2,1,0:T(8,128)S(1)} %get-tuple-element.44), channel_id=1, source_target_pairs={{0,8},{8,16},{16,24},{24,32},{32,40},{40,48},{48,56},{56,64},{64,7... | collective-permute-start | bytes 319496 | tf_op jit(solution)/shard_map/ppermute | solution.py:1116
  7.5 6.3 %collective-permute-start.1 = (f32[13,16,128]{2,1,0:T(8,128)S(1)}, f32[13,16,128]{2,1,0:T(8,128)S(1)}, u32[]{:S(2)}, u32[]{:S(2)}) collective-permute-start(f32[13,16,128]{2,1,0:T(8,128)S(1)} %get-tuple-element.45), channel_id=1, source_target_pairs={{0,1},{8,0},{16,8},{24,16},{32,24},{40,32},{48,40},{56,48},{64,56}... | collective-permute-start | bytes 319496 | tf_op jit(solution)/shard_map/ppermute | solution.py:1116
  7.5 3.4 %collective-permute-start.2 = (f32[16,128]{1,0:T(8,128)S(1)}, f32[16,128]{1,0:T(8,128)S(1)}, u32[]{:S(2)}, u32[]{:S(2)}) collective-permute-start(f32[16,128]{1,0:T(8,128)S(1)} %bitcast.21), channel_id=1, source_target_pairs={{0,16},{8,24},{16,32},{24,40},{32,48},{40,56},{48,64},{56,72},{64,... | collective-permute-start | bytes 24584 | tf_op jit(solution)/shard_map/ppermute | solution.py:1116
  8.8 4.7 %collective-permute-start.3 = (f32[16,128]{1,0:T(8,128)S(1)}, f32[16,128]{1,0:T(8,128)S(1)}, u32[]{:S(2)}, u32[]{:S(2)}) collective-permute-start(f32[16,128]{1,0:T(8,128)S(1)} %bitcast.22), channel_id=1, source_target_pairs={{0,1},{8,9},{16,0},{24,8},{32,16},{40,24},{48,32},{56,40},{64,48},... | collective-permute-start | bytes 24584 | tf_op jit(solution)/shard_map/ppermute | solution.py:1116
  9.0 4.9 %copy-start.1 = (s32[4096,1]{0,1:T(1,128)S(1)}, s32[4096,1]{0,1:T(1,128)}, u32[]{:S(2)}) copy-start(s32[4096,1]{0,1:T(1,128)} %param.15) | copy-start | bytes 49156
  9.0 4.9 %copy-start.2 = (s32[4096,1]{0,1:T(1,128)S(1)}, s32[4096,1]{0,1:T(1,128)}, u32[]{:S(2)}) copy-start(s32[4096,1]{0,1:T(1,128)} %param.16) | copy-start | bytes 49156
  9.0 4.9 %copy-start.3 = (s32[4096,1]{0,1:T(1,128)S(1)}, s32[4096,1]{0,1:T(1,128)}, u32[]{:S(2)}) copy-start(s32[4096,1]{0,1:T(1,128)} %param.17) | copy-start | bytes 49156
  13.8 7.2 %copy-start = (f32[5,16,16,256]{3,2,1,0:T(8,128)S(1)}, f32[5,16,16,256]{3,2,1,0:T(8,128)}, u32[]{:S(2)}) copy-start(f32[5,16,16,256]{3,2,1,0:T(8,128)} %tgt.3) | copy-start | bytes 3932164
  15.9 12.8 %collective-permute-start.4 = (f32[376,128]{1,0:T(8,128)S(1)}, f32[376,128]{1,0:T(8,128)S(1)}, u32[]{:S(2)}, u32[]{:S(2)}) collective-permute-start(f32[376,128]{1,0:T(8,128)S(1)} %get-tuple-element.59.own_up), channel_id=1, source_target_pairs={{0,1},{1,2},{2,3},{3,4},{4,5},{5,6},{6,7},{7,0},{8,9},{9,10},{10,1... | collective-permute-start | bytes 577544 | tf_op jit(solution)/shard_map/ppermute | solution.py:1103
  17.7 11.2 %collective-permute-start.5 = (f32[376,128]{1,0:T(8,128)S(1)}, f32[376,128]{1,0:T(8,128)S(1)}, u32[]{:S(2)}, u32[]{:S(2)}) collective-permute-start(f32[376,128]{1,0:T(8,128)S(1)} %get-tuple-element.60.own_down), channel_id=1, source_target_pairs={{0,7},{1,0},{2,1},{3,2},{4,3},{5,4},{6,5},{7,6},{8,15},{9,8},{10,9... | collective-permute-start | bytes 577544 | tf_op jit(solution)/shard_map/ppermute | solution.py:1103
  31.0 11.8 %collective-permute-start.6 = (f32[344,128]{1,0:T(8,128)S(1)}, f32[344,128]{1,0:T(8,128)S(1)}, u32[]{:S(2)}, u32[]{:S(2)}) collective-permute-start(f32[344,128]{1,0:T(8,128)S(1)} %get-tuple-element.69.own_up), channel_id=1, source_target_pairs={{0,1},{1,2},{2,3},{3,4},{4,5},{5,6},{6,7},{7,0},{8,9},{9,10},{10,1... | collective-permute-start | bytes 528392 | tf_op jit(solution)/shard_map/ppermute | solution.py:1103
  31.1 11.7 %collective-permute-start.7 = (f32[344,128]{1,0:T(8,128)S(1)}, f32[344,128]{1,0:T(8,128)S(1)}, u32[]{:S(2)}, u32[]{:S(2)}) collective-permute-start(f32[344,128]{1,0:T(8,128)S(1)} %get-tuple-element.70.own_down), channel_id=1, source_target_pairs={{0,7},{1,0},{2,1},{3,2},{4,3},{5,4},{6,5},{7,6},{8,15},{9,8},{10,9... | collective-permute-start | bytes 528392 | tf_op jit(solution)/shard_map/ppermute | solution.py:1103
  43.2 7.1 %collective-permute-start.8 = (f32[16,128]{1,0:T(8,128)S(1)}, f32[16,128]{1,0:T(8,128)S(1)}, u32[]{:S(2)}, u32[]{:S(2)}) collective-permute-start(f32[16,128]{1,0:T(8,128)S(1)} %get-tuple-element.73), channel_id=1, source_target_pairs={{0,8},{8,16},{16,24},{24,32},{32,40},{40,48},{48,56},{56,64},{64,7... | collective-permute-start | bytes 24584 | tf_op jit(solution)/shard_map/ppermute | solution.py:1116
  47.9 5.2 %collective-permute-start.9 = (f32[16,128]{1,0:T(8,128)S(1)}, f32[16,128]{1,0:T(8,128)S(1)}, u32[]{:S(2)}, u32[]{:S(2)}) collective-permute-start(f32[16,128]{1,0:T(8,128)S(1)} %get-tuple-element.74), channel_id=1, source_target_pairs={{0,1},{8,0},{16,8},{24,16},{32,24},{40,32},{48,40},{56,48},{64,56}... | collective-permute-start | bytes 24584 | tf_op jit(solution)/shard_map/ppermute | solution.py:1116

commit v5 on v4

--- a/solution.py
+++ b/solution.py
@@ -375,7 +375,7 @@
                 s1[c, z + 1, tile, OWN] = out[c]
         return carry
 
-    lax.fori_loop(0, layers, advance, 0)
+    lax.fori_loop(0, layers, advance, 0, unroll=2)
 
 
 def split_three(value):
@@ -400,8 +400,7 @@
     needle,
     near_first,
     near_second,
-    far_first,
-    far_second,
+    far,
     start,
     end,
     column,
@@ -439,17 +438,14 @@
     def half(take, c, turn):
         return take(c) if c < PAIRS else pltpu.roll(take(c - PAIRS), turn, 1)
 
-    near = lane_iota((1, LANES)) < LANES // 2
-
     def feet(ref):
-        far = jnp.where(near, feet_block(ref, md + 2, count), feet_block(ref, md - 2, count))
-        blocks = [feet_block(ref, md + d, count) for d in (-1, 0, 1)]
-        return jnp.concatenate(blocks + [far], axis=1)
+        return jnp.concatenate(
+            [feet_block(ref, md + d, count) for d in (-1, 0, 1, 2)], axis=1
+        )
 
     starts, ends, columns = feet(start), feet(end), feet(column)
-    far = jnp.where((lane < LANES // 2) == odd, far_first[...], far_second[...])
     rates = jnp.concatenate(
-        [from_left(PAIRS), needle[...], from_right(PAIRS), far], axis=1
+        [from_left(PAIRS), needle[...], from_right(PAIRS), far[...]], axis=1
     )
     needles = rates.shape[1]
     picked = jnp.where(row_iota((height, needles)) == columns, 1.0, 0.0)
@@ -616,7 +612,7 @@
                 )
         return carry
 
-    lax.fori_loop(0, layers, mend, 0)
+    lax.fori_loop(0, layers, mend, 0, unroll=2)
 
     def advance(z, carry):
         for tile in range(2):
@@ -636,7 +632,7 @@
             dots[at] = total
         return carry
 
-    lax.fori_loop(0, layers, advance, 0)
+    lax.fori_loop(0, layers, advance, 0, unroll=2)
     edge_x = merged(strip_coef, UX, slice(None))
 
     def retreat(z, carry):
@@ -650,7 +646,7 @@
                 adj1[c, z + 1, tile] = out[c]
         return carry
 
-    lax.fori_loop(0, layers, retreat, 0)
+    lax.fori_loop(0, layers, retreat, 0, unroll=2)
 
 
 def edge_kernel(
@@ -886,7 +882,7 @@
                 adj1[c, z + 1, tile, OWN] = adj1_in[c, z + 1, tile]
         return carry
 
-    lax.fori_loop(0, layers, gather, 0)
+    lax.fori_loop(0, layers, gather, 0, unroll=2)
     for tile in range(2):
         for number, row in enumerate((0, 1, 15, 14)):
             set_row(dots, 0, tile, row, dots_edge[number, tile])
@@ -945,7 +941,7 @@
                 s2_out[c, z, :, span(tile)] = s2[c, z + 1, tile]
         return carry
 
-    lax.fori_loop(0, layers, write, 0)
+    lax.fori_loop(0, layers, write, 0, unroll=2)
     edge_x = merged(strip_coef, UX, slice(None))
     last_delta = Field(adj1, strip_adj1, joint)
     last_delta.clear()
@@ -965,7 +961,7 @@
             sens[z, :, span(tile)] = -DT * total
         return carry
 
-    lax.fori_loop(0, layers, finish, 0)
+    lax.fori_loop(0, layers, finish, 0, unroll=2)
     starts, ends, columns = (needle_feet(ref, md, count) for ref in (start, end, column))
     cover = own_cover(md, length, starts, ends)
     product = covered_sum(sens[...].reshape(layers * height, length), cover)
@@ -1043,7 +1039,7 @@
                 adj0[c, z + 1, tile] = adj0_in[c, z + 1, tile]
         return carry
 
-    lax.fori_loop(0, layers, gather, 0)
+    lax.fori_loop(0, layers, gather, 0, unroll=2)
 
     for number, (weights, message, mine, valid) in enumerate(
         (
@@ -1095,7 +1091,7 @@
                 out_field[c, z, :, span(tile)] = adj0[c, z + 1, tile]
         return carry
 
-    lax.fori_loop(0, layers, scatter, 0)
+    lax.fori_loop(0, layers, scatter, 0, unroll=2)
 
 
 def ring(value, axis, steps):
@@ -1114,10 +1110,6 @@
             else:
                 pairs.append((row * columns + column, row * columns + (column ^ 1)))
     return lax.ppermute(value, ("md", "cd"), pairs)
-
-
-def both_ways(value, steps):
-    return winding(value, steps, 0), winding(value, steps, 1)
 
 
 def shape_of(*dims, dtype=F32):
@@ -1177,7 +1169,7 @@
             for field in (orientation, velocity, velocity_grad, rotary, target, rates)
         )
     )
-    far = both_ways(rates, 2)
+    far = ring(rates, "md", -2)
     near = winding(first, 1, 0), winding(second, 1, 1)
 
     s1 = pl.pallas_call(
@@ -1208,7 +1200,7 @@
             ],
             compiler_params=params(24),
             cost_estimate=cost(3),
-        )(packed, rates, *near, *far, *feet, field, coef, uy, s1)
+        )(packed, rates, *near, far, *feet, field, coef, uy, s1)
     )
     below = ring(up, "cd", 1)
     above = ring(down, "cd", -1)

time: 53.8 us -> 52.4 us (0.974)
  the two profiles are of different devices: /device:TPU:105 before, /device:TPU:16 now
where the time goes in v5:
time: 52.4 us; the launch traced here: 52.3 us
  Pallas kernels  24.4 us (47%)
  starting transfers between devices  18.8 us (36%)
  waiting for transfers between devices  7.87 us (15%)
  between operations  0.74 us (1%)
  other arithmetic  0.6 us (1%)
    ppermute x5, starting transfers between devices, ring(): lax.ppermute(value, axis, [(i, (i + steps) % count) for i in range(count)])  12.9 us
    pallas_call x1, Pallas kernels, local(): pl.pallas_call(advance_kernel, out_shape=[shape_of(5, *padded), shape_of(...  6.37 us
    pallas_call x1, Pallas kernels, local(): pl.pallas_call(functools.partial(second_kernel, 'md'), out_shape=[shape_o...  6.22 us
    ppermute x4, starting transfers between devices, winding(): return lax.ppermute(value, ('md', 'cd'), pairs)  5.84 us
    ppermute x5, waiting for transfers between devices, ring(): lax.ppermute(value, axis, [(i, (i + steps) % count) for i in range(count)])  4.91 us
    pallas_call x1, Pallas kernels, local(): pl.pallas_call(functools.partial(pack_kernel, 'cd'), in_specs=[hbm] * 6,...  3.47 us
    ppermute x4, waiting for transfers between devices, winding(): return lax.ppermute(value, ('md', 'cd'), pairs)  2.96 us
    pallas_call x1, Pallas kernels, local(): pl.pallas_call(functools.partial(fourth_kernel, 'cd'), out_shape=shape_of...  2.2 us
  transfers between devices with their start and end apart: 9, of which 4 were waited for; matrix products, arithmetic and copies ran while one was open for 0% of the time, Pallas kernels for 31%

profile of v5, /device:TPU:16, one launch (start us, length us, event | category | flops | bytes accessed | tf_op | source)
XLA Modules:
  0.0 52.3 jit_solution(13180060225526866513)
XLA Ops:
  0.6 0.0 copy-start.4
  0.6 3.5 %shard_map.112 = (f32[23,16,128]{2,1,0:T(8,128)S(1)}, f32[13,16,128]{2,1,0:T(8,128)S(1)}, f32[13,16,128]{2,1,0:T(8,128)S(1)}, f32[5,18,2,32,128]{4,3,2,1,0:T(8,1...) custom-call(f32[5,16,16,256]{3,2,1,0:T(8,128)} %s0.1, ...), custom_call_target="tpu_custom_call" | custom-call | flops 4000000 | bytes 12000000 | tf_op jit(solution)/shard_map/pallas_call | solution.py:1146
  4.1 2.2 %collective-permute-start = (f32[13,16,128]{2,1,0:T(8,128)S(1)}, f32[13,16,128]{2,1,0:T(8,128)S(1)}, u32[]{:S(2)}, u32[]{:S(2)}) collective-permute-start(f32[13,16,128]{2,1,0:T(8,128)S(1)} %get-tuple-element.44), channel_id=1, source_target_pairs={{0,8},{8,16},{16,24},{24,32},{32,40},{40,48},{48,56},{56,64},{64,7... | collective-permute-start | bytes 319496 | tf_op jit(solution)/shard_map/ppermute | solution.py:1112
  6.3 0.0 collective-permute-start.1
  6.3 0.0 copy-done.4
  6.3 5.0 %collective-permute-start.2 = (f32[16,128]{1,0:T(8,128)S(1)}, f32[16,128]{1,0:T(8,128)S(1)}, u32[]{:S(2)}, u32[]{:S(2)}) collective-permute-start(f32[16,128]{1,0:T(8,128)S(1)} %bitcast.21), channel_id=1, source_target_pairs={{0,240},{8,248},{16,0},{24,8},{32,16},{40,24},{48,32},{56,40},{64,... | collective-permute-start | bytes 24584 | tf_op jit(solution)/shard_map/ppermute | solution.py:1099
  11.3 0.0 copy-start.1
  11.3 0.0 copy-start.2
  11.3 0.0 copy-start.3
  11.3 1.5 %shard_map.113.s1.s1_in = f32[5,18,2,32,128]{4,3,2,1,0:T(8,128)S(1)} custom-call(f32[5,18,2,32,128]{4,3,2,1,0:T(8,128)S(1)} %get-tuple-element.39.field, f32[11,18,2,16,128]{4,3,2,1,0:T(8,128)S(1)} %get-tuple-element.40.coef, f32[18,2,16,128]{3,2,1,0:T(8,128)S(1)} %get-tuple-element.41.base.base_in, f32[18,2,32,128]{3,2,1,0:T(8,128)S(1)} %get-tuple-element.42.uy), custom_call_target="tpu_custom_call" | custom-call | flops 2000000 | bytes 6000000 | tf_op jit(solution)/shard_map/pallas_call | solution.py:1175
  12.8 0.0 collective-permute-done.2.far
  12.8 0.0 collective-permute-done.near_first
  12.8 0.0 collective-permute-done.1.near_second
  12.9 0.0 copy-done.1
  12.9 0.0 copy-done.2
  12.9 0.0 copy-done.3
  12.9 0.0 copy-start
  12.9 2.0 %shard_map.114 = (f32[18,2,16,128]{3,2,1,0:T(8,128)S(1)}, f32[5,2,32,128]{3,2,1,0:T(8,128)S(1)}, f32[11,2,16,128]{3,2,1,0:T(8,128)S(1)}, f32[2,16,128]{2,1,0:T(8...) custom-call(f32[23,16,128]{2,1,0:T(8,128)S(1)} %get-tuple-element.43, ...), custom_call_target="tpu_custom_call" | custom-call | flops 3000000 | bytes 9000000 | tf_op jit(solution)/shard_map/pallas_call | solution.py:1183
  14.9 2.8 %collective-permute-start.3 = (f32[376,128]{1,0:T(8,128)S(1)}, f32[376,128]{1,0:T(8,128)S(1)}, u32[]{:S(2)}, u32[]{:S(2)}) collective-permute-start(f32[376,128]{1,0:T(8,128)S(1)} %get-tuple-element.59.own_up), channel_id=1, source_target_pairs={{0,1},{1,2},{2,3},{3,4},{4,5},{5,6},{6,7},{7,0},{8,9},{9,10},{10,1... | collective-permute-start | bytes 577544 | tf_op jit(solution)/shard_map/ppermute | solution.py:1099
  17.8 0.7 %collective-permute-start.4 = (f32[376,128]{1,0:T(8,128)S(1)}, f32[376,128]{1,0:T(8,128)S(1)}, u32[]{:S(2)}, u32[]{:S(2)}) collective-permute-start(f32[376,128]{1,0:T(8,128)S(1)} %get-tuple-element.60.own_down), channel_id=1, source_target_pairs={{0,7},{1,0},{2,1},{3,2},{4,3},{5,4},{6,5},{7,6},{8,15},{9,8},{10,9... | collective-permute-start | bytes 577544 | tf_op jit(solution)/shard_map/ppermute | solution.py:1099
  18.5 0.0 copy-done
  18.5 6.4 %shard_map.115 = (f32[5,18,2,32,128]{4,3,2,1,0:T(8,128)S(1)}, f32[18,2,16,128]{3,2,1,0:T(8,128)S(1)}, f32[5,18,2,16,128]{4,3,2,1,0:T(8,128)S(1)}, f32[5,18,2,16,...) custom-call(f32[5,18,2,32,128]{4,3,2,1,0:T(8,128)S(1)} %shard_map.113.s1.s1_in, ...), custom_call_target="tpu_custom_call" | custom-call | flops 8000000 | bytes 24000000 | tf_op jit(solution)/shard_map/pallas_call | solution.py:1208
  24.9 2.4 %collective-permute-done.3.from_below.weights_below = f32[376,128]{1,0:T(8,128)S(1)} collective-permute-done((f32[376,128]{1,0:T(8,128)S(1)}, f32[376,128]{1,0:T(8,128)S(1)}, u32[]{:S(2)}, u32[]{:S(2)}) %collective-permute-start.3) | collective-permute-done | bytes 192544 | tf_op jit(solution)/shard_map/ppermute | solution.py:1099
  27.2 0.5 collective-permute-done.4.from_above.weights_above
  27.8 2.1 %shard_map.116 = (f32[5,4,2,16,128]{4,3,2,1,0:T(8,128)S(1)}, f32[5,4,2,16,128]{4,3,2,1,0:T(8,128)S(1)}, f32[5,2,2,16,128]{4,3,2,1,0:T(8,128)S(1)}, f32[4,2,16,12...) custom-call(f32[5,18,2,32,128]{4,3,2,1,0:T(8,128)S(1)} %get-tuple-el, ...), custom_call_target="tpu_custom_call" | custom-call | flops 2000000 | bytes 6000000 | tf_op jit(solution)/shard_map/pallas_call | solution.py:1238
  29.9 3.1 %collective-permute-start.5 = (f32[344,128]{1,0:T(8,128)S(1)}, f32[344,128]{1,0:T(8,128)S(1)}, u32[]{:S(2)}, u32[]{:S(2)}) collective-permute-start(f32[344,128]{1,0:T(8,128)S(1)} %get-tuple-element.69.own_up), channel_id=1, source_target_pairs={{0,1},{1,2},{2,3},{3,4},{4,5},{5,6},{6,7},{7,0},{8,9},{9,10},{10,1... | collective-permute-start | bytes 528392 | tf_op jit(solution)/shard_map/ppermute | solution.py:1099
  33.0 1.2 %collective-permute-start.6 = (f32[344,128]{1,0:T(8,128)S(1)}, f32[344,128]{1,0:T(8,128)S(1)}, u32[]{:S(2)}, u32[]{:S(2)}) collective-permute-start(f32[344,128]{1,0:T(8,128)S(1)} %get-tuple-element.70.own_down), channel_id=1, source_target_pairs={{0,7},{1,0},{2,1},{3,2},{4,3},{5,4},{6,5},{7,6},{8,15},{9,8},{10,9... | collective-permute-start | bytes 528392 | tf_op jit(solution)/shard_map/ppermute | solution.py:1099
  34.2 6.2 %shard_map.117 = (f32[5,16,16,256]{3,2,1,0:T(8,128)}, f32[5,18,2,16,128]{4,3,2,1,0:T(8,128)S(1)}, f32[16,384]{1,0:T(8,128)S(1)}) custom-call(f32[5,18,2,32,128]{4,3,2,1,0:T(8,128)S(1)} %get-tuple-element.53.s1, f32[5,18,2,16,128]{4,3,2,1,0:T(8,128)S(1)} %get-tuple-element.54.s2_in, f32[5,18,2,16,128]{4,3,2,1,0:T(8,128)S(1)} %get-tuple-element.55.goal, ...), custom_call_target="tpu_custom_call" | custom-call | flops 6000000 | bytes 18000000 | tf_op jit(solution)/shard_map/pallas_call | solution.py:1274
  40.5 2.0 %collective-permute-done.5.from_below = f32[344,128]{1,0:T(8,128)S(1)} collective-permute-done((f32[344,128]{1,0:T(8,128)S(1)}, f32[344,128]{1,0:T(8,128)S(1)}, u32[]{:S(2)}, u32[]{:S(2)}) %collective-permute-start.5) | collective-permute-done | bytes 176160 | tf_op jit(solution)/shard_map/ppermute | solution.py:1099
  42.5 0.0 collective-permute-done.6.from_above
  42.5 0.4 shard_map.119
  42.9 3.7 %collective-permute-start.7 = (f32[16,128]{1,0:T(8,128)S(1)}, f32[16,128]{1,0:T(8,128)S(1)}, u32[]{:S(2)}, u32[]{:S(2)}) collective-permute-start(f32[16,128]{1,0:T(8,128)S(1)} %get-tuple-element.73), channel_id=1, source_target_pairs={{0,8},{8,16},{16,24},{24,32},{32,40},{40,48},{48,56},{56,64},{64,7... | collective-permute-start | bytes 24584 | tf_op jit(solution)/shard_map/ppermute | solution.py:1112
  46.6 0.0 collective-permute-start.8
  46.6 2.2 %shard_map.118 = f32[5,16,16,256]{3,2,1,0:T(8,128)} custom-call(f32[5,18,2,16,128]{4,3,2,1,0:T(8,128)S(1)} %get-tuple-element.68.adj0_in, f32[5,18,2,32,128]{4,3,2,1,0:T(8,128)S(1)} %get-tuple-element.39.field, f32[11,18,2,16,128]{4,3,2,1,0:T(8,128)S(1)} %get-tuple-element.40.coef, f32[18,2,16,128]{3,2,1,0:T(8,128)S(1)} %get-tuple-element.58.base, ...), custom_call_target="tpu_custom_call" | custom-call | flops 2000000 | bytes 6000000 | tf_op jit(solution)/shard_map/pallas_call | solution.py:1319
  48.8 0.0 collective-permute-done.7
  48.8 2.9 %collective-permute-done.8 = f32[16,128]{1,0:T(8,128)S(1)} collective-permute-done((f32[16,128]{1,0:T(8,128)S(1)}, f32[16,128]{1,0:T(8,128)S(1)}, u32[]{:S(2)}, u32[]{:S(2)}) %collective-permute-start.8) | collective-permute-done | bytes 8224 | tf_op jit(solution)/shard_map/ppermute | solution.py:1112
  51.7 0.6 %add_bitcast_fusion = f32[128,1,16]{0,2,1:T(8,128)} fusion(f32[16,128]{1,0:T(8,128)S(1)} %collective-permute-done.8, f32[16,128]{1,0:T(8,128)S(1)} %get-tuple-element.72, f32[16,128]{1,0:T(8,128)S(1)} %collective-permute-done.7), kind=kLoop, calls=%fused_computation | loop fusion | flops 4096 | bytes 32768 | tf_op jit(solution)/shard_map/broadcast_in_dim | solution.py:1340
Async XLA Ops:
  0.6 5.6 %copy-start.4 = (f32[128,1,16]{0,2,1:T(8,128)S(1)}, f32[128,1,16]{0,2,1:T(8,128)}, u32[]{:S(2)}) copy-start(f32[128,1,16]{0,2,1:T(8,128)} %param.14) | copy-start | bytes 24580
  4.1 8.7 %collective-permute-start = (f32[13,16,128]{2,1,0:T(8,128)S(1)}, f32[13,16,128]{2,1,0:T(8,128)S(1)}, u32[]{:S(2)}, u32[]{:S(2)}) collective-permute-start(f32[13,16,128]{2,1,0:T(8,128)S(1)} %get-tuple-element.44), channel_id=1, source_target_pairs={{0,8},{8,16},{16,24},{24,32},{32,40},{40,48},{48,56},{56,64},{64,7... | collective-permute-start | bytes 319496 | tf_op jit(solution)/shard_map/ppermute | solution.py:1112
  6.3 6.6 %collective-permute-start.1 = (f32[13,16,128]{2,1,0:T(8,128)S(1)}, f32[13,16,128]{2,1,0:T(8,128)S(1)}, u32[]{:S(2)}, u32[]{:S(2)}) collective-permute-start(f32[13,16,128]{2,1,0:T(8,128)S(1)} %get-tuple-element.45), channel_id=1, source_target_pairs={{0,1},{8,0},{16,8},{24,16},{32,24},{40,32},{48,40},{56,48},{64,56}... | collective-permute-start | bytes 319496 | tf_op jit(solution)/shard_map/ppermute | solution.py:1112
  6.3 6.5 %collective-permute-start.2 = (f32[16,128]{1,0:T(8,128)S(1)}, f32[16,128]{1,0:T(8,128)S(1)}, u32[]{:S(2)}, u32[]{:S(2)}) collective-permute-start(f32[16,128]{1,0:T(8,128)S(1)} %bitcast.21), channel_id=1, source_target_pairs={{0,240},{8,248},{16,0},{24,8},{32,16},{40,24},{48,32},{56,40},{64,... | collective-permute-start | bytes 24584 | tf_op jit(solution)/shard_map/ppermute | solution.py:1099
  11.3 1.6 %copy-start.1 = (s32[4096,1]{0,1:T(1,128)S(1)}, s32[4096,1]{0,1:T(1,128)}, u32[]{:S(2)}) copy-start(s32[4096,1]{0,1:T(1,128)} %param.15) | copy-start | bytes 49156
  11.3 1.6 %copy-start.2 = (s32[4096,1]{0,1:T(1,128)S(1)}, s32[4096,1]{0,1:T(1,128)}, u32[]{:S(2)}) copy-start(s32[4096,1]{0,1:T(1,128)} %param.16) | copy-start | bytes 49156
  11.3 1.6 %copy-start.3 = (s32[4096,1]{0,1:T(1,128)S(1)}, s32[4096,1]{0,1:T(1,128)}, u32[]{:S(2)}) copy-start(s32[4096,1]{0,1:T(1,128)} %param.17) | copy-start | bytes 49156
  12.9 5.6 %copy-start = (f32[5,16,16,256]{3,2,1,0:T(8,128)S(1)}, f32[5,16,16,256]{3,2,1,0:T(8,128)}, u32[]{:S(2)}) copy-start(f32[5,16,16,256]{3,2,1,0:T(8,128)} %tgt.3) | copy-start | bytes 3932164
  14.9 12.3 %collective-permute-start.3 = (f32[376,128]{1,0:T(8,128)S(1)}, f32[376,128]{1,0:T(8,128)S(1)}, u32[]{:S(2)}, u32[]{:S(2)}) collective-permute-start(f32[376,128]{1,0:T(8,128)S(1)} %get-tuple-element.59.own_up), channel_id=1, source_target_pairs={{0,1},{1,2},{2,3},{3,4},{4,5},{5,6},{6,7},{7,0},{8,9},{9,10},{10,1... | collective-permute-start | bytes 577544 | tf_op jit(solution)/shard_map/ppermute | solution.py:1099
  17.8 10.0 %collective-permute-start.4 = (f32[376,128]{1,0:T(8,128)S(1)}, f32[376,128]{1,0:T(8,128)S(1)}, u32[]{:S(2)}, u32[]{:S(2)}) collective-permute-start(f32[376,128]{1,0:T(8,128)S(1)} %get-tuple-element.60.own_down), channel_id=1, source_target_pairs={{0,7},{1,0},{2,1},{3,2},{4,3},{5,4},{6,5},{7,6},{8,15},{9,8},{10,9... | collective-permute-start | bytes 577544 | tf_op jit(solution)/shard_map/ppermute | solution.py:1099
  29.9 12.6 %collective-permute-start.5 = (f32[344,128]{1,0:T(8,128)S(1)}, f32[344,128]{1,0:T(8,128)S(1)}, u32[]{:S(2)}, u32[]{:S(2)}) collective-permute-start(f32[344,128]{1,0:T(8,128)S(1)} %get-tuple-element.69.own_up), channel_id=1, source_target_pairs={{0,1},{1,2},{2,3},{3,4},{4,5},{5,6},{6,7},{7,0},{8,9},{9,10},{10,1... | collective-permute-start | bytes 528392 | tf_op jit(solution)/shard_map/ppermute | solution.py:1099
  33.0 9.5 %collective-permute-start.6 = (f32[344,128]{1,0:T(8,128)S(1)}, f32[344,128]{1,0:T(8,128)S(1)}, u32[]{:S(2)}, u32[]{:S(2)}) collective-permute-start(f32[344,128]{1,0:T(8,128)S(1)} %get-tuple-element.70.own_down), channel_id=1, source_target_pairs={{0,7},{1,0},{2,1},{3,2},{4,3},{5,4},{6,5},{7,6},{8,15},{9,8},{10,9... | collective-permute-start | bytes 528392 | tf_op jit(solution)/shard_map/ppermute | solution.py:1099
  42.9 5.9 %collective-permute-start.7 = (f32[16,128]{1,0:T(8,128)S(1)}, f32[16,128]{1,0:T(8,128)S(1)}, u32[]{:S(2)}, u32[]{:S(2)}) collective-permute-start(f32[16,128]{1,0:T(8,128)S(1)} %get-tuple-element.73), channel_id=1, source_target_pairs={{0,8},{8,16},{16,24},{24,32},{32,40},{40,48},{48,56},{56,64},{64,7... | collective-permute-start | bytes 24584 | tf_op jit(solution)/shard_map/ppermute | solution.py:1112
  46.6 5.2 %collective-permute-start.8 = (f32[16,128]{1,0:T(8,128)S(1)}, f32[16,128]{1,0:T(8,128)S(1)}, u32[]{:S(2)}, u32[]{:S(2)}) collective-permute-start(f32[16,128]{1,0:T(8,128)S(1)} %get-tuple-element.74), channel_id=1, source_target_pairs={{0,1},{8,0},{16,8},{24,16},{32,24},{40,32},{48,40},{56,48},{64,56}... | collective-permute-start | bytes 24584 | tf_op jit(solution)/shard_map/ppermute | solution.py:1112

commit v6 on v5

--- a/solution.py
+++ b/solution.py
@@ -378,6 +378,12 @@
     lax.fori_loop(0, layers, advance, 0, unroll=2)
 
 
+def choose(axis_md, low, high, first, second):
+    odd = lax.axis_index(axis_md) % 2 == 1
+    first[...] = jnp.where(odd, high[...], low[...])
+    second[...] = jnp.where(odd, low[...], high[...])
+
+
 def split_three(value):
     parts = []
     for _ in range(3):
@@ -417,6 +423,8 @@
     strip_tgt,
     up,
     down,
+    sent_first,
+    sent_second,
     spread,
     cover,
     source,
@@ -542,6 +550,7 @@
             message[planes(tile * 11 + 10, layers)] = outward
     for side in range(2):
         put(side)
+    choose(axis_md, up, down, sent_first, sent_second)
 
 
 def cd_flags(axis_cd):
@@ -650,6 +659,7 @@
 
 
 def edge_kernel(
+    axis_md,
     axis_cd,
     s1,
     strip_s1_in,
@@ -663,8 +673,8 @@
     strip_tgt,
     own_up,
     own_down,
-    from_below,
-    from_above,
+    got_first,
+    got_second,
     s2_edge,
     adj2_edge,
     adj1_edge,
@@ -673,10 +683,15 @@
     strip_adj1,
     up,
     down,
+    sent_first,
+    sent_second,
+    from_below,
+    from_above,
     strip_s1,
 ):
     layers = goal.shape[1] - 2
     has_below, has_above = cd_flags(axis_cd)
+    choose(axis_md, got_first, got_second, from_below, from_above)
 
     state, delta = Field(s1, strip_s1), Field(s1, strip_adj2)
     delta.clear_strips()
@@ -819,6 +834,7 @@
                 outgoing[planes(tile * 10 + c, layers)] = weight * b[c]
                 outgoing[planes(tile * 10 + 5 + c, layers)] = weight * out[c]
                 adj1_edge[c, number, tile] = out[c]
+    choose(axis_md, up, down, sent_first, sent_second)
 
 
 def needle_feet(ref, md, count):
@@ -977,15 +993,18 @@
     axis_cd,
     gained,
     field,
-    from_below,
-    from_above,
+    got_first,
+    got_second,
     start,
     end,
     column,
     first,
     kept,
     second,
+    from_below,
+    from_above,
 ):
+    choose(axis_md, got_first, got_second, from_below, from_above)
     layers = field.shape[1] - 2
     length = 2 * LANES
     md = lax.axis_index(axis_md)
@@ -1109,6 +1128,19 @@
                 pairs.append((row * columns + column, target * columns + column))
             else:
                 pairs.append((row * columns + column, row * columns + (column ^ 1)))
+    return lax.ppermute(value, ("md", "cd"), pairs)
+
+
+def weaving(value, turn):
+    rows, columns = lax.axis_size("md"), lax.axis_size("cd")
+    pairs = []
+    for row in range(rows):
+        for column in range(columns):
+            target = column + (1 if row % 2 == turn else -1)
+            if 0 <= target < columns:
+                pairs.append((row * columns + column, row * columns + target))
+            else:
+                pairs.append((row * columns + column, (row ^ 1) * columns + column))
     return lax.ppermute(value, ("md", "cd"), pairs)
 
 
@@ -1169,7 +1201,7 @@
             for field in (orientation, velocity, velocity_grad, rotary, target, rates)
         )
     )
-    far = ring(rates, "md", -2)
+    far = lax.ppermute(rates, "md", [(i + 2, i) for i in range(lax.axis_size("md") - 2)])
     near = winding(first, 1, 0), winding(second, 1, 1)
 
     s1 = pl.pallas_call(
@@ -1179,7 +1211,7 @@
         cost_estimate=cost(2),
     )(field, coef, base, uy)
 
-    gain, strip_s0, strip_coef, strip_base, strip_uy, strip_s1, strip_tgt, up, down = (
+    gain, strip_s0, strip_coef, strip_base, strip_uy, strip_s1, strip_tgt, up, down, *sent = (
         pl.pallas_call(
             functools.partial(first_kernel, "md", "cd"),
             out_shape=[
@@ -1190,8 +1222,7 @@
                 shape_of(*strip_padded),
                 shape_of(5, *strip_padded),
                 shape_of(5, *strip),
-                message,
-                message,
+                *[message] * 4,
             ],
             scratch_shapes=[
                 scratch(3, layers * height, 4 * LANES, dtype=jnp.bfloat16),
@@ -1202,8 +1233,7 @@
             cost_estimate=cost(3),
         )(packed, rates, *near, far, *feet, field, coef, uy, s1)
     )
-    below = ring(up, "cd", 1)
-    above = ring(down, "cd", -1)
+    got = weaving(sent[0], 0), weaving(sent[1], 1)
 
     s1, base, s2_part, goal, adj1_part, dots = pl.pallas_call(
         advance_kernel,
@@ -1234,9 +1264,9 @@
         strip_tgt,
     )
     edge_row = (2, layers, LANES)
-    s2_edge, adj2_edge, adj1_edge, dots_edge, strip_adj2, strip_adj1, back_up, back_down = (
+    s2_edge, adj2_edge, adj1_edge, dots_edge, strip_adj2, strip_adj1, back_up, back_down, *more = (
         pl.pallas_call(
-            functools.partial(edge_kernel, "cd"),
+            functools.partial(edge_kernel, "md", "cd"),
             out_shape=[
                 shape_of(5, 4, *edge_row),
                 shape_of(5, 4, *edge_row),
@@ -1244,8 +1274,9 @@
                 shape_of(4, *edge_row),
                 shape_of(5, *strip_padded),
                 shape_of(5, *strip_padded),
-                back_message,
-                back_message,
+                *[back_message] * 4,
+                message,
+                message,
             ],
             scratch_shapes=[scratch(5, *strip_padded)],
             compiler_params=params(16),
@@ -1263,12 +1294,11 @@
             strip_tgt,
             up,
             down,
-            below,
-            above,
+            *got,
         )
     )
-    back_below = ring(back_up, "cd", 1)
-    back_above = ring(back_down, "cd", -1)
+    back_sent, (below, above) = more[:2], more[2:]
+    back_got = weaving(back_sent[0], 0), weaving(back_sent[1], 1)
 
     part = shape_of(*rates.shape)
     s2, adj0_part, gained = pl.pallas_call(
@@ -1307,12 +1337,12 @@
         *feet,
     )
 
-    part_first, part_own, part_second = pl.pallas_call(
+    part_first, part_own, part_second, back_below, back_above = pl.pallas_call(
         functools.partial(third_kernel, "md", "cd"),
-        out_shape=[part, part, part],
+        out_shape=[part, part, part, back_message, back_message],
         compiler_params=params(16),
         cost_estimate=cost(1),
-    )(gained, field, back_below, back_above, *feet)
+    )(gained, field, *back_got, *feet)
     part_first = winding(part_first, 1, 0)
     part_second = winding(part_second, 1, 1)
 

time: 52.4 us -> 51.5 us (0.983)
  the two profiles are of different devices: /device:TPU:16 before, /device:TPU:107 now
where the time goes in v6:
time: 51.5 us; the launch traced here: 51.4 us
  Pallas kernels  24.5 us (48%)
  starting transfers between devices  16 us (31%)
  waiting for transfers between devices  9.58 us (19%)
  between operations  0.75 us (1%)
  other arithmetic  0.6 us (1%)
    ppermute x4, starting transfers between devices, winding(): return lax.ppermute(value, ('md', 'cd'), pairs)  7.8 us
    pallas_call x1, Pallas kernels, local(): pl.pallas_call(advance_kernel, out_shape=[shape_of(5, *padded), shape_of(...  6.37 us
    ppermute x4, starting transfers between devices, weaving(): return lax.ppermute(value, ('md', 'cd'), pairs)  6.28 us
    pallas_call x1, Pallas kernels, local(): pl.pallas_call(functools.partial(second_kernel, 'md'), out_shape=[shape_o...  6.22 us
    ppermute x4, waiting for transfers between devices, weaving(): return lax.ppermute(value, ('md', 'cd'), pairs)  3.58 us
    pallas_call x1, Pallas kernels, local(): pl.pallas_call(functools.partial(pack_kernel, 'cd'), in_specs=[hbm] * 6,...  3.47 us
    ppermute x1, waiting for transfers between devices, local(): lax.ppermute(rates, 'md', [(i + 2, i) for i in range(lax.axis_size('md')...  3.01 us
    ppermute x4, waiting for transfers between devices, winding(): return lax.ppermute(value, ('md', 'cd'), pairs)  2.99 us
  transfers between devices with their start and end apart: 9, of which 4 were waited for; matrix products, arithmetic and copies ran while one was open for 0% of the time, Pallas kernels for 32%

profile of v6, /device:TPU:107, one launch (start us, length us, event | category | flops | bytes accessed | tf_op | source)
XLA Modules:
  0.0 51.4 jit_solution(8989354132312371308)
XLA Ops:
  0.6 0.0 copy-start.4
  0.6 3.5 %shard_map.112 = (f32[23,16,128]{2,1,0:T(8,128)S(1)}, f32[13,16,128]{2,1,0:T(8,128)S(1)}, f32[13,16,128]{2,1,0:T(8,128)S(1)}, f32[5,18,2,32,128]{4,3,2,1,0:T(8,1...) custom-call(f32[5,16,16,256]{3,2,1,0:T(8,128)} %s0.1, ...), custom_call_target="tpu_custom_call" | custom-call | flops 4000000 | bytes 12000000 | tf_op jit(solution)/shard_map/pallas_call | solution.py:1178
  4.1 3.4 %collective-permute-start = (f32[13,16,128]{2,1,0:T(8,128)S(1)}, f32[13,16,128]{2,1,0:T(8,128)S(1)}, u32[]{:S(2)}, u32[]{:S(2)}) collective-permute-start(f32[13,16,128]{2,1,0:T(8,128)S(1)} %get-tuple-element.52), channel_id=1, source_target_pairs={{0,8},{8,16},{16,24},{24,32},{32,40},{40,48},{48,56},{56,64},{64,7... | collective-permute-start | bytes 319496 | tf_op jit(solution)/shard_map/ppermute | solution.py:1131
  7.5 0.0 collective-permute-start.1
  7.5 0.0 copy-done.4
  7.5 1.9 %collective-permute-start.2 = (f32[16,128]{1,0:T(8,128)S(1)}, f32[16,128]{1,0:T(8,128)S(1)}, u32[]{:S(2)}, u32[]{:S(2)}) collective-permute-start(f32[16,128]{1,0:T(8,128)S(1)} %bitcast.21), channel_id=1, source_target_pairs={{16,0},{24,8},{32,16},{40,24},{48,32},{56,40},{64,48},{72,56},{80,... | collective-permute-start | bytes 24584 | tf_op jit(solution)/shard_map/ppermute | solution.py:1204
  9.4 0.0 copy-start.1
  9.4 0.0 copy-start.2
  9.4 0.0 copy-start.3
  9.5 1.5 %shard_map.113.s1.s1_in = f32[5,18,2,32,128]{4,3,2,1,0:T(8,128)S(1)} custom-call(f32[5,18,2,32,128]{4,3,2,1,0:T(8,128)S(1)} %get-tuple-element.47.field, f32[11,18,2,16,128]{4,3,2,1,0:T(8,128)S(1)} %get-tuple-element.48.coef, f32[18,2,16,128]{3,2,1,0:T(8,128)S(1)} %get-tuple-element.49.base.base_in, f32[18,2,32,128]{3,2,1,0:T(8,128)S(1)} %get-tuple-element.50.uy), custom_call_target="tpu_custom_call" | custom-call | flops 2000000 | bytes 6000000 | tf_op jit(solution)/shard_map/pallas_call | solution.py:1207
  11.0 3.0 %collective-permute-done.2.far = f32[16,128]{1,0:T(8,128)S(1)} collective-permute-done((f32[16,128]{1,0:T(8,128)S(1)}, f32[16,128]{1,0:T(8,128)S(1)}, u32[]{:S(2)}, u32[]{:S(2)}) %collective-permute-start.2) | collective-permute-done | bytes 8224 | tf_op jit(solution)/shard_map/ppermute | solution.py:1204
  14.0 0.0 collective-permute-done.near_first
  14.0 0.0 collective-permute-done.1.near_second
  14.0 0.0 copy-done.1
  14.0 0.0 copy-done.2
  14.0 0.0 copy-done.3
  14.0 0.0 copy-start
  14.0 2.0 %shard_map.114 = (f32[18,2,16,128]{3,2,1,0:T(8,128)S(1)}, f32[5,2,32,128]{3,2,1,0:T(8,128)S(1)}, f32[11,2,16,128]{3,2,1,0:T(8,128)S(1)}, f32[2,16,128]{2,1,0:T(8...) custom-call(f32[23,16,128]{2,1,0:T(8,128)S(1)} %get-tuple-element.51, ...), custom_call_target="tpu_custom_call" | custom-call | flops 3000000 | bytes 9000000 | tf_op jit(solution)/shard_map/pallas_call | solution.py:1215
  16.1 2.6 %collective-permute-start.3 = (f32[376,128]{1,0:T(8,128)S(1)}, f32[376,128]{1,0:T(8,128)S(1)}, u32[]{:S(2)}, u32[]{:S(2)}) collective-permute-start(f32[376,128]{1,0:T(8,128)S(1)} %get-tuple-element.69), channel_id=1, source_target_pairs={{0,1},{1,2},{2,3},{3,4},{4,5},{5,6},{6,7},{7,15},{8,0},{9,8},{10,9... | collective-permute-start | bytes 577544 | tf_op jit(solution)/shard_map/ppermute | solution.py:1144
  18.7 0.4 collective-permute-start.4
  19.1 0.0 copy-done
  19.1 6.4 %shard_map.115 = (f32[5,18,2,32,128]{4,3,2,1,0:T(8,128)S(1)}, f32[18,2,16,128]{3,2,1,0:T(8,128)S(1)}, f32[5,18,2,16,128]{4,3,2,1,0:T(8,128)S(1)}, f32[5,18,2,16,...) custom-call(f32[5,18,2,32,128]{4,3,2,1,0:T(8,128)S(1)} %shard_map.113.s1.s1_in, ...), custom_call_target="tpu_custom_call" | custom-call | flops 8000000 | bytes 24000000 | tf_op jit(solution)/shard_map/pallas_call | solution.py:1238
  25.5 0.0 collective-permute-done.3.got_first
  25.5 1.4 %collective-permute-done.4.got_second = f32[376,128]{1,0:T(8,128)S(1)} collective-permute-done((f32[376,128]{1,0:T(8,128)S(1)}, f32[376,128]{1,0:T(8,128)S(1)}, u32[]{:S(2)}, u32[]{:S(2)}) %collective-permute-start.4) | collective-permute-done | bytes 192544 | tf_op jit(solution)/shard_map/ppermute | solution.py:1144
  26.9 2.2 %shard_map.116 = (f32[5,4,2,16,128]{4,3,2,1,0:T(8,128)S(1)}, f32[5,4,2,16,128]{4,3,2,1,0:T(8,128)S(1)}, f32[5,2,2,16,128]{4,3,2,1,0:T(8,128)S(1)}, f32[4,2,16,12...) custom-call(f32[5,18,2,32,128]{4,3,2,1,0:T(8,128)S(1)} %get-tuple-el, ...), custom_call_target="tpu_custom_call" | custom-call | flops 2000000 | bytes 6000000 | tf_op jit(solution)/shard_map/pallas_call | solution.py:1268
  29.1 3.0 %collective-permute-start.5 = (f32[344,128]{1,0:T(8,128)S(1)}, f32[344,128]{1,0:T(8,128)S(1)}, u32[]{:S(2)}, u32[]{:S(2)}) collective-permute-start(f32[344,128]{1,0:T(8,128)S(1)} %get-tuple-element.84), channel_id=1, source_target_pairs={{0,1},{1,2},{2,3},{3,4},{4,5},{5,6},{6,7},{7,15},{8,0},{9,8},{10,9... | collective-permute-start | bytes 528392 | tf_op jit(solution)/shard_map/ppermute | solution.py:1144
  32.1 0.3 collective-permute-start.6
  32.4 6.2 %shard_map.117 = (f32[5,16,16,256]{3,2,1,0:T(8,128)}, f32[5,18,2,16,128]{4,3,2,1,0:T(8,128)S(1)}, f32[16,384]{1,0:T(8,128)S(1)}) custom-call(f32[5,18,2,32,128]{4,3,2,1,0:T(8,128)S(1)} %get-tuple-element.61.s1, f32[5,18,2,16,128]{4,3,2,1,0:T(8,128)S(1)} %get-tuple-element.62.s2_in, f32[5,18,2,16,128]{4,3,2,1,0:T(8,128)S(1)} %get-tuple-element.63.goal, ...), custom_call_target="tpu_custom_call" | custom-call | flops 6000000 | bytes 18000000 | tf_op jit(solution)/shard_map/pallas_call | solution.py:1304
  38.6 0.0 collective-permute-done.5.got_first
  38.6 2.2 %collective-permute-done.6.got_second = f32[344,128]{1,0:T(8,128)S(1)} collective-permute-done((f32[344,128]{1,0:T(8,128)S(1)}, f32[344,128]{1,0:T(8,128)S(1)}, u32[]{:S(2)}, u32[]{:S(2)}) %collective-permute-start.6) | collective-permute-done | bytes 176160 | tf_op jit(solution)/shard_map/ppermute | solution.py:1144
  40.8 0.4 shard_map.118
  41.2 4.4 %collective-permute-start.7 = (f32[16,128]{1,0:T(8,128)S(1)}, f32[16,128]{1,0:T(8,128)S(1)}, u32[]{:S(2)}, u32[]{:S(2)}) collective-permute-start(f32[16,128]{1,0:T(8,128)S(1)} %get-tuple-element.89), channel_id=1, source_target_pairs={{0,8},{8,16},{16,24},{24,32},{32,40},{40,48},{48,56},{56,64},{64,7... | collective-permute-start | bytes 24584 | tf_op jit(solution)/shard_map/ppermute | solution.py:1131
  45.6 0.0 collective-permute-start.8
  45.6 2.2 %shard_map.119 = f32[5,16,16,256]{3,2,1,0:T(8,128)} custom-call(f32[5,18,2,16,128]{4,3,2,1,0:T(8,128)S(1)} %get-tuple-element.78.adj0_in, f32[5,18,2,32,128]{4,3,2,1,0:T(8,128)S(1)} %get-tuple-element.47.field, f32[11,18,2,16,128]{4,3,2,1,0:T(8,128)S(1)} %get-tuple-element.48.coef, f32[18,2,16,128]{3,2,1,0:T(8,128)S(1)} %get-tuple-element.66.base, ...), custom_call_target="tpu_custom_call" | custom-call | flops 2000000 | bytes 6000000 | tf_op jit(solution)/shard_map/pallas_call | solution.py:1349
  47.8 0.0 collective-permute-done.7
  47.8 3.0 %collective-permute-done.8 = f32[16,128]{1,0:T(8,128)S(1)} collective-permute-done((f32[16,128]{1,0:T(8,128)S(1)}, f32[16,128]{1,0:T(8,128)S(1)}, u32[]{:S(2)}, u32[]{:S(2)}) %collective-permute-start.8) | collective-permute-done | bytes 8224 | tf_op jit(solution)/shard_map/ppermute | solution.py:1131
  50.8 0.6 %add_bitcast_fusion = f32[128,1,16]{0,2,1:T(8,128)} fusion(f32[16,128]{1,0:T(8,128)S(1)} %collective-permute-done.8, f32[16,128]{1,0:T(8,128)S(1)} %get-tuple-element.88, f32[16,128]{1,0:T(8,128)S(1)} %collective-permute-done.7), kind=kLoop, calls=%fused_computation | loop fusion | flops 4096 | bytes 32768 | tf_op jit(solution)/shard_map/broadcast_in_dim | solution.py:1370
Async XLA Ops:
  0.6 6.9 %copy-start.4 = (f32[128,1,16]{0,2,1:T(8,128)S(1)}, f32[128,1,16]{0,2,1:T(8,128)}, u32[]{:S(2)}) copy-start(f32[128,1,16]{0,2,1:T(8,128)} %param.14) | copy-start | bytes 24580
  4.1 9.9 %collective-permute-start = (f32[13,16,128]{2,1,0:T(8,128)S(1)}, f32[13,16,128]{2,1,0:T(8,128)S(1)}, u32[]{:S(2)}, u32[]{:S(2)}) collective-permute-start(f32[13,16,128]{2,1,0:T(8,128)S(1)} %get-tuple-element.52), channel_id=1, source_target_pairs={{0,8},{8,16},{16,24},{24,32},{32,40},{40,48},{48,56},{56,64},{64,7... | collective-permute-start | bytes 319496 | tf_op jit(solution)/shard_map/ppermute | solution.py:1131
  7.5 6.5 %collective-permute-start.1 = (f32[13,16,128]{2,1,0:T(8,128)S(1)}, f32[13,16,128]{2,1,0:T(8,128)S(1)}, u32[]{:S(2)}, u32[]{:S(2)}) collective-permute-start(f32[13,16,128]{2,1,0:T(8,128)S(1)} %get-tuple-element.53), channel_id=1, source_target_pairs={{0,1},{8,0},{16,8},{24,16},{32,24},{40,32},{48,40},{56,48},{64,56}... | collective-permute-start | bytes 319496 | tf_op jit(solution)/shard_map/ppermute | solution.py:1131
  7.5 6.5 %collective-permute-start.2 = (f32[16,128]{1,0:T(8,128)S(1)}, f32[16,128]{1,0:T(8,128)S(1)}, u32[]{:S(2)}, u32[]{:S(2)}) collective-permute-start(f32[16,128]{1,0:T(8,128)S(1)} %bitcast.21), channel_id=1, source_target_pairs={{16,0},{24,8},{32,16},{40,24},{48,32},{56,40},{64,48},{72,56},{80,... | collective-permute-start | bytes 24584 | tf_op jit(solution)/shard_map/ppermute | solution.py:1204
  9.4 4.6 %copy-start.1 = (s32[4096,1]{0,1:T(1,128)S(1)}, s32[4096,1]{0,1:T(1,128)}, u32[]{:S(2)}) copy-start(s32[4096,1]{0,1:T(1,128)} %param.15) | copy-start | bytes 49156
  9.4 4.6 %copy-start.2 = (s32[4096,1]{0,1:T(1,128)S(1)}, s32[4096,1]{0,1:T(1,128)}, u32[]{:S(2)}) copy-start(s32[4096,1]{0,1:T(1,128)} %param.16) | copy-start | bytes 49156
  9.4 4.6 %copy-start.3 = (s32[4096,1]{0,1:T(1,128)S(1)}, s32[4096,1]{0,1:T(1,128)}, u32[]{:S(2)}) copy-start(s32[4096,1]{0,1:T(1,128)} %param.17) | copy-start | bytes 49156
  14.0 5.1 %copy-start = (f32[5,16,16,256]{3,2,1,0:T(8,128)S(1)}, f32[5,16,16,256]{3,2,1,0:T(8,128)}, u32[]{:S(2)}) copy-start(f32[5,16,16,256]{3,2,1,0:T(8,128)} %tgt.3) | copy-start | bytes 3932164
  16.1 9.4 %collective-permute-start.3 = (f32[376,128]{1,0:T(8,128)S(1)}, f32[376,128]{1,0:T(8,128)S(1)}, u32[]{:S(2)}, u32[]{:S(2)}) collective-permute-start(f32[376,128]{1,0:T(8,128)S(1)} %get-tuple-element.69), channel_id=1, source_target_pairs={{0,1},{1,2},{2,3},{3,4},{4,5},{5,6},{6,7},{7,15},{8,0},{9,8},{10,9... | collective-permute-start | bytes 577544 | tf_op jit(solution)/shard_map/ppermute | solution.py:1144
  18.7 8.2 %collective-permute-start.4 = (f32[376,128]{1,0:T(8,128)S(1)}, f32[376,128]{1,0:T(8,128)S(1)}, u32[]{:S(2)}, u32[]{:S(2)}) collective-permute-start(f32[376,128]{1,0:T(8,128)S(1)} %get-tuple-element.70), channel_id=1, source_target_pairs={{0,8},{1,0},{2,1},{3,2},{4,3},{5,4},{6,5},{7,6},{8,9},{9,10},{10,1... | collective-permute-start | bytes 577544 | tf_op jit(solution)/shard_map/ppermute | solution.py:1144
  29.1 9.5 %collective-permute-start.5 = (f32[344,128]{1,0:T(8,128)S(1)}, f32[344,128]{1,0:T(8,128)S(1)}, u32[]{:S(2)}, u32[]{:S(2)}) collective-permute-start(f32[344,128]{1,0:T(8,128)S(1)} %get-tuple-element.84), channel_id=1, source_target_pairs={{0,1},{1,2},{2,3},{3,4},{4,5},{5,6},{6,7},{7,15},{8,0},{9,8},{10,9... | collective-permute-start | bytes 528392 | tf_op jit(solution)/shard_map/ppermute | solution.py:1144
  32.1 8.7 %collective-permute-start.6 = (f32[344,128]{1,0:T(8,128)S(1)}, f32[344,128]{1,0:T(8,128)S(1)}, u32[]{:S(2)}, u32[]{:S(2)}) collective-permute-start(f32[344,128]{1,0:T(8,128)S(1)} %get-tuple-element.85), channel_id=1, source_target_pairs={{0,8},{1,0},{2,1},{3,2},{4,3},{5,4},{6,5},{7,6},{8,9},{9,10},{10,1... | collective-permute-start | bytes 528392 | tf_op jit(solution)/shard_map/ppermute | solution.py:1144
  41.2 6.6 %collective-permute-start.7 = (f32[16,128]{1,0:T(8,128)S(1)}, f32[16,128]{1,0:T(8,128)S(1)}, u32[]{:S(2)}, u32[]{:S(2)}) collective-permute-start(f32[16,128]{1,0:T(8,128)S(1)} %get-tuple-element.89), channel_id=1, source_target_pairs={{0,8},{8,16},{16,24},{24,32},{32,40},{40,48},{48,56},{56,64},{64,7... | collective-permute-start | bytes 24584 | tf_op jit(solution)/shard_map/ppermute | solution.py:1131
  45.6 5.2 %collective-permute-start.8 = (f32[16,128]{1,0:T(8,128)S(1)}, f32[16,128]{1,0:T(8,128)S(1)}, u32[]{:S(2)}, u32[]{:S(2)}) collective-permute-start(f32[16,128]{1,0:T(8,128)S(1)} %get-tuple-element.90), channel_id=1, source_target_pairs={{0,1},{8,0},{16,8},{24,16},{32,24},{40,32},{48,40},{56,48},{64,56}... | collective-permute-start | bytes 24584 | tf_op jit(solution)/shard_map/ppermute | solution.py:1131
